TPU v7x, 32 devices: a whole 2x2x4 slice. The times are simulated.
32 devices in a mesh: dp: 4 (over z), fsdp: 8 (over y, x, core).
Axes of the slice: x: 2, y: 2, z: 4, core: 2. Of those that a mesh axis runs over, the one named last changes fastest.
Arguments:
- inputs: bfloat16 [8, 1024, 1024], P('dp', 'fsdp'), may hold values from -6 to 6
- norm_in: bfloat16 [1024], P('fsdp'), may hold values from 0.099609375 to 1.8984375
- w_in: bfloat16 [1024, 3072], P('fsdp'), may hold values from -0.1875 to 0.1875
- taps: bfloat16 [3, 1024], P(None, 'fsdp'), may hold values from -3.5 to 3.5
- w_out: bfloat16 [1024, 1024], P('fsdp'), may hold values from -0.1875 to 0.1875
- norm_mid: bfloat16 [1024], P('fsdp'), may hold values from 0.099609375 to 1.8984375
- w_gate: bfloat16 [1024, 4608], P('fsdp'), may hold values from -0.1875 to 0.1875
- w_up: bfloat16 [1024, 4608], P('fsdp'), may hold values from -0.1875 to 0.1875
- w_down: bfloat16 [4608, 1024], P('fsdp'), may hold values from -0.09375 to 0.09375
- cotangent: bfloat16 [8, 1024, 1024], P('dp', 'fsdp'), may hold values from -6 to 6
Outputs:
- block_out: bfloat16 [8, 1024, 1024], P('dp', 'fsdp')
- grad_inputs: float32 [8, 1024, 1024], P('dp', 'fsdp')
- grad_norm_in: float32 [1024], P('fsdp')
- grad_w_in: float32 [1024, 3072], P('fsdp')
- grad_taps: float32 [3, 1024], P(None, 'fsdp')
- grad_w_out: float32 [1024, 1024], P('fsdp')
- grad_norm_mid: float32 [1024], P('fsdp')
- grad_w_gate: float32 [1024, 4608], P('fsdp')
- grad_w_up: float32 [1024, 4608], P('fsdp')
- grad_w_down: float32 [4608, 1024], P('fsdp')
All inputs are finite; a program needn't handle non-finite values.
Results may differ from a plain program's by a relative error of at most 0.011.
Values may be sent and summed in bfloat16 or wider, within the bound.
No kernel may reach another device: no remote copies, remote signals or barrier semaphores. Data moves between devices by JAX's collectives and lax.ppermute only.
A program may use at most 320 MiB of HBM per device.

v0:
```python
import jax
import jax.numpy as jnp
from jax import lax
from jax.sharding import PartitionSpec as P

epsilon = 1e-05


def from_behind(shard, axis, by):
    peers = lax.axis_size(axis)
    pairs = [(i, i + by) for i in range(peers) if 0 <= i + by < peers]
    return lax.ppermute(shard, axis, pairs)


def inverse_rms(values):
    return lax.rsqrt(jnp.mean(values * values, axis=-1, keepdims=True) + epsilon)


def norm_back(values, scale, gain, incoming):
    normed = values * scale
    gain_grad = jnp.sum(incoming * normed, axis=0)
    weighted = incoming * gain
    projection = jnp.mean(weighted * normed, axis=-1, keepdims=True)
    return (scale * (weighted - normed * projection), gain_grad)


def over_tokens(left, right):
    return lax.dot_general(
        left, right, (((0,), (0,)), ((), ())), preferred_element_type=jnp.float32
    )


def against_rows(left, right):
    return lax.dot_general(
        left, right, (((1,), (1,)), ((), ())), preferred_element_type=jnp.float32
    )


def make_row_terms(
    normed_in, grad_proj, gated, grad_branch, normed_mid, grad_gate, grad_up, small_terms
):

    def row_terms(start, count):
        return jnp.concatenate(
            [
                over_tokens(normed_in, grad_proj),
                over_tokens(gated, grad_branch),
                over_tokens(normed_mid, grad_gate),
                over_tokens(normed_mid, grad_up),
                small_terms,
            ],
            axis=1,
        )

    return row_terms


def make_down_terms(activ, grad_out):

    def down_terms(start, count):
        return over_tokens(activ, grad_out)

    return down_terms


def unpack_weights(gathered):
    gain_in_w, full_in, full_taps, full_out, gain_mid_w, full_gate, full_up, full_down = gathered
    return (
        gain_in_w.astype(jnp.float32),
        full_in,
        full_taps.astype(jnp.float32),
        full_out,
        gain_mid_w.astype(jnp.float32),
        full_gate,
        full_up,
        full_down,
    )


def per_device(inputs, norm_in, w_in, taps, w_out, norm_mid, w_gate, w_up, w_down, cotangent):
    micros = inputs.shape[0]
    rows = inputs.shape[1]
    width = w_in.shape[1] // 3
    hidden_units = w_gate.shape[1]
    reach = taps.shape[0] - 1
    owned_width = w_in.shape[0]
    owned_hidden = w_down.shape[0]
    padding = 128 - 2 - (reach + 1)
    all_rows = micros * rows
    gathered = (
        lax.all_gather(norm_in, "fsdp", axis=0, tiled=True),
        lax.all_gather(w_in, "fsdp", axis=0, tiled=True),
        lax.all_gather(taps, "fsdp", axis=1, tiled=True),
        lax.all_gather(w_out, "fsdp", axis=0, tiled=True),
        lax.all_gather(norm_mid, "fsdp", axis=0, tiled=True),
        lax.all_gather(w_gate, "fsdp", axis=0, tiled=True),
        lax.all_gather(w_up, "fsdp", axis=0, tiled=True),
        lax.all_gather(w_down, "fsdp", axis=0, tiled=True),
    )
    gain_in, full_in, tap_values, full_out, gain_mid, full_gate, full_up, full_down = (
        unpack_weights(gathered)
    )
    resid = inputs.reshape(all_rows, width).astype(jnp.float32)
    scale_in = inverse_rms(resid)
    normed_in = (resid * scale_in * gain_in).astype(jnp.bfloat16)
    projected = jnp.dot(normed_in, full_in, preferred_element_type=jnp.float32)
    gate_b = projected[:, :width]
    gate_c = projected[:, width : 2 * width]
    values = projected[:, 2 * width :]
    mixed = (gate_b * values).astype(jnp.bfloat16).reshape(micros, rows, width)
    earlier = from_behind(mixed[:, rows - reach :], "fsdp", 1)
    extended = jnp.concatenate([earlier, mixed], axis=1).astype(jnp.float32)
    convolved = jnp.zeros((micros, rows, width), jnp.float32)
    for offset in range(reach + 1):
        convolved = convolved + tap_values[offset] * extended[:, offset : offset + rows]
    convolved = convolved.reshape(all_rows, width)
    gated = (gate_c * convolved).astype(jnp.bfloat16)
    middle = resid + jnp.dot(gated, full_out, preferred_element_type=jnp.float32)
    scale_mid = inverse_rms(middle)
    normed_mid = (middle * scale_mid * gain_mid).astype(jnp.bfloat16)
    gate_pre = jnp.dot(normed_mid, full_gate, preferred_element_type=jnp.float32)
    up_pre = jnp.dot(normed_mid, full_up, preferred_element_type=jnp.float32)
    activ = (jax.nn.silu(gate_pre) * up_pre).astype(jnp.bfloat16)
    final = middle + jnp.dot(activ, full_down, preferred_element_type=jnp.float32)
    block_out = final.astype(jnp.bfloat16).reshape(micros, rows, width)
    grad_out = cotangent.reshape(all_rows, width)
    grad_activ = against_rows(grad_out, full_down)
    sigmoid_gate = jax.nn.sigmoid(gate_pre)
    grad_gate = (
        grad_activ * up_pre * sigmoid_gate * (1.0 + gate_pre * (1.0 - sigmoid_gate))
    ).astype(jnp.bfloat16)
    grad_up = (grad_activ * gate_pre * sigmoid_gate).astype(jnp.bfloat16)
    grad_normed_mid = against_rows(grad_gate, full_gate) + against_rows(grad_up, full_up)
    back_mid, gain_mid_grad = norm_back(middle, scale_mid, gain_mid, grad_normed_mid)
    grad_middle = grad_out.astype(jnp.float32) + back_mid
    grad_branch = grad_middle.astype(jnp.bfloat16)
    grad_gated = against_rows(grad_branch, full_out)
    grad_c = grad_gated * convolved
    grad_conv = (grad_gated * gate_c).astype(jnp.bfloat16).reshape(micros, rows, width)
    later = from_behind(grad_conv[:, :reach], "fsdp", -1)
    ext_grad = jnp.concatenate([grad_conv, later], axis=1).astype(jnp.float32)
    grad_mixed = jnp.zeros((micros, rows, width), jnp.float32)
    tap_terms = []
    for offset in range(reach + 1):
        grad_mixed = (
            grad_mixed + tap_values[offset] * ext_grad[:, reach - offset : reach - offset + rows]
        )
        tap_terms.append(
            jnp.sum(extended[:, offset : offset + rows] * ext_grad[:, :rows], axis=(0, 1))
        )
    tap_grad = jnp.stack(tap_terms, axis=1)
    grad_mixed = grad_mixed.reshape(all_rows, width)
    grad_proj = jnp.concatenate([grad_mixed * values, grad_c, grad_mixed * gate_b], axis=1).astype(
        jnp.bfloat16
    )
    grad_normed_in = against_rows(grad_proj, full_in)
    back_in, gain_in_grad = norm_back(resid, scale_in, gain_in, grad_normed_in)
    grad_inputs = (grad_middle + back_in).reshape(micros, rows, width)
    small_terms = jnp.concatenate(
        [
            gain_in_grad[:, None],
            gain_mid_grad[:, None],
            tap_grad,
            jnp.zeros((width, padding), jnp.float32),
        ],
        axis=1,
    )
    row_terms = make_row_terms(
        normed_in, grad_proj, gated, grad_branch, normed_mid, grad_gate, grad_up, small_terms
    )
    down_terms = make_down_terms(activ, grad_out)
    owned_rows = lax.psum_scatter(
        row_terms(jnp.int32(0), owned_width * lax.axis_size("fsdp")),
        "fsdp",
        scatter_dimension=0,
        tiled=True,
    )
    owned_down = lax.psum_scatter(
        down_terms(jnp.int32(0), owned_hidden * lax.axis_size("fsdp")),
        "fsdp",
        scatter_dimension=0,
        tiled=True,
    )
    owned_rows, owned_down = lax.psum((owned_rows, owned_down), "dp")
    grad_w_in = owned_rows[:, : 3 * width]
    grad_w_out = owned_rows[:, 3 * width : 4 * width]
    grad_w_gate = owned_rows[:, 4 * width : 4 * width + hidden_units]
    grad_w_up = owned_rows[:, 4 * width + hidden_units : 4 * width + 2 * hidden_units]
    small_owned = owned_rows[:, 4 * width + 2 * hidden_units :]
    grad_norm_in = small_owned[:, 0]
    grad_norm_mid = small_owned[:, 1]
    grad_taps = jnp.transpose(small_owned[:, 2 : 3 + reach])
    return (
        block_out,
        grad_inputs,
        grad_norm_in,
        grad_w_in,
        grad_taps,
        grad_w_out,
        grad_norm_mid,
        grad_w_gate,
        grad_w_up,
        owned_down,
    )


def solution(mesh):
    return jax.shard_map(
        per_device,
        mesh=mesh,
        in_specs=(
            P("dp", "fsdp", None),
            P("fsdp"),
            P("fsdp", None),
            P(None, "fsdp"),
            P("fsdp", None),
            P("fsdp"),
            P("fsdp", None),
            P("fsdp", None),
            P("fsdp", None),
            P("dp", "fsdp", None),
        ),
        out_specs=(
            P("dp", "fsdp", None),
            P("dp", "fsdp", None),
            P("fsdp"),
            P("fsdp", None),
            P(None, "fsdp"),
            P("fsdp", None),
            P("fsdp"),
            P("fsdp", None),
            P("fsdp", None),
            P("fsdp", None),
        ),
        check_vma=False,
    )
```

profile of v0, /device:TPU:0, one launch (start us, length us, event | category | flops | bytes accessed | tf_op | source)
XLA Modules:
  0.0 1072.8 jit_solution(5592125510112454536)
XLA Ops:
  7.3 0.7 all-gather.8.cloned.1.call-update
  8.0 0.7 all-gather.10.cloned.1.call-update
  10.6 10.2 all-gather
  20.9 8.9 all_gather.26
  30.1 28.1 %all-gather.8.cloned.1.call-done = bf16[1024,3072]{1,0:T(8,128)(2,1)} async-done(((bf16[128,3072]{1,0:T(8,128)(2,1)}), bf16[1024,3072]{1,0:T(8,128)(2,1)}) %all-gather.8.cloned.1.call-update) | async-done | bytes 6291472 | tf_op jit(solution)/shard_map/all_gather | solution.py:92
  58.2 4.6 fusion.17
  63.0 2.2 collective-permute-start
  65.2 8.7 all-gather.1
  74.4 1.0 copy-done.3
  75.5 12.5 %all-gather.10.cloned.1.call-done = bf16[1024,1024]{1,0:T(8,128)(2,1)} async-done(((bf16[128,1024]{1,0:T(8,128)(2,1)}), bf16[1024,1024]{1,0:T(8,128)(2,1)}) %all-gather.10.cloned.1.call-update) | async-done | bytes 2097168 | tf_op jit(solution)/shard_map/all_gather | solution.py:94
  88.0 2.4 multiply_reduce_fusion.7
  90.6 58.2 %all-gather.14.cloned.1.call-done = bf16[1024,4608]{1,0:T(8,128)(2,1)} async-done(((bf16[128,4608]{1,0:T(8,128)(2,1)}), bf16[1024,4608]{1,0:T(8,128)(2,1)}) %all-gather.14.cloned.1.call-update) | async-done | bytes 9437200 | tf_op jit(solution)/shard_map/all_gather | solution.py:97
  148.8 8.1 fusion.19
  156.9 52.5 %all-gather.12.cloned.1.call-done = bf16[1024,4608]{1,0:T(8,128)(2,1)} async-done(((bf16[128,4608]{1,0:T(8,128)(2,1)}), bf16[1024,4608]{1,0:T(8,128)(2,1)}) %all-gather.12.cloned.1.call-update) | async-done | bytes 9437200 | tf_op jit(solution)/shard_map/all_gather | solution.py:96
  209.4 7.9 fusion.18
  217.3 52.7 %all-gather.16.cloned.1.call-done = bf16[4608,1024]{1,0:T(8,128)(2,1)} async-done(((bf16[576,1024]{1,0:T(8,128)(2,1)}), bf16[4608,1024]{1,0:T(8,128)(2,1)}) %all-gather.16.cloned.1.call-update) | async-done | bytes 9437200 | tf_op jit(solution)/shard_map/all_gather | solution.py:98
  270.0 10.4 multiply_convert_fusion
  280.4 1.4 copy-done.12
  281.8 7.9 fusion.23
  289.9 6.1 fusion.20
  296.1 7.0 multiply_reduce_fusion.3
  303.1 2.0 multiply_add_fusion.1
  305.1 1.1 copy-done.5
  306.2 3.2 fusion.6
  309.4 1.6 collective-permute-start.1
  311.0 9.7 fusion.22
  320.7 8.2 fusion.21
  328.9 2.7 fusion.9
  331.6 1.0 copy.31
  332.7 1.6 multiply_reduce_fusion
  334.8 2.2 fusion.3
  337.1 6.1 multiply_reduce_fusion.4
  343.2 1.0 copy.30
  344.2 1.0 copy.32
  345.3 8.2 fusion.7
  353.4 0.8 broadcast_in_dim.8
  354.3 61.9 %concatenate.16 = f32[1024,13440]{1,0:T(8,128)} concatenate(f32[1024,3072]{1,0:T(8,128)} %fusion.7, f32[1024,1024]{1,0:T(8,128)} %fusion.9, f32[1024,4608]{1,0:T(8,128)} %fusion.21, f32[1024,4608]{1,0:T(8,128)} %fusion.22, f32[1024,1]{1,0:T(8,128)} %copy.30, f32[1024,1]{1,0:T(8,128)S(1)} %copy-done.15, f32[1024,1]{1,0:T(8,128)} %copy.32, f32[1024,1]{1,0:T(8,128)S(1)} %copy.33, ...), dimensions={1} | concatenate | bytes 110100480 | tf_op jit(solution)/shard_map/concatenate | solution.py:44
  416.5 313.4 %reduce-scatter.3.cloned.1.call-done = f32[128,13440]{1,0:T(8,128)} async-done(((f32[1024,13440]{1,0:T(8,128)}), f32[128,13440]{1,0:T(8,128)}) %reduce-scatter.3.cloned.1.call-update) | async-done | bytes 6881296 | tf_op jit(solution)/shard_map/reduce_scatter | solution.py:172
  729.9 1.2 copy-done.2
  731.1 7.9 fusion
  739.0 1.3 multiply_add_fusion
  740.3 311.5 %all-reduce.3.cloned.1.call-done = (f32[128,13440]{1,0:T(8,128)}, f32[576,1024]{1,0:T(8,128)}) async-done(((f32[128,13440]{1,0:T(8,128)}, f32[576,1024]{1,0:T(8,128)}), (f32[128,13440]{1,0:T(8,128)}, f32[576,1024]{1,0:T(8,128)})) %all-reduce.3.cloned.1.call-update) | async-done | bytes 9240592 | tf_op jit(solution)/shard_map/psum | solution.py:184
  1051.7 1.6 slice_reduce_fusion
  1053.3 0.9 slice_bitcast_fusion
  1054.3 1.9 slice.114
  1056.2 2.7 slice.112
  1058.9 5.0 fusion.15
  1064.5 1.4 copy.39
  (85 shorter events, 5.2 us)
Async XLA Ops:
  7.2 3.5 copy-start.24
  7.2 13.7 %copy-start.23 = (bf16[3,128]{1,0:T(4,128)(2,1)S(1)}, bf16[3,128]{1,0:T(4,128)(2,1)}, u32[]{:S(2)}) copy-start(bf16[3,128]{1,0:T(4,128)(2,1)} %param.13) | copy-start | bytes 2308
  7.2 22.5 %copy-start.6 = (bf16[2,128,1024]{2,1,0:T(8,128)(2,1)S(1)}, bf16[2,128,1024]{2,1,0:T(8,128)(2,1)}, u32[]{:S(2)}) copy-start(bf16[2,128,1024]{2,1,0:T(8,128)(2,1)} %param.10) | copy-start | bytes 1572868
  7.2 51.0 %all-gather.8.cloned.1.call-start = ((), (), s32[]{:S(2)}) async-start(), calls=%async_computation.2 | async-start | bytes 7077888 | tf_op jit(solution)/shard_map/all_gather | solution.py:92
  7.9 80.1 %all-gather.10.cloned.1.call-start = ((), (), s32[]{:S(2)}) async-start(), calls=%async_computation.3 | async-start | bytes 2359296 | tf_op jit(solution)/shard_map/all_gather | solution.py:94
  8.7 140.1 %all-gather.14.cloned.1.call-start = ((), (), s32[]{:S(2)}) async-start(), calls=%async_computation.5 | async-start | bytes 10616832 | tf_op jit(solution)/shard_map/all_gather | solution.py:97
  9.4 200.0 %all-gather.12.cloned.1.call-start = ((), (), s32[]{:S(2)}) async-start(), calls=%async_computation.4 | async-start | bytes 10616832 | tf_op jit(solution)/shard_map/all_gather | solution.py:96
  10.0 260.0 %all-gather.16.cloned.1.call-start = ((), (), s32[]{:S(2)}) async-start(), calls=%async_computation.6 | async-start | bytes 10616832 | tf_op jit(solution)/shard_map/all_gather | solution.py:98
  10.6 405.9 %reduce-scatter.5.cloned.1.call-start = ((), (), s32[]{:S(2)}) async-start(), calls=%async_computation.8 | async-start | bytes 21233664 | tf_op jit(solution)/shard_map/reduce_scatter | solution.py:178
  30.1 32.7 %copy-start.16 = (bf16[256,1024]{1,0:T(8,128)(2,1)}, bf16[256,1024]{1,0:T(8,128)(2,1)S(1)}, u32[]{:S(2)}) copy-start(bf16[256,1024]{1,0:T(8,128)(2,1)S(1)} %multiply_convert_fusion.6) | copy-start | bytes 1572868
  30.1 35.0 %copy-start.25 = (bf16[128]{0:T(256)(128)(2,1)S(1)}, bf16[128]{0:T(256)(128)(2,1)}, u32[]{:S(2)}) copy-start(bf16[128]{0:T(256)(128)(2,1)} %param.15) | copy-start | bytes 772
  62.8 11.6 %copy-start = (f32[256,3072]{1,0:T(8,128)}, f32[256,3072]{1,0:T(8,128)S(1)}, u32[]{:S(2)}) copy-start(f32[256,3072]{1,0:T(8,128)S(1)} %fusion.17) | copy-start | bytes 9437188
  63.0 10.9 %collective-permute-start = (bf16[2,2,1024]{2,1,0:T(2,128)(2,1)S(1)}, bf16[2,2,1024]{2,1,0:T(2,128)(2,1)S(1)}, u32[]{:S(2)}, u32[]{:S(2)}) collective-permute-start(bf16[2,2,1024]{2,1,0:T(2,128)(2,1)S(1)} %slice.101), channel_id=1, source_target_pairs={{0,1},{1,2},{2,3},{3,4},{4,5},{5,6},{6,7},{8,9},{9,10},{10,11},{11... | collective-permute-start | bytes 24584 | tf_op jit(solution)/shard_map/ppermute | solution.py:12
  74.4 1.0 copy-start.3
  75.5 14.9 %copy-start.7 = (bf16[256,1024]{1,0:T(8,128)(2,1)}, bf16[256,1024]{1,0:T(8,128)(2,1)S(1)}, u32[]{:S(2)}) copy-start(bf16[256,1024]{1,0:T(8,128)(2,1)S(1)} %fusion.5) | copy-start | bytes 1572868
  90.4 205.6 %copy-start.1 = (f32[256,1024]{1,0:T(8,128)}, f32[256,1024]{1,0:T(8,128)S(1)}, u32[]{:S(2)}) copy-start(f32[256,1024]{1,0:T(8,128)S(1)} %get-tuple-element.65) | copy-start | bytes 3145732
  270.0 11.8 %copy-start.18 = (bf16[2,128,1024]{2,1,0:T(8,128)(2,1)S(1)}, bf16[2,128,1024]{2,1,0:T(8,128)(2,1)}, u32[]{:S(2)}) copy-start(bf16[2,128,1024]{2,1,0:T(8,128)(2,1)} %param.19) | copy-start | bytes 1572868
  280.4 1.4 copy-start.12
  289.7 440.2 %reduce-scatter.3.cloned.1.call-start = ((), (), s32[]{:S(2)}) async-start(), calls=%async_computation.7 | async-start | bytes 61931520 | tf_op jit(solution)/shard_map/reduce_scatter | solution.py:172
  289.9 6.1 copy-start.10
  296.1 7.1 copy-start.19
  303.1 2.0 copy-start.4
  303.1 3.1 copy-start.5
  309.4 11.3 %copy-start.13 = (bf16[256,1024]{1,0:T(8,128)(2,1)}, bf16[256,1024]{1,0:T(8,128)(2,1)S(1)}, u32[]{:S(2)}) copy-start(bf16[256,1024]{1,0:T(8,128)(2,1)S(1)} %get-tuple-element.60) | copy-start | bytes 1572868
  309.4 11.3 %copy-start.9 = (bf16[256,4608]{1,0:T(8,128)(2,1)S(1)}, bf16[256,4608]{1,0:T(8,128)(2,1)}, u32[]{:S(2)}) copy-start(bf16[256,4608]{1,0:T(8,128)(2,1)} %get-tuple-element.52) | copy-start | bytes 7077892
  309.4 23.2 %collective-permute-start.1 = (bf16[2,2,1024]{2,1,0:T(2,128)(2,1)S(1)}, bf16[2,2,1024]{2,1,0:T(2,128)(2,1)S(1)}, u32[]{:S(2)}, u32[]{:S(2)}) collective-permute-start(bf16[2,2,1024]{2,1,0:T(2,128)(2,1)S(1)} %slice.107), channel_id=1, source_target_pairs={{1,0},{2,1},{3,2},{4,3},{5,4},{6,5},{7,6},{9,8},{10,9},{11,10},{12... | collective-permute-start | bytes 24584 | tf_op jit(solution)/shard_map/ppermute | solution.py:12
  320.7 8.2 copy-start.8
  328.9 3.7 copy-start.14
  334.3 2.7 copy-start.17
  337.0 6.1 copy-start.20
  337.1 6.1 copy-start.21
  345.3 9.0 copy-start.15
  416.2 635.6 %all-reduce.3.cloned.1.call-start = ((), (), s32[]{:S(2)}) async-start(), calls=%async_computation.9 | async-start | bytes 18481152 | tf_op jit(solution)/shard_map/psum | solution.py:184
  729.9 1.2 copy-start.2
  731.1 7.9 copy-start.22
  1058.9 5.7 copy-start.11
Sparse Core Ops, SparseCore 0:
  9.9 48.2 all-gather.7
  60.1 27.8 all-gather.9
  89.9 58.8 all-gather.13
  150.5 58.8 all-gather.11
  211.1 58.8 all-gather.15
  289.8 126.0 reduce-scatter.4
  419.6 310.2 reduce-scatter.2
  732.7 318.9 all-reduce.2
where the time goes:
time: 1080 us; the launch traced here: 1070 us
  waiting for transfers between devices  832 us (77%)
  matrix products  100 us (9%)
  local copies, waits for them, and re-layouts  85.2 us (8%)
  blocking collectives  27.8 us (3%)
  between operations  14.5 us (1%)
    reduce_scatter x1, waiting for transfers between devices, per_device(): lax.psum_scatter(row_terms(jnp.int32(0), owned_width * lax.axis_size('fsd...  313 us
    psum x1, waiting for transfers between devices, per_device(): owned_rows, owned_down = lax.psum((owned_rows, owned_down), 'dp')  311 us
    concatenate x1, local copies, waits for them, and re-layouts, row_terms(): jnp.concatenate([over_tokens(normed_in, grad_proj), over_tokens(gated, gr...  61.9 us
    all_gather x1, waiting for transfers between devices, per_device(): lax.all_gather(w_up, 'fsdp', axis=0, tiled=True)  58.2 us
    all_gather x1, waiting for transfers between devices, per_device(): lax.all_gather(w_down, 'fsdp', axis=0, tiled=True)  52.7 us
    all_gather x1, waiting for transfers between devices, per_device(): lax.all_gather(w_gate, 'fsdp', axis=0, tiled=True)  52.5 us
    dot_general x5, matrix products, over_tokens(): lax.dot_general(left, right, (((0,), (0,)), ((), ())), preferred_element_...  36.6 us
    dot_general x5, matrix products, against_rows(): lax.dot_general(left, right, (((1,), (1,)), ((), ())), preferred_element_...  32.8 us
  transfers between devices with their start and end apart: 10, of which 7 were waited for; matrix products, arithmetic and copies ran while one was open for 15% of the time, Pallas kernels for 0%

commit v1 on v0

v1 whole, which is shorter than its diff:
```python
import jax
import jax.numpy as jnp
from jax import lax
from jax.sharding import PartitionSpec as P

epsilon = 1e-05
bf16 = jnp.bfloat16
f32 = jnp.float32


def along(shard, axis, pairs):
    return lax.ppermute(shard, axis, pairs)


def flip(shard, bits):
    peers = lax.axis_size("fsdp")
    return along(shard, "fsdp", [(i, i ^ bits) for i in range(peers)])


def flip_by_core(shard, even_bits, odd_bits):
    peers = lax.axis_size("fsdp")
    return along(
        shard, "fsdp", [(i, i ^ (odd_bits if i & 1 else even_bits)) for i in range(peers)]
    )


def is_cube():
    return lax.axis_size("fsdp") == 8


def on_odd_core():
    return (lax.axis_index("fsdp") & 1) == 1


def gather_relative(shard):
    if not is_cube():
        whole = lax.all_gather(shard, "fsdp", axis=0)
        return [whole[j] for j in range(lax.axis_size("fsdp"))]
    from_x = flip(shard, 2)
    from_y = flip(shard, 4)
    from_core = flip(shard, 1)
    across = flip_by_core(jnp.where(on_odd_core(), from_y, from_x), 4, 2)
    return [
        shard,
        from_core,
        from_x,
        flip(from_x, 1),
        from_y,
        flip(from_y, 1),
        across,
        flip(across, 1),
    ]


def scatter_relative(parts):
    if not is_cube():
        return lax.psum_scatter(
            jnp.stack([part.astype(bf16) for part in parts]), "fsdp", scatter_dimension=0
        ).astype(f32)
    parts = [part.astype(bf16) for part in parts]
    far = flip(parts[7], 1)
    near = flip(jnp.stack([parts[1], parts[3], parts[5]]), 1)
    odd = on_odd_core()
    across = flip_by_core((parts[6].astype(f32) + far).astype(bf16), 2, 4).astype(f32)
    zero = jnp.zeros((), f32)
    to_x = parts[2].astype(f32) + near[1] + jnp.where(odd, across, zero)
    to_y = parts[4].astype(f32) + near[2] + jnp.where(odd, zero, across)
    got_x = flip(to_x.astype(bf16), 2)
    got_y = flip(to_y.astype(bf16), 4)
    return parts[0].astype(f32) + near[0] + got_x + got_y


def exchange(blocks):
    peers = lax.axis_size("fsdp")
    if not is_cube():
        return lax.all_to_all(blocks, "fsdp", 0, 0)
    me = lax.axis_index("fsdp")
    result = blocks
    for j in range(1, peers):
        block = lax.dynamic_index_in_dim(blocks, me ^ j, 0, keepdims=False)
        result = lax.dynamic_update_index_in_dim(result, flip(block, j), me ^ j, 0)
    return result


def relabel(columns):
    peers = lax.axis_size("fsdp")
    if not is_cube():
        return columns
    size = columns.shape[-1] // peers
    me = lax.axis_index("fsdp")
    blocks = [columns[..., k * size : (k + 1) * size] for k in range(peers)]
    for bit in (1, 2, 4):
        swap = (me & bit) != 0
        blocks = [jnp.where(swap, blocks[k ^ bit], blocks[k]) for k in range(peers)]
    return jnp.concatenate(blocks, axis=-1)


def sum_over_groups(term):
    groups = lax.axis_size("dp")
    term = term.astype(bf16)
    if groups != 4:
        return lax.psum(term, "dp").astype(f32)
    inner = (lax.axis_index("dp") == 1) | (lax.axis_index("dp") == 2)
    pair = (term.astype(f32) + along(term, "dp", [(0, 1), (3, 2)])).astype(bf16)
    total = (pair.astype(f32) + along(pair, "dp", [(1, 2), (2, 1)])).astype(bf16)
    return jnp.where(inner, total, along(total, "dp", [(1, 0), (2, 3)])).astype(f32)


def from_behind(shard, axis, by):
    peers = lax.axis_size(axis)
    pairs = [(i, i + by) for i in range(peers) if 0 <= i + by < peers]
    return lax.ppermute(shard, axis, pairs)


def inverse_rms(values):
    return lax.rsqrt(jnp.mean(values * values, axis=-1, keepdims=True) + epsilon)


def norm_back(values, scale, gain, incoming):
    normed = values * scale
    gain_grad = jnp.sum(incoming * normed, axis=0)
    weighted = incoming * gain
    projection = jnp.mean(weighted * normed, axis=-1, keepdims=True)
    return (scale * (weighted - normed * projection), gain_grad)


def times(left, right):
    return jnp.dot(left, right, preferred_element_type=f32)


def over_tokens(left, right):
    return lax.dot_general(left, right, (((0,), (0,)), ((), ())), preferred_element_type=f32)


def against_rows(left, right):
    return lax.dot_general(left, right, (((1,), (1,)), ((), ())), preferred_element_type=f32)


def per_device(inputs, norm_in, w_in, taps, w_out, norm_mid, w_gate, w_up, w_down, cotangent):
    micros, rows, width = inputs.shape
    peers = lax.axis_size("fsdp")
    reach = taps.shape[0] - 1
    owned = w_in.shape[0]
    hidden = w_down.shape[0]
    all_rows = micros * rows
    small_rows = 16

    small = jnp.concatenate([norm_in, norm_mid, taps.reshape(-1)])
    small = jnp.pad(small, (0, small_rows * width - small.shape[0])).reshape(small_rows, width)
    packed = jnp.concatenate(
        [w_in[:, :width], w_in[:, width : 2 * width], w_in[:, 2 * width :], small], axis=0
    )
    in_pieces = gather_relative(packed)
    full_in = [
        jnp.concatenate([piece[k * owned : (k + 1) * owned] for piece in in_pieces], axis=0)
        for k in range(3)
    ]
    count = owned * (reach + 3)
    smalls = relabel(
        jnp.concatenate(
            [piece[3 * owned].reshape(-1)[:count].reshape(reach + 3, owned) for piece in in_pieces],
            axis=1,
        )
    ).astype(f32)
    gain_in, gain_mid, tap_values = smalls[0], smalls[1], smalls[2:]
    full_out = jnp.concatenate(gather_relative(w_out), axis=0)

    gate_up = jnp.stack(
        [w_gate.reshape(owned, peers, hidden), w_up.reshape(owned, peers, hidden)]
    )
    gate_up = exchange(jnp.transpose(gate_up, (2, 0, 1, 3)))
    own_gate = gate_up[:, 0].reshape(width, hidden)
    own_up = gate_up[:, 1].reshape(width, hidden)

    grad_out = cotangent.reshape(all_rows, width)
    grad_out_all = jnp.concatenate(gather_relative(grad_out), axis=0)

    resid = inputs.reshape(all_rows, width).astype(f32)
    scale_in = inverse_rms(resid)
    normed_in = relabel((resid * scale_in * gain_in).astype(bf16))
    gate_b = times(normed_in, full_in[0])
    gate_c = times(normed_in, full_in[1])
    values = times(normed_in, full_in[2])
    mixed = (gate_b * values).astype(bf16).reshape(micros, rows, width)
    earlier = from_behind(mixed[:, rows - reach :], "fsdp", 1)
    extended = jnp.concatenate([earlier, mixed], axis=1).astype(f32)
    convolved = jnp.zeros((micros, rows, width), f32)
    for offset in range(reach + 1):
        convolved = convolved + tap_values[offset] * extended[:, offset : offset + rows]
    convolved = convolved.reshape(all_rows, width)
    gated = relabel((gate_c * convolved).astype(bf16))
    middle = resid + times(gated, full_out)
    scale_mid = inverse_rms(middle)
    normed_mid = (middle * scale_mid * gain_mid).astype(bf16)

    normed_all = jnp.concatenate(gather_relative(normed_mid), axis=0)
    gate_pre = times(normed_all, own_gate)
    up_pre = times(normed_all, own_up)
    sigmoid_gate = jax.nn.sigmoid(gate_pre)
    activ = (gate_pre * sigmoid_gate * up_pre).astype(bf16)
    grad_w_down = over_tokens(activ, grad_out_all)
    half = hidden // 2
    grad_w_down = jnp.concatenate(
        [sum_over_groups(grad_w_down[:half]), sum_over_groups(grad_w_down[half:])], axis=0
    )
    grad_activ = against_rows(grad_out_all, w_down)
    grad_gate = (
        grad_activ * up_pre * sigmoid_gate * (1.0 + gate_pre * (1.0 - sigmoid_gate))
    ).astype(bf16)
    grad_up = (grad_activ * gate_pre * sigmoid_gate).astype(bf16)
    grad_normed = (against_rows(grad_gate, own_gate) + against_rows(grad_up, own_up)).astype(bf16)
    grad_normed_mid = scatter_relative(
        [grad_normed[j * all_rows : (j + 1) * all_rows] for j in range(peers)]
    )
    final = times(activ, w_down).astype(bf16)
    final = scatter_relative([final[j * all_rows : (j + 1) * all_rows] for j in range(peers)])
    block_out = (middle + final).astype(bf16).reshape(micros, rows, width)

    def to_owner(left, right):
        total = sum_over_groups(over_tokens(left, right)).astype(bf16)
        mine = exchange(total.reshape(peers, owned, hidden))
        return jnp.transpose(mine, (1, 0, 2)).reshape(owned, peers * hidden).astype(f32)

    grad_w_gate = to_owner(normed_all, grad_gate)
    grad_w_up = to_owner(normed_all, grad_up)

    back_mid, gain_mid_grad = norm_back(middle, scale_mid, gain_mid, grad_normed_mid)
    grad_middle = grad_out.astype(f32) + back_mid
    grad_branch = grad_middle.astype(bf16)
    grad_gated = relabel(against_rows(grad_branch, full_out))
    grad_c = grad_gated * convolved
    grad_conv = (grad_gated * gate_c).astype(bf16).reshape(micros, rows, width)
    later = from_behind(grad_conv[:, :reach], "fsdp", -1)
    ext_grad = jnp.concatenate([grad_conv, later], axis=1).astype(f32)
    grad_mixed = jnp.zeros((micros, rows, width), f32)
    tap_terms = []
    for offset in range(reach + 1):
        grad_mixed = (
            grad_mixed + tap_values[offset] * ext_grad[:, reach - offset : reach - offset + rows]
        )
        tap_terms.append(
            jnp.sum(extended[:, offset : offset + rows] * ext_grad[:, :rows], axis=(0, 1))
        )
    grad_mixed = grad_mixed.reshape(all_rows, width)
    grad_proj = [
        (grad_mixed * values).astype(bf16),
        grad_c.astype(bf16),
        (grad_mixed * gate_b).astype(bf16),
    ]
    grad_normed_in = relabel(
        against_rows(grad_proj[0], full_in[0])
        + against_rows(grad_proj[1], full_in[1])
        + against_rows(grad_proj[2], full_in[2])
    )
    back_in, gain_in_grad = norm_back(resid, scale_in, gain_in, grad_normed_in)
    grad_inputs = (grad_middle + back_in).reshape(micros, rows, width)

    def to_rows(term, extra=None):
        parts = [term[j * owned : (j + 1) * owned].astype(bf16) for j in range(peers)]
        if extra is not None:
            parts = [
                jnp.concatenate([part, more.astype(bf16)], axis=0)
                for part, more in zip(parts, extra)
            ]
        return sum_over_groups(scatter_relative(parts))

    grad_w_out = to_rows(over_tokens(gated, grad_branch))
    small_grads = relabel(jnp.stack([gain_in_grad, gain_mid_grad] + tap_terms))
    small_parts = []
    for j in range(peers):
        part = small_grads[:, j * owned : (j + 1) * owned].reshape(-1)
        small_parts.append(
            jnp.pad(part, (0, small_rows * width - part.shape[0])).reshape(small_rows, width)
        )
    grad_in_b = to_rows(over_tokens(normed_in, grad_proj[0]))
    grad_in_c = to_rows(over_tokens(normed_in, grad_proj[1]))
    grad_in_v = to_rows(over_tokens(normed_in, grad_proj[2]), small_parts)
    grad_w_in = jnp.concatenate([grad_in_b, grad_in_c, grad_in_v[:owned]], axis=1)
    small_owned = grad_in_v[owned:].reshape(-1)[:count].reshape(reach + 3, owned)
    return (
        block_out,
        grad_inputs,
        small_owned[0],
        grad_w_in,
        small_owned[2:],
        grad_w_out,
        small_owned[1],
        grad_w_gate,
        grad_w_up,
        grad_w_down,
    )


def solution(mesh):
    return jax.shard_map(
        per_device,
        mesh=mesh,
        in_specs=(
            P("dp", "fsdp", None),
            P("fsdp"),
            P("fsdp", None),
            P(None, "fsdp"),
            P("fsdp", None),
            P("fsdp"),
            P("fsdp", None),
            P("fsdp", None),
            P("fsdp", None),
            P("dp", "fsdp", None),
        ),
        out_specs=(
            P("dp", "fsdp", None),
            P("dp", "fsdp", None),
            P("fsdp"),
            P("fsdp", None),
            P(None, "fsdp"),
            P("fsdp", None),
            P("fsdp"),
            P("fsdp", None),
            P("fsdp", None),
            P("fsdp", None),
        ),
        check_vma=False,
    )
```

time: 1080 us -> 504 us (0.47)
  waiting for transfers between devices: 832 us -> 228 us
  starting transfers between devices: 4.43 us -> 99.3 us
  other arithmetic: 8.54 us -> 55.5 us
  matrix products: 100 us -> 60.3 us
  local copies, waits for them, and re-layouts: 85.2 us -> 50.4 us
  blocking collectives: 27.8 us -> 0 us
  between operations: 14.5 us -> 3.09 us
    reduce_scatter x2 -> x0, waiting for transfers between devices: 313 us -> none  [the longest x1 313 us: per_device(): lax.psum_scatter(row_terms(jnp.int32(0), owned_width * lax.axis_size('fsd...]
    psum x1 -> x0, waiting for transfers between devices: 311 us -> none  [per_device(): owned_rows, owned_down = lax.psum((owned_rows, owned_down), 'dp')]
    ppermute x0 -> x103, waiting for transfers between devices: none -> 228 us  [along(): return lax.ppermute(shard, axis, pairs)]
    all_gather x5 -> x0, waiting for transfers between devices: 204 us -> none  [the longest x1 58.2 us: per_device(): lax.all_gather(w_up, 'fsdp', axis=0, tiled=True)]
    ppermute x0 -> x103, starting transfers between devices: none -> 95.2 us  [along(): return lax.ppermute(shard, axis, pairs)]
    concatenate x1 -> x5, local copies, waits for them, and re-layouts: 61.9 us -> 0.96 us  [the longest x1 0.86 us: per_device(): jnp.concatenate([piece[k * owned:(k + 1) * owned] for piece in in_pieces]...]
    all_gather x3 -> x0, blocking collectives: 27.8 us -> none  [the longest x1 10.2 us: per_device(): lax.all_gather(norm_in, 'fsdp', axis=0, tiled=True)]
    convert_element_type x8 -> x42, other arithmetic: 0.95 us -> 25.9 us  [the longest x8 7.77 us: sum_over_groups(): (pair.astype(f32) + along(pair, 'dp', [(1, 2), (2, 1)])).astype(bf16)]
  transfers between devices with their start and end apart: 10 -> 105, of which waited for: 7 -> 39; matrix products, arithmetic and copies ran while one was open for 15% -> 28% of each run, Pallas kernels for 0% -> 0%
where the time goes in v1:
time: 504 us; the launch traced here: 497 us
  waiting for transfers between devices  228 us (45%)
  starting transfers between devices  99.3 us (20%)
  matrix products  60.3 us (12%)
  other arithmetic  55.5 us (11%)
  local copies, waits for them, and re-layouts  50.4 us (10%)
    ppermute x103, waiting for transfers between devices, along(): return lax.ppermute(shard, axis, pairs)  228 us
    ppermute x103, starting transfers between devices, along(): return lax.ppermute(shard, axis, pairs)  95.2 us
    dot_general x7, matrix products, against_rows(): lax.dot_general(left, right, (((1,), (1,)), ((), ())), preferred_element_...  27.4 us
    unnamed x136, local copies, waits for them, and re-layouts  22.2 us
    dot_general x7, matrix products, times(): return jnp.dot(left, right, preferred_element_type=f32)  17.1 us
    dot_general x7, matrix products, over_tokens(): lax.dot_general(left, right, (((0,), (0,)), ((), ())), preferred_element_...  15.8 us
  transfers between devices with their start and end apart: 105, of which 39 were waited for; matrix products, arithmetic and copies ran while one was open for 28% of the time, Pallas kernels for 0%

profile of v1, /device:TPU:0, one launch (start us, length us, event | category | flops | bytes accessed | tf_op | source)
XLA Modules:
  0.0 496.5 jit_solution(2638903204630895571)
XLA Ops:
  0.7 3.0 collective-permute-start.9
  25.1 21.6 %collective-permute-done.23 = bf16[2,128,576]{1,2,0:T(8,128)(2,1)S(1)} collective-permute-done((bf16[2,128,576]{1,2,0:T(8,128)(2,1)}, bf16[2,128,576]{1,2,0:T(8,128)(2,1)S(1)}, u32[]{:S(2)}, u32[]{:S(2)}) %collective-permute-start.23) | collective-permute-done | bytes 294944 | tf_op jit(solution)/shard_map/ppermute | solution.py:12
  47.3 4.3 collective-permute-done.24
  57.7 4.6 collective-permute-done.13
  65.9 6.2 %collective-permute-done.37 = bf16[256,1024]{1,0:T(8,128)(2,1)S(1)} collective-permute-done((bf16[256,1024]{1,0:T(8,128)(2,1)S(1)}, bf16[256,1024]{1,0:T(8,128)(2,1)S(1)}, u32[]{:S(2)}, u32[]{:S(2)}) %collective-permute-start.37) | collective-permute-done | bytes 524320 | tf_op jit(solution)/shard_map/ppermute | solution.py:12
  72.6 4.6 collective-permute-done.35
  80.5 18.1 %collective-permute-done.2 = bf16[400,1024]{1,0:T(8,128)(2,1)S(1)} collective-permute-done((bf16[400,1024]{1,0:T(8,128)(2,1)S(1)}, bf16[400,1024]{1,0:T(8,128)(2,1)S(1)}, u32[]{:S(2)}, u32[]{:S(2)}) %collective-permute-start.2) | collective-permute-done | bytes 819232 | tf_op jit(solution)/shard_map/ppermute | solution.py:12
  107.9 2.7 collective-permute-start.7
  116.7 2.9 collective-permute-start.18
  120.6 11.6 %collective-permute-done.18 = bf16[256,1024]{1,0:T(8,128)(2,1)S(1)} collective-permute-done((bf16[256,1024]{1,0:T(8,128)(2,1)S(1)}, bf16[256,1024]{1,0:T(8,128)(2,1)S(1)}, u32[]{:S(2)}, u32[]{:S(2)}) %collective-permute-start.18) | collective-permute-done | bytes 524320 | tf_op jit(solution)/shard_map/ppermute | solution.py:12
  136.9 6.2 %collective-permute-done.20 = bf16[256,1024]{1,0:T(8,128)(2,1)S(1)} collective-permute-done((bf16[256,1024]{1,0:T(8,128)(2,1)S(1)}, bf16[256,1024]{1,0:T(8,128)(2,1)S(1)}, u32[]{:S(2)}, u32[]{:S(2)}) %collective-permute-start.20) | collective-permute-done | bytes 524320 | tf_op jit(solution)/shard_map/ppermute | solution.py:12
  145.1 2.7 fusion.3
  147.8 4.5 fusion.7
  152.3 8.2 %multiply_convert_fusion = (bf16[2048,576]{0,1:T(8,128)(2,1)}, bf16[2048,576]{0,1:T(8,128)(2,1)}, bf16[2048,576]{0,1:T(8,128)(2,1)}) fusion(f32[2048,576]{0,1:T(8,128)} %fusion.7, f32[2048,576]{0,1:T(8,128)S(1)} %fusion.3, bf16[2048,1024]{1,0:T(8,128)(2,1)S(1)} %constant_dynamic-update-slice_fusion.43, bf16[576,1024]{1,0:T(8,128)(2,1)S(1)} %copy-done), kind=kOutput, calls=%fused_computation.1 | convolution fusion | flops 2434793472 | bytes 21889024 | tf_op jit(solution)/shard_map/dot_general | solution.py:136
  160.5 4.5 convolution_convert_fusion.7
  164.9 3.8 convolution_convert_fusion
  168.8 3.5 collective-permute-start.99
  174.2 6.1 %fusion.5 = f32[2048,1024]{1,0:T(8,128)} fusion(bf16[2048,576]{0,1:T(8,128)(2,1)S(1)} %copy-done.47, bf16[72,8,8,128]{3,2,1,0:T(8,128)(2,1)S(1)} %bitcast.455), kind=kOutput, calls=%fused_computation.46 | convolution fusion | flops 2415919104 | bytes 11927552 | tf_op jit(solution)/shard_map/dot_general | solution.py:136
  180.2 6.8 %add_convert_fusion = bf16[2048,1024]{1,0:T(8,128)(2,1)S(1)} fusion(f32[2048,1024]{1,0:T(8,128)} %fusion.5, bf16[2048,576]{0,1:T(8,128)(2,1)} %get-tuple-element.103, bf16[72,8,8,128]{3,2,1,0:T(8,128)(2,1)S(1)} %bitcast.457), kind=kOutput, calls=%fused_computation | convolution fusion | flops 2420113408 | bytes 16121856 | tf_op jit(solution)/shard_map/dot_general | solution.py:136
  189.2 4.3 convolution_convert_fusion.5
  193.6 4.2 collective-permute-done.102
  199.0 2.7 convolution_convert_fusion.6
  201.7 7.2 %collective-permute-start.79 = (bf16[1024,576]{0,1:T(8,128)(2,1)S(1)}, bf16[1024,576]{0,1:T(8,128)(2,1)S(1)}, u32[]{:S(2)}, u32[]{:S(2)}) collective-permute-start(bf16[1024,576]{0,1:T(8,128)(2,1)S(1)} %convolution_convert_fusion.6), channel_id=1, source_target_pairs={{0,8},{24,16},{1,9},{25,17},{2,10},{26,18},{3,11},{27,19},{4,12},{... | collective-permute-start | bytes 3538952 | tf_op jit(solution)/shard_map/ppermute | solution.py:12
  213.3 22.0 %collective-permute-done.79 = bf16[1024,576]{0,1:T(8,128)(2,1)S(1)} collective-permute-done((bf16[1024,576]{0,1:T(8,128)(2,1)S(1)}, bf16[1024,576]{0,1:T(8,128)(2,1)S(1)}, u32[]{:S(2)}, u32[]{:S(2)}) %collective-permute-start.79) | collective-permute-done | bytes 1179680 | tf_op jit(solution)/shard_map/ppermute | solution.py:12
  236.0 22.5 %collective-permute-done.89 = bf16[1024,576]{0,1:T(8,128)(2,1)S(1)} collective-permute-done((bf16[1024,576]{0,1:T(8,128)(2,1)S(1)}, bf16[1024,576]{0,1:T(8,128)(2,1)S(1)}, u32[]{:S(2)}, u32[]{:S(2)}) %collective-permute-start.89) | collective-permute-done | bytes 1179680 | tf_op jit(solution)/shard_map/ppermute | solution.py:12
  268.1 8.6 %collective-permute-done.101 = bf16[288,1024]{1,0:T(8,128)(2,1)S(1)} collective-permute-done((bf16[288,1024]{1,0:T(8,128)(2,1)S(1)}, bf16[288,1024]{1,0:T(8,128)(2,1)S(1)}, u32[]{:S(2)}, u32[]{:S(2)}) %collective-permute-start.101) | collective-permute-done | bytes 589856 | tf_op jit(solution)/shard_map/ppermute | solution.py:12
  277.2 9.3 %collective-permute-done.104 = bf16[288,1024]{1,0:T(8,128)(2,1)S(1)} collective-permute-done((bf16[288,1024]{1,0:T(8,128)(2,1)S(1)}, bf16[288,1024]{1,0:T(8,128)(2,1)S(1)}, u32[]{:S(2)}, u32[]{:S(2)}) %collective-permute-start.104) | collective-permute-done | bytes 589856 | tf_op jit(solution)/shard_map/ppermute | solution.py:12
  291.0 6.6 %collective-permute-done.33 = bf16[256,1024]{1,0:T(8,128)(2,1)S(1)} collective-permute-done((bf16[256,1024]{1,0:T(8,128)(2,1)S(1)}, bf16[256,1024]{1,0:T(8,128)(2,1)S(1)}, u32[]{:S(2)}, u32[]{:S(2)}) %collective-permute-start.33) | collective-permute-done | bytes 524320 | tf_op jit(solution)/shard_map/ppermute | solution.py:12
  301.9 2.4 fusion.100
  323.5 2.7 fusion.94
  363.7 2.9 collective-permute-done.65
  372.3 5.4 %collective-permute-done.49 = bf16[144,1024]{1,0:T(8,128)(2,1)S(1)} collective-permute-done((bf16[144,1024]{1,0:T(8,128)(2,1)S(1)}, bf16[144,1024]{1,0:T(8,128)(2,1)S(1)}, u32[]{:S(2)}, u32[]{:S(2)}) %collective-permute-start.49) | collective-permute-done | bytes 294944 | tf_op jit(solution)/shard_map/ppermute | solution.py:12
  379.3 4.0 collective-permute-done.74
  385.7 3.2 collective-permute-done.66
  391.4 2.7 collective-permute-done.58
  395.3 4.6 collective-permute-start.76
  403.1 3.6 collective-permute-done.76
  406.7 4.4 collective-permute-start.52
  416.5 3.8 collective-permute-done.91
  432.1 4.6 collective-permute-done.93
  436.9 5.8 %collective-permute-done.94 = bf16[128,576]{0,1:T(8,128)(2,1)S(1)} collective-permute-done((bf16[128,576]{0,1:T(8,128)(2,1)S(1)}, bf16[128,576]{0,1:T(8,128)(2,1)S(1)}, u32[]{:S(2)}, u32[]{:S(2)}) %collective-permute-start.94) | collective-permute-done | bytes 147488 | tf_op jit(solution)/shard_map/ppermute | solution.py:12
  442.8 2.5 collective-permute-start.87
  448.4 6.4 %collective-permute-done.83 = bf16[128,576]{0,1:T(8,128)(2,1)S(1)} collective-permute-done((bf16[128,576]{0,1:T(8,128)(2,1)S(1)}, bf16[128,576]{0,1:T(8,128)(2,1)S(1)}, u32[]{:S(2)}, u32[]{:S(2)}) %collective-permute-start.83) | collective-permute-done | bytes 147488 | tf_op jit(solution)/shard_map/ppermute | solution.py:12
  455.6 5.1 %collective-permute-done.84 = bf16[128,576]{0,1:T(8,128)(2,1)S(1)} collective-permute-done((bf16[128,576]{0,1:T(8,128)(2,1)S(1)}, bf16[128,576]{0,1:T(8,128)(2,1)S(1)}, u32[]{:S(2)}, u32[]{:S(2)}) %collective-permute-start.84) | collective-permute-done | bytes 147488 | tf_op jit(solution)/shard_map/ppermute | solution.py:12
  472.8 4.3 collective-permute-done.78
  478.9 3.8 collective-permute-done.70
  483.8 4.6 collective-permute-done.62
  489.4 4.4 collective-permute-done.54
  (509 shorter events, 198.6 us)
Async XLA Ops:
  0.7 20.2 %collective-permute-start.9 = (bf16[128,1024]{1,0:T(8,128)(2,1)}, bf16[128,1024]{1,0:T(8,128)(2,1)}, u32[]{:S(2)}, u32[]{:S(2)}) collective-permute-start(bf16[128,1024]{1,0:T(8,128)(2,1)} %param.14), channel_id=1, source_target_pairs={{0,2},{1,3},{2,0},{3,1},{4,6},{5,7},{6,4},{7,5},{8,10},{9,11},{10,... | collective-permute-start | bytes 786440 | tf_op jit(solution)/shard_map/ppermute | solution.py:12
  3.7 17.4 %collective-permute-start.11 = (bf16[128,1024]{1,0:T(8,128)(2,1)}, bf16[128,1024]{1,0:T(8,128)(2,1)}, u32[]{:S(2)}, u32[]{:S(2)}) collective-permute-start(bf16[128,1024]{1,0:T(8,128)(2,1)} %param.14), channel_id=1, source_target_pairs={{0,4},{1,5},{2,6},{3,7},{4,0},{5,1},{6,2},{7,3},{8,12},{9,13},{10,... | collective-permute-start | bytes 786440 | tf_op jit(solution)/shard_map/ppermute | solution.py:12
  5.2 51.2 %collective-permute-start.34 = (bf16[256,1024]{1,0:T(8,128)(2,1)}, bf16[256,1024]{1,0:T(8,128)(2,1)}, u32[]{:S(2)}, u32[]{:S(2)}) collective-permute-start(bf16[256,1024]{1,0:T(8,128)(2,1)} %bitcast.450), channel_id=1, source_target_pairs={{0,1},{1,0},{2,3},{3,2},{4,5},{5,4},{6,7},{7,6},{8,9},{9,8},{10,11... | collective-permute-start | bytes 1572872 | tf_op jit(solution)/shard_map/ppermute | solution.py:12
  19.3 45.4 %collective-permute-start.1 = (bf16[400,1024]{1,0:T(8,128)(2,1)S(1)}, bf16[400,1024]{1,0:T(8,128)(2,1)S(1)}, u32[]{:S(2)}, u32[]{:S(2)}) collective-permute-start(bf16[400,1024]{1,0:T(8,128)(2,1)S(1)} %pad_maximum_fusion.5), channel_id=1, source_target_pairs={{0,2},{1,3},{2,0},{3,1},{4,6},{5,7},{6,4},{7,5},{8,10},{9,11},{10,... | collective-permute-start | bytes 2457608 | tf_op jit(solution)/shard_map/ppermute | solution.py:12
  20.9 44.8 %collective-permute-start = (bf16[400,1024]{1,0:T(8,128)(2,1)S(1)}, bf16[400,1024]{1,0:T(8,128)(2,1)S(1)}, u32[]{:S(2)}, u32[]{:S(2)}) collective-permute-start(bf16[400,1024]{1,0:T(8,128)(2,1)S(1)} %pad_maximum_fusion.5), channel_id=1, source_target_pairs={{0,4},{1,5},{2,6},{3,7},{4,0},{5,1},{6,2},{7,3},{8,12},{9,13},{10,... | collective-permute-start | bytes 2457608 | tf_op jit(solution)/shard_map/ppermute | solution.py:12
  21.1 25.7 %collective-permute-start.23 = (bf16[2,128,576]{1,2,0:T(8,128)(2,1)}, bf16[2,128,576]{1,2,0:T(8,128)(2,1)S(1)}, u32[]{:S(2)}, u32[]{:S(2)}) collective-permute-start(bf16[2,128,576]{1,2,0:T(8,128)(2,1)} %get-tuple-element.128), channel_id=1, source_target_pairs={{0,2},{1,3},{2,0},{3,1},{4,6},{5,7},{6,4},{7,5},{8,10},{9,11},{10,... | collective-permute-start | bytes 884744 | tf_op jit(solution)/shard_map/ppermute | solution.py:12
  24.0 27.7 %collective-permute-start.24 = (bf16[2,128,576]{1,2,0:T(8,128)(2,1)S(1)}, bf16[2,128,576]{1,2,0:T(8,128)(2,1)S(1)}, u32[]{:S(2)}, u32[]{:S(2)}) collective-permute-start(bf16[2,128,576]{1,2,0:T(8,128)(2,1)S(1)} %copy-done.29), channel_id=1, source_target_pairs={{0,3},{1,2},{2,1},{3,0},{4,7},{5,6},{6,5},{7,4},{8,11},{9,10},{10,... | collective-permute-start | bytes 884744 | tf_op jit(solution)/shard_map/ppermute | solution.py:12
  56.1 22.1 %collective-permute-start.6 = (bf16[400,1024]{1,0:T(8,128)(2,1)S(1)}, bf16[400,1024]{1,0:T(8,128)(2,1)S(1)}, u32[]{:S(2)}, u32[]{:S(2)}) collective-permute-start(bf16[400,1024]{1,0:T(8,128)(2,1)S(1)} %pad_maximum_fusion.5), channel_id=1, source_target_pairs={{0,1},{1,0},{2,3},{3,2},{4,5},{5,4},{6,7},{7,6},{8,9},{9,8},{10,11... | collective-permute-start | bytes 2457608 | tf_op jit(solution)/shard_map/ppermute | solution.py:12
  64.7 55.0 %collective-permute-start.27 = (bf16[2,128,576]{1,2,0:T(8,128)(2,1)S(1)}, bf16[2,128,576]{1,2,0:T(8,128)(2,1)S(1)}, u32[]{:S(2)}, u32[]{:S(2)}) collective-permute-start(bf16[2,128,576]{1,2,0:T(8,128)(2,1)S(1)} %copy-done.30), channel_id=1, source_target_pairs={{0,6},{1,7},{2,4},{3,5},{4,2},{5,3},{6,0},{7,1},{8,14},{9,15},{10,... | collective-permute-start | bytes 884744 | tf_op jit(solution)/shard_map/ppermute | solution.py:12
  65.7 54.0 %collective-permute-start.28 = (bf16[2,128,576]{1,2,0:T(8,128)(2,1)S(1)}, bf16[2,128,576]{1,2,0:T(8,128)(2,1)S(1)}, u32[]{:S(2)}, u32[]{:S(2)}) collective-permute-start(bf16[2,128,576]{1,2,0:T(8,128)(2,1)S(1)} %copy-done.26), channel_id=1, source_target_pairs={{0,7},{1,6},{2,5},{3,4},{4,3},{5,2},{6,1},{7,0},{8,15},{9,14},{10,... | collective-permute-start | bytes 884744 | tf_op jit(solution)/shard_map/ppermute | solution.py:12
  72.1 26.5 %collective-permute-start.2 = (bf16[400,1024]{1,0:T(8,128)(2,1)S(1)}, bf16[400,1024]{1,0:T(8,128)(2,1)S(1)}, u32[]{:S(2)}, u32[]{:S(2)}) collective-permute-start(bf16[400,1024]{1,0:T(8,128)(2,1)S(1)} %broadcast_select_fusion), channel_id=1, source_target_pairs={{0,4},{1,3},{2,6},{3,1},{4,0},{5,7},{6,2},{7,5},{8,12},{9,11},{10,... | collective-permute-start | bytes 2457608 | tf_op jit(solution)/shard_map/ppermute | solution.py:12
  78.2 22.2 %collective-permute-start.4 = (bf16[400,1024]{1,0:T(8,128)(2,1)S(1)}, bf16[400,1024]{1,0:T(8,128)(2,1)S(1)}, u32[]{:S(2)}, u32[]{:S(2)}) collective-permute-start(bf16[400,1024]{1,0:T(8,128)(2,1)S(1)} %collective-permute-done), channel_id=1, source_target_pairs={{0,1},{1,0},{2,3},{3,2},{4,5},{5,4},{6,7},{7,6},{8,9},{9,8},{10,11... | collective-permute-start | bytes 2457608 | tf_op jit(solution)/shard_map/ppermute | solution.py:12
  80.5 36.1 %collective-permute-start.26 = (bf16[2,128,576]{1,2,0:T(8,128)(2,1)S(1)}, bf16[2,128,576]{1,2,0:T(8,128)(2,1)S(1)}, u32[]{:S(2)}, u32[]{:S(2)}) collective-permute-start(bf16[2,128,576]{1,2,0:T(8,128)(2,1)S(1)} %copy-done.27), channel_id=1, source_target_pairs={{0,5},{1,4},{2,7},{3,6},{4,1},{5,0},{6,3},{7,2},{8,13},{9,12},{10,... | collective-permute-start | bytes 884744 | tf_op jit(solution)/shard_map/ppermute | solution.py:12
  100.4 19.6 %collective-permute-start.39 = (bf16[256,1024]{1,0:T(8,128)(2,1)S(1)}, bf16[256,1024]{1,0:T(8,128)(2,1)S(1)}, u32[]{:S(2)}, u32[]{:S(2)}) collective-permute-start(bf16[256,1024]{1,0:T(8,128)(2,1)S(1)} %get-tuple-element.208), channel_id=1, source_target_pairs={{0,4},{1,3},{2,6},{3,1},{4,0},{5,7},{6,2},{7,5},{8,12},{9,11},{10,... | collective-permute-start | bytes 1572872 | tf_op jit(solution)/shard_map/ppermute | solution.py:12
  119.8 17.1 %collective-permute-start.38 = (bf16[256,1024]{1,0:T(8,128)(2,1)S(1)}, bf16[256,1024]{1,0:T(8,128)(2,1)S(1)}, u32[]{:S(2)}, u32[]{:S(2)}) collective-permute-start(bf16[256,1024]{1,0:T(8,128)(2,1)S(1)} %collective-permute-done.37), channel_id=1, source_target_pairs={{0,1},{1,0},{2,3},{3,2},{4,5},{5,4},{6,7},{7,6},{8,9},{9,8},{10,11... | collective-permute-start | bytes 1572872 | tf_op jit(solution)/shard_map/ppermute | solution.py:12
  120.3 22.8 %collective-permute-start.40 = (bf16[256,1024]{1,0:T(8,128)(2,1)S(1)}, bf16[256,1024]{1,0:T(8,128)(2,1)S(1)}, u32[]{:S(2)}, u32[]{:S(2)}) collective-permute-start(bf16[256,1024]{1,0:T(8,128)(2,1)S(1)} %collective-permute-done.39), channel_id=1, source_target_pairs={{0,1},{1,0},{2,3},{3,2},{4,5},{5,4},{6,7},{7,6},{8,9},{9,8},{10,11... | collective-permute-start | bytes 1572872 | tf_op jit(solution)/shard_map/ppermute | solution.py:12
  168.8 24.7 %collective-permute-start.99 = (bf16[288,1024]{1,0:T(8,128)(2,1)S(1)}, bf16[288,1024]{1,0:T(8,128)(2,1)S(1)}, u32[]{:S(2)}, u32[]{:S(2)}) collective-permute-start(bf16[288,1024]{1,0:T(8,128)(2,1)S(1)} %get-tuple-element.154), channel_id=1, source_target_pairs={{0,8},{24,16},{1,9},{25,17},{2,10},{26,18},{3,11},{27,19},{4,12},{... | collective-permute-start | bytes 1769480 | tf_op jit(solution)/shard_map/ppermute | solution.py:12
  172.4 25.4 %collective-permute-start.102 = (bf16[288,1024]{1,0:T(8,128)(2,1)S(1)}, bf16[288,1024]{1,0:T(8,128)(2,1)S(1)}, u32[]{:S(2)}, u32[]{:S(2)}) collective-permute-start(bf16[288,1024]{1,0:T(8,128)(2,1)S(1)} %get-tuple-element.155), channel_id=1, source_target_pairs={{0,8},{24,16},{1,9},{25,17},{2,10},{26,18},{3,11},{27,19},{4,12},{... | collective-permute-start | bytes 1769480 | tf_op jit(solution)/shard_map/ppermute | solution.py:12
  174.1 36.6 %collective-permute-start.30 = (bf16[256,1024]{1,0:T(8,128)(2,1)S(1)}, bf16[256,1024]{1,0:T(8,128)(2,1)S(1)}, u32[]{:S(2)}, u32[]{:S(2)}) collective-permute-start(bf16[256,1024]{1,0:T(8,128)(2,1)S(1)} %get-tuple-element.115), channel_id=1, source_target_pairs={{0,1},{1,0},{2,3},{3,2},{4,5},{5,4},{6,7},{7,6},{8,9},{9,8},{10,11... | collective-permute-start | bytes 1572872 | tf_op jit(solution)/shard_map/ppermute | solution.py:12
  187.2 23.5 %collective-permute-start.42 = (bf16[256,1024]{1,0:T(8,128)(2,1)S(1)}, bf16[256,1024]{1,0:T(8,128)(2,1)S(1)}, u32[]{:S(2)}, u32[]{:S(2)}) collective-permute-start(bf16[256,1024]{1,0:T(8,128)(2,1)S(1)} %get-tuple-element.111), channel_id=1, source_target_pairs={{0,1},{1,0},{2,3},{3,2},{4,5},{5,4},{6,7},{7,6},{8,9},{9,8},{10,11... | collective-permute-start | bytes 1572872 | tf_op jit(solution)/shard_map/ppermute | solution.py:12
  201.7 33.6 %collective-permute-start.79 = (bf16[1024,576]{0,1:T(8,128)(2,1)S(1)}, bf16[1024,576]{0,1:T(8,128)(2,1)S(1)}, u32[]{:S(2)}, u32[]{:S(2)}) collective-permute-start(bf16[1024,576]{0,1:T(8,128)(2,1)S(1)} %convolution_convert_fusion.6), channel_id=1, source_target_pairs={{0,8},{24,16},{1,9},{25,17},{2,10},{26,18},{3,11},{27,19},{4,12},{... | collective-permute-start | bytes 3538952 | tf_op jit(solution)/shard_map/ppermute | solution.py:12
  208.9 49.6 %collective-permute-start.89 = (bf16[1024,576]{0,1:T(8,128)(2,1)S(1)}, bf16[1024,576]{0,1:T(8,128)(2,1)S(1)}, u32[]{:S(2)}, u32[]{:S(2)}) collective-permute-start(bf16[1024,576]{0,1:T(8,128)(2,1)S(1)} %convolution_convert_fusion.5), channel_id=1, source_target_pairs={{0,8},{24,16},{1,9},{25,17},{2,10},{26,18},{3,11},{27,19},{4,12},{... | collective-permute-start | bytes 3538952 | tf_op jit(solution)/shard_map/ppermute | solution.py:12
  210.7 51.9 %collective-permute-start.29 = (bf16[3,256,1024]{2,1,0:T(8,128)(2,1)S(1)}, bf16[3,256,1024]{2,1,0:T(8,128)(2,1)S(1)}, u32[]{:S(2)}, u32[]{:S(2)}) collective-permute-start(bf16[3,256,1024]{2,1,0:T(8,128)(2,1)S(1)} %pad_maximum_fusion.1), channel_id=1, source_target_pairs={{0,1},{1,0},{2,3},{3,2},{4,5},{5,4},{6,7},{7,6},{8,9},{9,8},{10,11... | collective-permute-start | bytes 4718600 | tf_op jit(solution)/shard_map/ppermute | solution.py:12
  211.7 54.0 %collective-permute-start.41 = (bf16[3,256,1024]{2,1,0:T(8,128)(2,1)S(1)}, bf16[3,256,1024]{2,1,0:T(8,128)(2,1)S(1)}, u32[]{:S(2)}, u32[]{:S(2)}) collective-permute-start(bf16[3,256,1024]{2,1,0:T(8,128)(2,1)S(1)} %pad_maximum_fusion.2), channel_id=1, source_target_pairs={{0,1},{1,0},{2,3},{3,2},{4,5},{5,4},{6,7},{7,6},{8,9},{9,8},{10,11... | collective-permute-start | bytes 4718600 | tf_op jit(solution)/shard_map/ppermute | solution.py:12
  212.7 48.6 %collective-permute-start.31 = (bf16[256,1024]{1,0:T(8,128)(2,1)S(1)}, bf16[256,1024]{1,0:T(8,128)(2,1)S(1)}, u32[]{:S(2)}, u32[]{:S(2)}) collective-permute-start(bf16[256,1024]{1,0:T(8,128)(2,1)S(1)} %add_convert_fusion.10), channel_id=1, source_target_pairs={{0,2},{1,5},{2,0},{3,7},{4,6},{5,1},{6,4},{7,3},{8,10},{9,13},{10,... | collective-permute-start | bytes 1572872 | tf_op jit(solution)/shard_map/ppermute | solution.py:12
  235.3 30.1 %collective-permute-start.43 = (bf16[256,1024]{1,0:T(8,128)(2,1)S(1)}, bf16[256,1024]{1,0:T(8,128)(2,1)S(1)}, u32[]{:S(2)}, u32[]{:S(2)}) collective-permute-start(bf16[256,1024]{1,0:T(8,128)(2,1)S(1)} %add_convert_fusion.9), channel_id=1, source_target_pairs={{0,2},{1,5},{2,0},{3,7},{4,6},{5,1},{6,4},{7,3},{8,10},{9,13},{10,... | collective-permute-start | bytes 1572872 | tf_op jit(solution)/shard_map/ppermute | solution.py:12
  258.5 18.1 %collective-permute-start.101 = (bf16[288,1024]{1,0:T(8,128)(2,1)S(1)}, bf16[288,1024]{1,0:T(8,128)(2,1)S(1)}, u32[]{:S(2)}, u32[]{:S(2)}) collective-permute-start(bf16[288,1024]{1,0:T(8,128)(2,1)S(1)} %add_convert_fusion.7), channel_id=1, source_target_pairs={{8,0},{16,24},{9,1},{17,25},{10,2},{18,26},{11,3},{19,27},{12,4},{... | collective-permute-start | bytes 1769480 | tf_op jit(solution)/shard_map/ppermute | solution.py:12
  261.3 25.2 %collective-permute-start.104 = (bf16[288,1024]{1,0:T(8,128)(2,1)S(1)}, bf16[288,1024]{1,0:T(8,128)(2,1)S(1)}, u32[]{:S(2)}, u32[]{:S(2)}) collective-permute-start(bf16[288,1024]{1,0:T(8,128)(2,1)S(1)} %add_convert_fusion.5), channel_id=1, source_target_pairs={{8,0},{16,24},{9,1},{17,25},{10,2},{18,26},{11,3},{19,27},{12,4},{... | collective-permute-start | bytes 1769480 | tf_op jit(solution)/shard_map/ppermute | solution.py:12
  262.6 89.2 %collective-permute-start.80 = (bf16[1024,576]{0,1:T(8,128)(2,1)S(1)}, bf16[1024,576]{0,1:T(8,128)(2,1)}, u32[]{:S(2)}, u32[]{:S(2)}) collective-permute-start(bf16[1024,576]{0,1:T(8,128)(2,1)S(1)} %add_convert_fusion.4), channel_id=1, source_target_pairs={{8,16},{16,8},{9,17},{17,9},{10,18},{18,10},{11,19},{19,11},{12,20... | collective-permute-start | bytes 3538952 | tf_op jit(solution)/shard_map/ppermute | solution.py:12
  265.3 25.7 %collective-permute-start.32 = (bf16[256,1024]{1,0:T(8,128)(2,1)S(1)}, bf16[256,1024]{1,0:T(8,128)(2,1)S(1)}, u32[]{:S(2)}, u32[]{:S(2)}) collective-permute-start(bf16[256,1024]{1,0:T(8,128)(2,1)S(1)} %get-tuple-element.108), channel_id=1, source_target_pairs={{0,2},{1,3},{2,0},{3,1},{4,6},{5,7},{6,4},{7,5},{8,10},{9,11},{10,... | collective-permute-start | bytes 1572872 | tf_op jit(solution)/shard_map/ppermute | solution.py:12
  266.3 22.5 %collective-permute-start.44 = (bf16[256,1024]{1,0:T(8,128)(2,1)S(1)}, bf16[256,1024]{1,0:T(8,128)(2,1)S(1)}, u32[]{:S(2)}, u32[]{:S(2)}) collective-permute-start(bf16[256,1024]{1,0:T(8,128)(2,1)S(1)} %get-tuple-element.106), channel_id=1, source_target_pairs={{0,2},{1,3},{2,0},{3,1},{4,6},{5,7},{6,4},{7,5},{8,10},{9,11},{10,... | collective-permute-start | bytes 1572872 | tf_op jit(solution)/shard_map/ppermute | solution.py:12
  288.7 65.0 %collective-permute-start.90 = (bf16[1024,576]{0,1:T(8,128)(2,1)}, bf16[1024,576]{0,1:T(8,128)(2,1)}, u32[]{:S(2)}, u32[]{:S(2)}) collective-permute-start(bf16[1024,576]{0,1:T(8,128)(2,1)} %add_convert_fusion.2), channel_id=1, source_target_pairs={{8,16},{16,8},{9,17},{17,9},{10,18},{18,10},{11,19},{19,11},{12,20... | collective-permute-start | bytes 3538952 | tf_op jit(solution)/shard_map/ppermute | solution.py:12
  306.1 43.0 %collective-permute-start.72 = (bf16[128,1024]{1,0:T(8,128)(2,1)}, bf16[128,1024]{1,0:T(8,128)(2,1)}, u32[]{:S(2)}, u32[]{:S(2)}) collective-permute-start(bf16[128,1024]{1,0:T(8,128)(2,1)} %get-tuple-element.133), channel_id=1, source_target_pairs={{0,1},{1,0},{2,3},{3,2},{4,5},{5,4},{6,7},{7,6},{8,9},{9,8},{10,11... | collective-permute-start | bytes 786440 | tf_op jit(solution)/shard_map/ppermute | solution.py:12
  307.1 54.5 %collective-permute-start.71 = (bf16[3,128,1024]{2,1,0:T(8,128)(2,1)}, bf16[3,128,1024]{2,1,0:T(8,128)(2,1)}, u32[]{:S(2)}, u32[]{:S(2)}) collective-permute-start(bf16[3,128,1024]{2,1,0:T(8,128)(2,1)} %pad_maximum_fusion.8), channel_id=1, source_target_pairs={{0,1},{1,0},{2,3},{3,2},{4,5},{5,4},{6,7},{7,6},{8,9},{9,8},{10,11... | collective-permute-start | bytes 2359304 | tf_op jit(solution)/shard_map/ppermute | solution.py:12
  310.8 39.3 %collective-permute-start.64 = (bf16[128,1024]{1,0:T(8,128)(2,1)}, bf16[128,1024]{1,0:T(8,128)(2,1)}, u32[]{:S(2)}, u32[]{:S(2)}) collective-permute-start(bf16[128,1024]{1,0:T(8,128)(2,1)} %get-tuple-element.141), channel_id=1, source_target_pairs={{0,1},{1,0},{2,3},{3,2},{4,5},{5,4},{6,7},{7,6},{8,9},{9,8},{10,11... | collective-permute-start | bytes 786440 | tf_op jit(solution)/shard_map/ppermute | solution.py:12
  349.1 18.8 %collective-permute-start.63 = (bf16[3,128,1024]{2,1,0:T(8,128)(2,1)}, bf16[3,128,1024]{2,1,0:T(8,128)(2,1)S(1)}, u32[]{:S(2)}, u32[]{:S(2)}) collective-permute-start(bf16[3,128,1024]{2,1,0:T(8,128)(2,1)} %pad_maximum_fusion.7), channel_id=1, source_target_pairs={{0,1},{1,0},{2,3},{3,2},{4,5},{5,4},{6,7},{7,6},{8,9},{9,8},{10,11... | collective-permute-start | bytes 2359304 | tf_op jit(solution)/shard_map/ppermute | solution.py:12
  357.3 21.7 %collective-permute-start.47 = (bf16[3,144,1024]{2,1,0:T(8,128)(2,1)S(1)}, bf16[3,144,1024]{2,1,0:T(8,128)(2,1)S(1)}, u32[]{:S(2)}, u32[]{:S(2)}) collective-permute-start(bf16[3,144,1024]{2,1,0:T(8,128)(2,1)S(1)} %copy-done.23), channel_id=1, source_target_pairs={{0,1},{1,0},{2,3},{3,2},{4,5},{5,4},{6,7},{7,6},{8,9},{9,8},{10,11... | collective-permute-start | bytes 2654216 | tf_op jit(solution)/shard_map/ppermute | solution.py:12
  366.5 49.1 %collective-permute-start.81 = (bf16[1024,576]{0,1:T(8,128)(2,1)S(1)}, bf16[1024,576]{0,1:T(8,128)(2,1)S(1)}, u32[]{:S(2)}, u32[]{:S(2)}) collective-permute-start(bf16[1024,576]{0,1:T(8,128)(2,1)S(1)} %add_convert_fusion.3), channel_id=1, source_target_pairs={{8,0},{16,24},{9,1},{17,25},{10,2},{18,26},{11,3},{19,27},{12,4},{... | collective-permute-start | bytes 3538952 | tf_op jit(solution)/shard_map/ppermute | solution.py:12
  394.0 26.3 %collective-permute-start.91 = (bf16[1024,576]{0,1:T(8,128)(2,1)S(1)}, bf16[1024,576]{0,1:T(8,128)(2,1)S(1)}, u32[]{:S(2)}, u32[]{:S(2)}) collective-permute-start(bf16[1024,576]{0,1:T(8,128)(2,1)S(1)} %add_convert_fusion.1), channel_id=1, source_target_pairs={{8,0},{16,24},{9,1},{17,25},{10,2},{18,26},{11,3},{19,27},{12,4},{... | collective-permute-start | bytes 3538952 | tf_op jit(solution)/shard_map/ppermute | solution.py:12
  420.9 26.5 %collective-permute-start.98 = (bf16[128,576]{0,1:T(8,128)(2,1)S(1)}, bf16[128,576]{0,1:T(8,128)(2,1)S(1)}, u32[]{:S(2)}, u32[]{:S(2)}) collective-permute-start(bf16[128,576]{0,1:T(8,128)(2,1)S(1)} %get-tuple-element.156), channel_id=1, source_target_pairs={{0,7},{1,6},{2,5},{3,4},{4,3},{5,2},{6,1},{7,0},{8,15},{9,14},{10,... | collective-permute-start | bytes 442376 | tf_op jit(solution)/shard_map/ppermute | solution.py:12
  421.3 24.3 %collective-permute-start.97 = (bf16[128,576]{0,1:T(8,128)(2,1)S(1)}, bf16[128,576]{0,1:T(8,128)(2,1)S(1)}, u32[]{:S(2)}, u32[]{:S(2)}) collective-permute-start(bf16[128,576]{0,1:T(8,128)(2,1)S(1)} %get-tuple-element.157), channel_id=1, source_target_pairs={{0,6},{1,7},{2,4},{3,5},{4,2},{5,3},{6,0},{7,1},{8,14},{9,15},{10,... | collective-permute-start | bytes 442376 | tf_op jit(solution)/shard_map/ppermute | solution.py:12
  423.1 22.1 %collective-permute-start.96 = (bf16[128,576]{0,1:T(8,128)(2,1)S(1)}, bf16[128,576]{0,1:T(8,128)(2,1)S(1)}, u32[]{:S(2)}, u32[]{:S(2)}) collective-permute-start(bf16[128,576]{0,1:T(8,128)(2,1)S(1)} %get-tuple-element.158), channel_id=1, source_target_pairs={{0,5},{1,4},{2,7},{3,6},{4,1},{5,0},{6,3},{7,2},{8,13},{9,12},{10,... | collective-permute-start | bytes 442376 | tf_op jit(solution)/shard_map/ppermute | solution.py:12
  442.7 23.4 %collective-permute-start.88 = (bf16[128,576]{0,1:T(8,128)(2,1)S(1)}, bf16[128,576]{0,1:T(8,128)(2,1)S(1)}, u32[]{:S(2)}, u32[]{:S(2)}) collective-permute-start(bf16[128,576]{0,1:T(8,128)(2,1)S(1)} %get-tuple-element.163), channel_id=1, source_target_pairs={{0,7},{1,6},{2,5},{3,4},{4,3},{5,2},{6,1},{7,0},{8,15},{9,14},{10,... | collective-permute-start | bytes 442376 | tf_op jit(solution)/shard_map/ppermute | solution.py:12
  442.8 22.0 %collective-permute-start.87 = (bf16[128,576]{0,1:T(8,128)(2,1)S(1)}, bf16[128,576]{0,1:T(8,128)(2,1)S(1)}, u32[]{:S(2)}, u32[]{:S(2)}) collective-permute-start(bf16[128,576]{0,1:T(8,128)(2,1)S(1)} %get-tuple-element.164), channel_id=1, source_target_pairs={{0,6},{1,7},{2,4},{3,5},{4,2},{5,3},{6,0},{7,1},{8,14},{9,15},{10,... | collective-permute-start | bytes 442376 | tf_op jit(solution)/shard_map/ppermute | solution.py:12
  445.3 18.2 %collective-permute-start.86 = (bf16[128,576]{0,1:T(8,128)(2,1)S(1)}, bf16[128,576]{0,1:T(8,128)(2,1)S(1)}, u32[]{:S(2)}, u32[]{:S(2)}) collective-permute-start(bf16[128,576]{0,1:T(8,128)(2,1)S(1)} %get-tuple-element.165), channel_id=1, source_target_pairs={{0,5},{1,4},{2,7},{3,6},{4,1},{5,0},{6,3},{7,2},{8,13},{9,12},{10,... | collective-permute-start | bytes 442376 | tf_op jit(solution)/shard_map/ppermute | solution.py:12
  463.4 19.3 %collective-permute-start.70 = (bf16[128,1024]{1,0:T(8,128)(2,1)}, bf16[128,1024]{1,0:T(8,128)(2,1)}, u32[]{:S(2)}, u32[]{:S(2)}) collective-permute-start(bf16[128,1024]{1,0:T(8,128)(2,1)} %add_convert_fusion.17), channel_id=1, source_target_pairs={{8,0},{16,24},{9,1},{17,25},{10,2},{18,26},{11,3},{19,27},{12,4},{... | collective-permute-start | bytes 786440 | tf_op jit(solution)/shard_map/ppermute | solution.py:12
  464.8 23.6 %collective-permute-start.62 = (bf16[128,1024]{1,0:T(8,128)(2,1)}, bf16[128,1024]{1,0:T(8,128)(2,1)}, u32[]{:S(2)}, u32[]{:S(2)}) collective-permute-start(bf16[128,1024]{1,0:T(8,128)(2,1)} %add_convert_fusion.20), channel_id=1, source_target_pairs={{8,0},{16,24},{9,1},{17,25},{10,2},{18,26},{11,3},{19,27},{12,4},{... | collective-permute-start | bytes 786440 | tf_op jit(solution)/shard_map/ppermute | solution.py:12
  471.5 22.3 %collective-permute-start.54 = (bf16[144,1024]{1,0:T(8,128)(2,1)S(1)}, bf16[144,1024]{1,0:T(8,128)(2,1)S(1)}, u32[]{:S(2)}, u32[]{:S(2)}) collective-permute-start(bf16[144,1024]{1,0:T(8,128)(2,1)S(1)} %add_convert_fusion.11), channel_id=1, source_target_pairs={{8,0},{16,24},{9,1},{17,25},{10,2},{18,26},{11,3},{19,27},{12,4},{... | collective-permute-start | bytes 884744 | tf_op jit(solution)/shard_map/ppermute | solution.py:12
  (107 other events, 1071.3 us)

commit v2 on v1

v2 whole, which is shorter than its diff:
```python
import jax
import jax.numpy as jnp
from jax import lax
from jax.sharding import PartitionSpec as P

epsilon = 1e-05
bf16 = jnp.bfloat16
f32 = jnp.float32


def along(shard, axis, pairs):
    return lax.ppermute(shard, axis, pairs)


def after(value, *others):
    return lax.optimization_barrier((value,) + others)[0]


def flip(shard, bits):
    peers = lax.axis_size("fsdp")
    return along(shard, "fsdp", [(i, i ^ bits) for i in range(peers)])


def flip_by_core(shard, even_bits, odd_bits):
    peers = lax.axis_size("fsdp")
    return along(
        shard, "fsdp", [(i, i ^ (odd_bits if i & 1 else even_bits)) for i in range(peers)]
    )


def is_cube():
    return lax.axis_size("fsdp") == 8


def on_odd_core():
    return (lax.axis_index("fsdp") & 1) == 1


def gather_parts(shard):
    if not is_cube():
        return [lax.all_gather(shard, "fsdp", axis=0)], ()
    from_x = flip(shard, 2)
    from_y = flip(shard, 4)
    across = flip_by_core(jnp.where(on_odd_core(), from_y, from_x), 4, 2)
    mine = jnp.stack([shard, from_x, from_y])
    theirs = flip(mine, 1)
    last = flip(across, 1)
    return [theirs, last[None], mine, across[None]], (from_x, from_y)


def gather(shard):
    parts, first = gather_parts(shard)
    return jnp.concatenate(parts, axis=0), first


def places():
    return [1, 3, 5, 7, 0, 2, 4, 6] if is_cube() else list(range(lax.axis_size("fsdp")))


def scatter(theirs, mine):
    peers = lax.axis_size("fsdp")
    theirs = theirs.astype(bf16)
    if not is_cube():
        whole = jnp.concatenate([theirs, mine.astype(bf16)], axis=0)
        whole = whole.reshape(peers, whole.shape[0] // peers, -1)
        return lax.psum_scatter(whole, "fsdp", scatter_dimension=0).astype(f32), ()
    size = mine.shape[0] // 4
    near = flip(theirs, 1)
    mine = [mine[k * size : (k + 1) * size].astype(f32) for k in range(4)]
    mine = [mine[k] + near[k * size : (k + 1) * size] for k in range(4)]
    odd = on_odd_core()
    across = flip_by_core(mine[3].astype(bf16), 2, 4)
    zero = jnp.zeros((), f32)
    to_x = (mine[1] + jnp.where(odd, across.astype(f32), zero)).astype(bf16)
    to_y = (mine[2] + jnp.where(odd, zero, across.astype(f32))).astype(bf16)
    return mine[0] + flip(to_x, 2) + flip(to_y, 4), (near, across)


def exchange_parts(blocks):
    if not is_cube():
        return [lax.all_to_all(blocks, "fsdp", 0, 0)]
    chip, odd = lax.axis_index("fsdp") >> 1, on_odd_core()
    pairs = blocks.reshape((4, 2) + blocks.shape[1:])
    to_even, to_odd = pairs[:, 0], pairs[:, 1]
    kept = jnp.where(odd, to_odd, to_even)
    came = flip(jnp.where(odd, to_even, to_odd), 1)
    both = jnp.stack([jnp.where(odd, came, kept), jnp.where(odd, kept, came)], axis=1)
    return [both] + [
        flip(lax.dynamic_index_in_dim(both, chip ^ k, 0, keepdims=False), 2 * k)
        for k in (1, 2, 3)
    ]


def exchanged(parts):
    if not is_cube():
        return parts[0]
    chip, result = lax.axis_index("fsdp") >> 1, parts[0]
    for k in (1, 2, 3):
        result = lax.dynamic_update_index_in_dim(result, parts[k], chip ^ k, 0)
    return result.reshape((8,) + result.shape[2:])


def relabel(columns, back=False):
    peers = lax.axis_size("fsdp")
    if not is_cube():
        return columns
    size = columns.shape[-1] // peers
    me = lax.axis_index("fsdp")
    blocks = [columns[..., k * size : (k + 1) * size] for k in range(peers)]
    if back:
        blocks = [blocks[places().index(j)] for j in range(peers)]
    for bit in (1, 2, 4):
        swap = (me & bit) != 0
        blocks = [jnp.where(swap, blocks[k ^ bit], blocks[k]) for k in range(peers)]
    if not back:
        blocks = [blocks[j] for j in places()]
    return jnp.concatenate(blocks, axis=-1)


def in_line():
    return lax.axis_size("dp") == 4


def inward(term):
    if not in_line():
        return lax.psum(term, "dp")
    return along(term, "dp", [(0, 1), (3, 2)])


def between(pair):
    return along(pair, "dp", [(1, 2), (2, 1)]) if in_line() else pair


def outward(total):
    return along(total, "dp", [(1, 0), (2, 3)]) if in_line() else total


def add_pair(one, other):
    return (one.astype(f32) + other.astype(f32)).astype(bf16) if in_line() else other


def settle(total, came):
    if not in_line():
        return total
    inner = (lax.axis_index("dp") == 1) | (lax.axis_index("dp") == 2)
    return jnp.where(inner, total, came)


def together(*values):
    return lax.optimization_barrier(values)


def from_behind(shard, axis, by):
    peers = lax.axis_size(axis)
    pairs = [(i, i + by) for i in range(peers) if 0 <= i + by < peers]
    return lax.ppermute(shard, axis, pairs)


def inverse_rms(values):
    return lax.rsqrt(jnp.mean(values * values, axis=-1, keepdims=True) + epsilon)


def norm_back(values, scale, gain, incoming):
    normed = values * scale
    gain_grad = jnp.sum(incoming * normed, axis=0)
    weighted = incoming * gain
    projection = jnp.mean(weighted * normed, axis=-1, keepdims=True)
    return (scale * (weighted - normed * projection), gain_grad)


def times(left, right):
    return jnp.dot(left, right, preferred_element_type=f32)


def over_tokens(left, right):
    return lax.dot_general(left, right, (((0,), (0,)), ((), ())), preferred_element_type=f32)


def against_rows(left, right):
    return lax.dot_general(left, right, (((1,), (1,)), ((), ())), preferred_element_type=f32)


def per_device(inputs, norm_in, w_in, taps, w_out, norm_mid, w_gate, w_up, w_down, cotangent):
    micros, rows, width = inputs.shape
    peers = lax.axis_size("fsdp")
    reach = taps.shape[0] - 1
    owned = w_in.shape[0]
    hidden = w_down.shape[0]
    all_rows = micros * rows

    gate_up = jnp.concatenate(
        [jnp.transpose(w.reshape(owned, peers, hidden), (1, 0, 2)) for w in (w_gate, w_up)],
        axis=1,
    )
    gate_up = exchange_parts(gate_up)
    whole, first = gather(w_in)
    full_in = whole.reshape(width, 3 * width)
    smalls = jnp.concatenate([norm_in[None], norm_mid[None], taps], axis=0)
    smalls = jnp.pad(smalls, ((0, 8 - (reach + 3)), (0, 0)))
    smalls = jnp.transpose(gather(smalls)[0][:, : reach + 3], (1, 0, 2))
    smalls = relabel(smalls.reshape(reach + 3, width), back=True).astype(f32)
    gain_in, gain_mid, tap_values = smalls[0], smalls[1], smalls[2:]
    out_parts, first = gather_parts(after(w_out, *first))
    full_out = jnp.concatenate(out_parts, axis=0).reshape(width, width)
    grad_out = cotangent.reshape(all_rows, width)
    grad_out_parts = gather_parts(after(grad_out, *gate_up[1:], *out_parts[-1:]))[0]
    early = gate_up[1:]
    gate_up = exchanged(gate_up)
    own_gate = gate_up[:, :owned].reshape(width, hidden)
    own_up = gate_up[:, owned:].reshape(width, hidden)

    resid = inputs.reshape(all_rows, width).astype(f32)
    scale_in = inverse_rms(resid)
    normed_in = relabel((resid * scale_in * gain_in).astype(bf16))
    normed_in = after(normed_in, *early)
    projected = times(normed_in, full_in)
    gate_b = projected[:, :width]
    gate_c = projected[:, width : 2 * width]
    values = projected[:, 2 * width :]
    mixed = (gate_b * values).astype(bf16).reshape(micros, rows, width)
    earlier = from_behind(mixed[:, rows - reach :], "fsdp", 1)
    extended = jnp.concatenate([earlier, mixed], axis=1).astype(f32)
    convolved = jnp.zeros((micros, rows, width), f32)
    for offset in range(reach + 1):
        convolved = convolved + tap_values[offset] * extended[:, offset : offset + rows]
    convolved = convolved.reshape(all_rows, width)
    gated = relabel((gate_c * convolved).astype(bf16))
    middle = resid + times(gated, full_out)
    scale_mid = inverse_rms(middle)
    normed_mid = (middle * scale_mid * gain_mid).astype(bf16)

    normed_mid = after(normed_mid, *grad_out_parts)
    grad_out_all = jnp.concatenate(grad_out_parts, axis=0).reshape(peers * all_rows, width)
    normed_all = gather(normed_mid)[0].reshape(peers * all_rows, width)
    gate_pre = times(normed_all, own_gate)
    up_pre = times(normed_all, own_up)
    sigmoid_gate = jax.nn.sigmoid(gate_pre)
    activ = (gate_pre * sigmoid_gate * up_pre).astype(bf16)
    grad_activ = against_rows(grad_out_all, w_down)
    grad_gate = (
        grad_activ * up_pre * sigmoid_gate * (1.0 + gate_pre * (1.0 - sigmoid_gate))
    ).astype(bf16)
    grad_up = (grad_activ * gate_pre * sigmoid_gate).astype(bf16)
    half = peers * all_rows // 2

    def through_gates(part):
        return (
            against_rows(grad_gate[part], own_gate) + against_rows(grad_up[part], own_up)
        ).astype(bf16)

    theirs, ours = through_gates(slice(None, half)), through_gates(slice(half, None))
    grad_normed_mid, steps_mid = scatter(theirs, ours)

    gate_now, up_now = together(grad_gate, grad_up, theirs, ours)[:2]
    term_gate = over_tokens(normed_all, gate_now).astype(bf16)
    came_gate = inward(term_gate)
    up_now, activ_now = together(up_now, activ, term_gate)[:2]
    term_up = over_tokens(normed_all, up_now).astype(bf16)
    term_down = over_tokens(activ_now, grad_out_all).astype(bf16)
    half = peers * all_rows // 2
    final_theirs = times(activ_now[:half], w_down).astype(bf16)
    final_ours = times(activ_now[half:], w_down).astype(bf16)
    grad_normed_mid, came_gate, term_up = together(
        grad_normed_mid, came_gate, after(term_up, term_down, final_theirs, final_ours)
    )
    pair_gate = add_pair(term_gate, came_gate)
    far_gate = between(pair_gate)
    came_up = inward(term_up)

    back_mid, gain_mid_grad = norm_back(middle, scale_mid, gain_mid, grad_normed_mid)
    grad_middle = grad_out.astype(f32) + back_mid
    grad_branch = grad_middle.astype(bf16)
    grad_gated = relabel(against_rows(grad_branch, full_out), back=True)
    grad_c = grad_gated * convolved
    grad_conv = (grad_gated * gate_c).astype(bf16).reshape(micros, rows, width)
    later = from_behind(grad_conv[:, :reach], "fsdp", -1)
    ext_grad = jnp.concatenate([grad_conv, later], axis=1).astype(f32)
    grad_mixed = jnp.zeros((micros, rows, width), f32)
    tap_terms = []
    for offset in range(reach + 1):
        grad_mixed = (
            grad_mixed + tap_values[offset] * ext_grad[:, reach - offset : reach - offset + rows]
        )
        tap_terms.append(
            jnp.sum(extended[:, offset : offset + rows] * ext_grad[:, :rows], axis=(0, 1))
        )
    grad_mixed = grad_mixed.reshape(all_rows, width)
    grad_proj = [
        (grad_mixed * values).astype(bf16),
        grad_c.astype(bf16),
        (grad_mixed * gate_b).astype(bf16),
    ]

    grad_branch, far_gate, came_up, *grad_proj = together(
        grad_branch, far_gate, came_up, *grad_proj
    )
    half = width // 2
    normed_theirs, normed_ours = normed_in[:, :half], normed_in[:, half:]
    grad_b_v = jnp.concatenate([grad_proj[0], grad_proj[2]], axis=1)
    rows_out_c = scatter(
        *[
            jnp.concatenate([over_tokens(p, grad_branch), over_tokens(q, grad_proj[1])], axis=1)
            for p, q in ((gated[:, :half], normed_theirs), (gated[:, half:], normed_ours))
        ]
    )[0].astype(bf16)
    grad_normed_in = relabel(
        against_rows(jnp.concatenate(grad_proj, axis=1), full_in), back=True
    )
    back_in, gain_in_grad = norm_back(resid, scale_in, gain_in, grad_normed_in)
    grad_inputs = (grad_middle + back_in).reshape(micros, rows, width)
    smalls = relabel(jnp.stack([gain_in_grad, gain_mid_grad] + tap_terms))
    smalls = jnp.pad(jnp.transpose(smalls), ((0, 0), (0, 128 - (reach + 3))))
    rows_b_v = scatter(
        jnp.concatenate([over_tokens(normed_theirs, grad_b_v), smalls[:half]], axis=1),
        jnp.concatenate([over_tokens(normed_ours, grad_b_v), smalls[half:]], axis=1),
    )[0].astype(bf16)

    total_gate = add_pair(pair_gate, far_gate)
    out_gate = outward(total_gate)
    pair_up = add_pair(term_up, came_up)
    far_up = between(pair_up)
    came_down = inward(after(term_down, far_gate))

    rows_out_c, out_gate, far_up, came_down = together(rows_out_c, out_gate, far_up, came_down)
    total_up = add_pair(pair_up, far_up)
    out_up = outward(total_up)
    pair_down = add_pair(term_down, came_down)
    far_down = between(pair_down)
    came_out_c = inward(rows_out_c)
    mine_gate = exchange_parts(settle(total_gate, out_gate).reshape(peers, owned, hidden))
    final = scatter(after(final_theirs, rows_out_c), final_ours)[0]
    block_out = (middle + final).astype(bf16).reshape(micros, rows, width)

    rows_b_v, out_up, far_down, came_out_c, *mine_gate = together(
        rows_b_v, out_up, far_down, came_out_c, *mine_gate
    )
    total_down = add_pair(pair_down, far_down)
    out_down = outward(total_down)
    pair_out_c = add_pair(rows_out_c, came_out_c)
    far_out_c = between(pair_out_c)
    came_b_v = inward(rows_b_v)
    mine_up = exchange_parts(settle(total_up, out_up).reshape(peers, owned, hidden))

    out_down, far_out_c, came_b_v, *mine_up = together(out_down, far_out_c, came_b_v, *mine_up)
    total_out_c = add_pair(pair_out_c, far_out_c)
    out_out_c = outward(total_out_c)
    pair_b_v = add_pair(rows_b_v, came_b_v)
    total_b_v = add_pair(pair_b_v, between(pair_b_v))
    grad_w_down = settle(total_down, out_down).astype(f32)
    grad_w_gate, grad_w_up = [
        jnp.transpose(exchanged(parts), (1, 0, 2)).reshape(owned, peers * hidden).astype(f32)
        for parts in (mine_gate, mine_up)
    ]
    total_out_c = settle(total_out_c, out_out_c).astype(f32)
    total_b_v = settle(total_b_v, outward(total_b_v)).astype(f32)
    grad_w_out = total_out_c[:, :width]
    grad_w_in = jnp.concatenate(
        [total_b_v[:, :width], total_out_c[:, width:], total_b_v[:, width : 2 * width]], axis=1
    )
    smalls = jnp.transpose(total_b_v[:, 2 * width : 2 * width + reach + 3])
    return (
        block_out,
        grad_inputs,
        smalls[0],
        grad_w_in,
        smalls[2:],
        grad_w_out,
        smalls[1],
        grad_w_gate,
        grad_w_up,
        grad_w_down,
    )


def solution(mesh):
    return jax.shard_map(
        per_device,
        mesh=mesh,
        in_specs=(
            P("dp", "fsdp", None),
            P("fsdp"),
            P("fsdp", None),
            P(None, "fsdp"),
            P("fsdp", None),
            P("fsdp"),
            P("fsdp", None),
            P("fsdp", None),
            P("fsdp", None),
            P("dp", "fsdp", None),
        ),
        out_specs=(
            P("dp", "fsdp", None),
            P("dp", "fsdp", None),
            P("fsdp"),
            P("fsdp", None),
            P(None, "fsdp"),
            P("fsdp", None),
            P("fsdp"),
            P("fsdp", None),
            P("fsdp", None),
            P("fsdp", None),
        ),
        check_vma=False,
    )
```

time: 504 us -> 433 us (0.86)
  waiting for transfers between devices: 228 us -> 140 us
  other arithmetic: 55.5 us -> 73 us
    ppermute x103 -> x68, waiting for transfers between devices: 228 us -> 139 us  [along(): return lax.ppermute(shard, axis, pairs)]
    convert_element_type x38 -> x28, other arithmetic: 25.1 us -> 35.2 us  [the longest x10 13.3 us: add_pair(): (one.astype(f32) + other.astype(f32)).astype(bf16)]
    dot_general x7, matrix products: 27.4 us -> 18.9 us  [against_rows(): lax.dot_general(left, right, (((1,), (1,)), ((), ())), preferred_element_...]
    dot_general x7 -> x6, matrix products: 17.1 us -> 23.3 us  [times(): return jnp.dot(left, right, preferred_element_type=f32)]
    convert_element_type x8 -> x2, local copies, waits for them, and re-layouts: 9.01 us -> 3.12 us  [per_device(): jnp.transpose(exchanged(parts), (1, 0, 2)).reshape(owned, peers * hidden)]
    another operation x6 -> x4, local copies, waits for them, and re-layouts: 3.21 us -> 9.06 us  [the longest x2 7.98 us: exchange_parts(): pairs = blocks.reshape((4, 2) + blocks.shape[1:])]
    pad x9 -> x0, local copies, waits for them, and re-layouts: 5.71 us -> none  [the longest x8 5.09 us: per_device(): jnp.pad(part, (0, small_rows * width - part.shape[0]))]
    unnamed x136 -> x180, local copies, waits for them, and re-layouts: 22.2 us -> 24.8 us
  transfers between devices with their start and end apart: 105 -> 70, of which waited for: 39 -> 29; matrix products, arithmetic and copies ran while one was open for 28% -> 31% of each run, Pallas kernels for 0% -> 0%
where the time goes in v2:
time: 433 us; the launch traced here: 426 us
  waiting for transfers between devices  140 us (32%)
  starting transfers between devices  104 us (24%)
  other arithmetic  73 us (17%)
  matrix products  58.7 us (14%)
  local copies, waits for them, and re-layouts  46.8 us (11%)
    ppermute x68, waiting for transfers between devices, along(): return lax.ppermute(shard, axis, pairs)  139 us
    ppermute x68, starting transfers between devices, along(): return lax.ppermute(shard, axis, pairs)  96.4 us
    unnamed x180, local copies, waits for them, and re-layouts  24.8 us
    dot_general x6, matrix products, times(): return jnp.dot(left, right, preferred_element_type=f32)  23.3 us
    dot_general x7, matrix products, against_rows(): lax.dot_general(left, right, (((1,), (1,)), ((), ())), preferred_element_...  18.9 us
    dot_general x9, matrix products, over_tokens(): lax.dot_general(left, right, (((0,), (0,)), ((), ())), preferred_element_...  16.5 us
    convert_element_type x10, other arithmetic, add_pair(): (one.astype(f32) + other.astype(f32)).astype(bf16)  13.3 us
  transfers between devices with their start and end apart: 70, of which 29 were waited for; matrix products, arithmetic and copies ran while one was open for 31% of the time, Pallas kernels for 0%

profile of v2, /device:TPU:0, one launch (start us, length us, event | category | flops | bytes accessed | tf_op | source)
XLA Modules:
  0.0 425.5 jit_solution(3775852089821214121)
XLA Ops:
  2.1 2.9 collective-permute-start
  18.2 7.4 %collective-permute-done.3 = bf16[8,128]{1,0:T(8,128)(2,1)} collective-permute-done((bf16[8,128]{1,0:T(8,128)(2,1)}, bf16[8,128]{1,0:T(8,128)(2,1)}, u32[]{:S(2)}, u32[]{:S(2)}) %collective-permute-start.3) | collective-permute-done | bytes 2080 | tf_op jit(solution)/shard_map/ppermute | solution.py:12
  42.9 10.2 %collective-permute-done.6 = bf16[2,256,576]{1,2,0:T(8,128)(2,1)S(1)} collective-permute-done((bf16[2,256,576]{1,2,0:T(8,128)(2,1)S(1)}, bf16[2,256,576]{1,2,0:T(8,128)(2,1)S(1)}, u32[]{:S(2)}, u32[]{:S(2)}) %collective-permute-start.6) | collective-permute-done | bytes 589856 | tf_op jit(solution)/shard_map/ppermute | solution.py:12
  53.1 13.8 %collective-permute-start.11 = (bf16[3,128,3072]{2,1,0:T(8,128)(2,1)S(1)}, bf16[3,128,3072]{2,1,0:T(8,128)(2,1)S(1)}, u32[]{:S(2)}, u32[]{:S(2)}) collective-permute-start(bf16[3,128,3072]{2,1,0:T(8,128)(2,1)S(1)} %pad_maximum_fusion.2), channel_id=1, source_target_pairs={{0,1},{1,0},{2,3},{3,2},{4,5},{5,4},{6,7},{7,6},{8,9},{9,8},{10,11... | collective-permute-start | bytes 7077896 | tf_op jit(solution)/shard_map/ppermute | solution.py:12
  66.9 2.4 collective-permute-done.18
  73.5 10.7 %collective-permute-done.21 = bf16[256,1024]{1,0:T(8,128)(2,1)S(1)} collective-permute-done((bf16[256,1024]{1,0:T(8,128)(2,1)S(1)}, bf16[256,1024]{1,0:T(8,128)(2,1)S(1)}, u32[]{:S(2)}, u32[]{:S(2)}) %collective-permute-start.21) | collective-permute-done | bytes 524320 | tf_op jit(solution)/shard_map/ppermute | solution.py:12
  89.6 5.9 %collective-permute-start.14 = (bf16[2,2,1024]{2,1,0:T(2,128)(2,1)S(1)}, bf16[2,2,1024]{2,1,0:T(2,128)(2,1)S(1)}, u32[]{:S(2)}, u32[]{:S(2)}) collective-permute-start(bf16[2,2,1024]{2,1,0:T(2,128)(2,1)S(1)} %slice.534), channel_id=1, source_target_pairs={{0,1},{1,2},{2,3},{3,4},{4,5},{5,6},{6,7},{8,9},{9,10},{10,11},{11... | collective-permute-start | bytes 24584 | tf_op jit(solution)/shard_map/ppermute | solution.py:156
  101.9 2.8 collective-permute-start.26
  104.9 10.9 %collective-permute-done.26 = bf16[256,1024]{1,0:T(8,128)(2,1)S(1)} collective-permute-done((bf16[256,1024]{1,0:T(8,128)(2,1)S(1)}, bf16[256,1024]{1,0:T(8,128)(2,1)S(1)}, u32[]{:S(2)}, u32[]{:S(2)}) %collective-permute-start.26) | collective-permute-done | bytes 524320 | tf_op jit(solution)/shard_map/ppermute | solution.py:12
  118.1 7.5 %collective-permute-done.28 = bf16[256,1024]{1,0:T(8,128)(2,1)S(1)} collective-permute-done((bf16[256,1024]{1,0:T(8,128)(2,1)S(1)}, bf16[256,1024]{1,0:T(8,128)(2,1)S(1)}, u32[]{:S(2)}, u32[]{:S(2)}) %collective-permute-start.28) | collective-permute-done | bytes 524320 | tf_op jit(solution)/shard_map/ppermute | solution.py:12
  125.5 4.3 %fusion.133 = f32[2048,576]{0,1:T(8,128)} fusion(bf16[2048,1024]{1,0:T(8,128)(2,1)S(1)} %bitcast.309, bf16[576,1024]{1,0:T(8,128)(2,1)S(1)} %copy-done), kind=kOutput, calls=%fused_computation.484 | convolution fusion | flops 2415919104 | bytes 10092544 | tf_op jit(solution)/shard_map/dot_general | solution.py:180
  130.2 4.3 %fusion.10 = f32[2048,576]{0,1:T(8,128)} fusion(bf16[2048,1024]{1,0:T(8,128)(2,1)S(1)} %bitcast.311, bf16[8,72,8,128]{3,2,1,0:T(8,128)(2,1)S(1)} %get-tuple-element.245), kind=kOutput, calls=%fused_computation.79 | convolution fusion | flops 2415919104 | bytes 10092544 | tf_op jit(solution)/shard_map/dot_general | solution.py:172
  134.6 9.9 %multiply_convert_fusion = (bf16[2048,576]{0,1:T(8,128)(2,1)}, bf16[2048,576]{0,1:T(8,128)(2,1)S(1)}, bf16[2048,576]{0,1:T(8,128)(2,1)}) fusion(f32[2048,576]{0,1:T(8,128)} %fusion.10, f32[2048,576]{0,1:T(8,128)} %fusion.133, bf16[2048,1024]{1,0:T(8,128)(2,1)} %bitcast.312, bf16[8,72,8,128]{3,2,1,0:T(8,128)(2,1)S(1)} %get-tuple-element.244), kind=kOutput, calls=%fused_computation.9 | convolution fusion | flops 2434793472 | bytes 21889024 | tf_op jit(solution)/shard_map/dot_general | solution.py:172
  149.6 3.9 fusion.6
  153.4 4.2 add_convert_fusion
  157.6 4.5 %convolution_convert_fusion.4 = bf16[1024,576]{0,1:T(8,128)(2,1)S(1)} fusion(bf16[2048,576]{0,1:T(8,128)(2,1)} %copy-done.68, bf16[2048,1024]{1,0:T(8,128)(2,1)S(1)} %bitcast.313), kind=kOutput, calls=%fused_computation.62 | convolution fusion | flops 2416508928 | bytes 7733248 | tf_op jit(solution)/shard_map/dot_general | solution.py:176
  162.1 4.0 collective-permute-start.34
  166.2 3.6 convolution_convert_fusion.5
  171.6 2.6 convolution_convert_fusion.3
  174.2 5.1 %collective-permute-done.31 = bf16[256,1024]{1,0:T(8,128)(2,1)S(1)} collective-permute-done((bf16[256,1024]{1,0:T(8,128)(2,1)S(1)}, bf16[256,1024]{1,0:T(8,128)(2,1)S(1)}, u32[]{:S(2)}, u32[]{:S(2)}) %collective-permute-start.31) | collective-permute-done | bytes 524320 | tf_op jit(solution)/shard_map/ppermute | solution.py:12
  182.9 3.3 convolution_convert_fusion.2
  186.2 3.2 convolution_convert_fusion.1
  189.4 3.2 collective-permute-done.32
  196.9 4.3 %collective-permute-start.36 = (bf16[1024,576]{0,1:T(8,128)(2,1)S(1)}, bf16[1024,576]{0,1:T(8,128)(2,1)S(1)}, u32[]{:S(2)}, u32[]{:S(2)}) collective-permute-start(bf16[1024,576]{0,1:T(8,128)(2,1)S(1)} %convolution_convert_fusion.3), channel_id=1, source_target_pairs={{0,8},{24,16},{1,9},{25,17},{2,10},{26,18},{3,11},{27,19},{4,12},{... | collective-permute-start | bytes 3538952 | tf_op jit(solution)/shard_map/ppermute | solution.py:12
  206.3 18.9 %collective-permute-done.36 = bf16[1024,576]{0,1:T(8,128)(2,1)S(1)} collective-permute-done((bf16[1024,576]{0,1:T(8,128)(2,1)S(1)}, bf16[1024,576]{0,1:T(8,128)(2,1)S(1)}, u32[]{:S(2)}, u32[]{:S(2)}) %collective-permute-start.36) | collective-permute-done | bytes 1179680 | tf_op jit(solution)/shard_map/ppermute | solution.py:12
  241.4 4.6 %collective-permute-start.44 = (bf16[576,1024]{1,0:T(8,128)(2,1)}, bf16[576,1024]{1,0:T(8,128)(2,1)S(1)}, u32[]{:S(2)}, u32[]{:S(2)}) collective-permute-start(bf16[576,1024]{1,0:T(8,128)(2,1)} %convolution_convert_fusion.5), channel_id=1, source_target_pairs={{0,8},{24,16},{1,9},{25,17},{2,10},{26,18},{3,11},{27,19},{4,12},{... | collective-permute-start | bytes 3538952 | tf_op jit(solution)/shard_map/ppermute | solution.py:12
  258.6 5.9 %collective-permute-done.39 = bf16[128,2048]{1,0:T(8,128)(2,1)S(1)} collective-permute-done((bf16[128,2048]{1,0:T(8,128)(2,1)S(1)}, bf16[128,2048]{1,0:T(8,128)(2,1)S(1)}, u32[]{:S(2)}, u32[]{:S(2)}) %collective-permute-start.39) | collective-permute-done | bytes 524320 | tf_op jit(solution)/shard_map/ppermute | solution.py:12
  267.6 5.5 %collective-permute-done.50 = bf16[128,2176]{1,0:T(8,128)(2,1)S(1)} collective-permute-done((bf16[128,2176]{1,0:T(8,128)(2,1)S(1)}, bf16[128,2176]{1,0:T(8,128)(2,1)S(1)}, u32[]{:S(2)}, u32[]{:S(2)}) %collective-permute-start.50) | collective-permute-done | bytes 557088 | tf_op jit(solution)/shard_map/ppermute | solution.py:12
  274.7 2.7 fusion.25
  277.4 4.3 %collective-permute-done.40 = bf16[128,2048]{1,0:T(8,128)(2,1)S(1)} collective-permute-done((bf16[128,2048]{1,0:T(8,128)(2,1)S(1)}, bf16[128,2048]{1,0:T(8,128)(2,1)S(1)}, u32[]{:S(2)}, u32[]{:S(2)}) %collective-permute-start.40) | collective-permute-done | bytes 524320 | tf_op jit(solution)/shard_map/ppermute | solution.py:12
  287.9 5.6 %collective-permute-start.55 = (bf16[128,2048]{1,0:T(8,128)(2,1)}, bf16[128,2048]{1,0:T(8,128)(2,1)}, u32[]{:S(2)}, u32[]{:S(2)}) collective-permute-start(bf16[128,2048]{1,0:T(8,128)(2,1)} %fusion.58), channel_id=1, source_target_pairs={{0,8},{24,16},{1,9},{25,17},{2,10},{26,18},{3,11},{27,19},{4,12},{... | collective-permute-start | bytes 1572872 | tf_op jit(solution)/shard_map/ppermute | solution.py:12
  294.7 4.0 reshape_reshape.6
  298.6 3.7 fusion.128
  311.3 2.5 fusion.35
  314.9 3.6 collective-permute-done.59
  318.5 4.0 collective-permute-done.57
  323.8 11.1 %collective-permute-done.53 = bf16[1024,576]{0,1:T(8,128)(2,1)S(1)} collective-permute-done((bf16[1024,576]{0,1:T(8,128)(2,1)S(1)}, bf16[1024,576]{0,1:T(8,128)(2,1)S(1)}, u32[]{:S(2)}, u32[]{:S(2)}) %collective-permute-start.53) | collective-permute-done | bytes 1179680 | tf_op jit(solution)/shard_map/ppermute | solution.py:12
  336.0 4.0 reshape_reshape.7
  343.7 3.2 collective-permute-start.62
  356.0 3.0 copy.110
  370.3 3.0 collective-permute-done.66
  373.2 3.9 collective-permute-done.64
  377.7 5.1 %collective-permute-done.60 = bf16[576,1024]{1,0:T(8,128)(2,1)} collective-permute-done((bf16[576,1024]{1,0:T(8,128)(2,1)}, bf16[576,1024]{1,0:T(8,128)(2,1)}, u32[]{:S(2)}, u32[]{:S(2)}) %collective-permute-start.60) | collective-permute-done | bytes 1179680 | tf_op jit(solution)/shard_map/ppermute | solution.py:12
  391.4 3.0 copy.111
  394.5 3.0 select_convert_fusion
  407.1 5.7 %collective-permute-done.47 = bf16[256,1024]{1,0:T(8,128)(2,1)S(1)} collective-permute-done((bf16[256,1024]{1,0:T(8,128)(2,1)S(1)}, bf16[256,1024]{1,0:T(8,128)(2,1)S(1)}, u32[]{:S(2)}, u32[]{:S(2)}) %collective-permute-start.47) | collective-permute-done | bytes 524320 | tf_op jit(solution)/shard_map/ppermute | solution.py:12
  414.2 2.9 multiply_add_fusion
  417.2 5.0 %collective-permute-done.68 = bf16[128,2176]{1,0:T(8,128)(2,1)S(1)} collective-permute-done((bf16[128,2176]{1,0:T(8,128)(2,1)S(1)}, bf16[128,2176]{1,0:T(8,128)(2,1)S(1)}, u32[]{:S(2)}, u32[]{:S(2)}) %collective-permute-start.68) | collective-permute-done | bytes 557088 | tf_op jit(solution)/shard_map/ppermute | solution.py:12
  (454 shorter events, 169.3 us)
Async XLA Ops:
  2.1 12.1 %collective-permute-start = (bf16[8,128]{1,0:T(8,128)(2,1)}, bf16[8,128]{1,0:T(8,128)(2,1)S(1)}, u32[]{:S(2)}, u32[]{:S(2)}) collective-permute-start(bf16[8,128]{1,0:T(8,128)(2,1)} %fusion.121), channel_id=1, source_target_pairs={{0,2},{1,3},{2,0},{3,1},{4,6},{5,7},{6,4},{7,5},{8,10},{9,11},{10,... | collective-permute-start | bytes 6152 | tf_op jit(solution)/shard_map/ppermute | solution.py:12
  6.6 23.9 %collective-permute-start.10 = (bf16[128,3072]{1,0:T(8,128)(2,1)}, bf16[128,3072]{1,0:T(8,128)(2,1)}, u32[]{:S(2)}, u32[]{:S(2)}) collective-permute-start(bf16[128,3072]{1,0:T(8,128)(2,1)} %param.12), channel_id=1, source_target_pairs={{0,4},{1,5},{2,6},{3,7},{4,0},{5,1},{6,2},{7,3},{8,12},{9,13},{10,... | collective-permute-start | bytes 2359304 | tf_op jit(solution)/shard_map/ppermute | solution.py:12
  7.1 23.4 %collective-permute-start.9 = (bf16[128,3072]{1,0:T(8,128)(2,1)}, bf16[128,3072]{1,0:T(8,128)(2,1)}, u32[]{:S(2)}, u32[]{:S(2)}) collective-permute-start(bf16[128,3072]{1,0:T(8,128)(2,1)} %param.12), channel_id=1, source_target_pairs={{0,2},{1,3},{2,0},{3,1},{4,6},{5,7},{6,4},{7,5},{8,10},{9,11},{10,... | collective-permute-start | bytes 2359304 | tf_op jit(solution)/shard_map/ppermute | solution.py:12
  14.0 20.6 %collective-permute-start.5 = (bf16[4,256,576]{1,2,0:T(8,128)(2,1)}, bf16[4,256,576]{1,2,0:T(8,128)(2,1)}, u32[]{:S(2)}, u32[]{:S(2)}) collective-permute-start(bf16[4,256,576]{1,2,0:T(8,128)(2,1)} %select_bitcast_fusion), channel_id=1, source_target_pairs={{0,1},{1,0},{2,3},{3,2},{4,5},{5,4},{6,7},{7,6},{8,9},{9,8},{10,11... | collective-permute-start | bytes 3538952 | tf_op jit(solution)/shard_map/ppermute | solution.py:12
  32.8 36.6 %collective-permute-start.12 = (bf16[128,3072]{1,0:T(8,128)(2,1)S(1)}, bf16[128,3072]{1,0:T(8,128)(2,1)S(1)}, u32[]{:S(2)}, u32[]{:S(2)}) collective-permute-start(bf16[128,3072]{1,0:T(8,128)(2,1)S(1)} %broadcast_select_fusion.3), channel_id=1, source_target_pairs={{0,4},{1,3},{2,6},{3,1},{4,0},{5,7},{6,2},{7,5},{8,12},{9,11},{10,... | collective-permute-start | bytes 2359304 | tf_op jit(solution)/shard_map/ppermute | solution.py:12
  36.3 16.8 %collective-permute-start.6 = (bf16[2,256,576]{1,2,0:T(8,128)(2,1)S(1)}, bf16[2,256,576]{1,2,0:T(8,128)(2,1)S(1)}, u32[]{:S(2)}, u32[]{:S(2)}) collective-permute-start(bf16[2,256,576]{1,2,0:T(8,128)(2,1)S(1)} %get-tuple-element.247), channel_id=1, source_target_pairs={{0,2},{1,3},{2,0},{3,1},{4,6},{5,7},{6,4},{7,5},{8,10},{9,11},{10,... | collective-permute-start | bytes 1769480 | tf_op jit(solution)/shard_map/ppermute | solution.py:12
  39.5 30.4 %collective-permute-start.7 = (bf16[2,256,576]{1,2,0:T(8,128)(2,1)S(1)}, bf16[2,256,576]{1,2,0:T(8,128)(2,1)S(1)}, u32[]{:S(2)}, u32[]{:S(2)}) collective-permute-start(bf16[2,256,576]{1,2,0:T(8,128)(2,1)S(1)} %get-tuple-element.248), channel_id=1, source_target_pairs={{0,4},{1,5},{2,6},{3,7},{4,0},{5,1},{6,2},{7,3},{8,12},{9,13},{10,... | collective-permute-start | bytes 1769480 | tf_op jit(solution)/shard_map/ppermute | solution.py:12
  40.5 28.8 %collective-permute-start.18 = (bf16[128,1024]{1,0:T(8,128)(2,1)S(1)}, bf16[128,1024]{1,0:T(8,128)(2,1)S(1)}, u32[]{:S(2)}, u32[]{:S(2)}) collective-permute-start(bf16[128,1024]{1,0:T(8,128)(2,1)S(1)} %broadcast_select_fusion.8), channel_id=1, source_target_pairs={{0,4},{1,3},{2,6},{3,1},{4,0},{5,7},{6,2},{7,5},{8,12},{9,11},{10,... | collective-permute-start | bytes 786440 | tf_op jit(solution)/shard_map/ppermute | solution.py:12
  42.2 27.9 %collective-permute-start.8 = (bf16[2,256,576]{1,2,0:T(8,128)(2,1)S(1)}, bf16[2,256,576]{1,2,0:T(8,128)(2,1)S(1)}, u32[]{:S(2)}, u32[]{:S(2)}) collective-permute-start(bf16[2,256,576]{1,2,0:T(8,128)(2,1)S(1)} %get-tuple-element.246), channel_id=1, source_target_pairs={{0,6},{1,7},{2,4},{3,5},{4,2},{5,3},{6,0},{7,1},{8,14},{9,15},{10,... | collective-permute-start | bytes 1769480 | tf_op jit(solution)/shard_map/ppermute | solution.py:12
  53.1 31.8 %collective-permute-start.11 = (bf16[3,128,3072]{2,1,0:T(8,128)(2,1)S(1)}, bf16[3,128,3072]{2,1,0:T(8,128)(2,1)S(1)}, u32[]{:S(2)}, u32[]{:S(2)}) collective-permute-start(bf16[3,128,3072]{2,1,0:T(8,128)(2,1)S(1)} %pad_maximum_fusion.2), channel_id=1, source_target_pairs={{0,1},{1,0},{2,3},{3,2},{4,5},{5,4},{6,7},{7,6},{8,9},{9,8},{10,11... | collective-permute-start | bytes 7077896 | tf_op jit(solution)/shard_map/ppermute | solution.py:12
  69.9 15.2 %collective-permute-start.13 = (bf16[128,3072]{1,0:T(8,128)(2,1)S(1)}, bf16[128,3072]{1,0:T(8,128)(2,1)S(1)}, u32[]{:S(2)}, u32[]{:S(2)}) collective-permute-start(bf16[128,3072]{1,0:T(8,128)(2,1)S(1)} %collective-permute-done.12), channel_id=1, source_target_pairs={{0,1},{1,0},{2,3},{3,2},{4,5},{5,4},{6,7},{7,6},{8,9},{9,8},{10,11... | collective-permute-start | bytes 2359304 | tf_op jit(solution)/shard_map/ppermute | solution.py:12
  71.3 12.9 %collective-permute-start.21 = (bf16[256,1024]{1,0:T(8,128)(2,1)S(1)}, bf16[256,1024]{1,0:T(8,128)(2,1)S(1)}, u32[]{:S(2)}, u32[]{:S(2)}) collective-permute-start(bf16[256,1024]{1,0:T(8,128)(2,1)S(1)} %bitcast.285), channel_id=1, source_target_pairs={{0,4},{1,5},{2,6},{3,7},{4,0},{5,1},{6,2},{7,3},{8,12},{9,13},{10,... | collective-permute-start | bytes 1572872 | tf_op jit(solution)/shard_map/ppermute | solution.py:12
  72.8 11.4 %collective-permute-start.20 = (bf16[256,1024]{1,0:T(8,128)(2,1)S(1)}, bf16[256,1024]{1,0:T(8,128)(2,1)S(1)}, u32[]{:S(2)}, u32[]{:S(2)}) collective-permute-start(bf16[256,1024]{1,0:T(8,128)(2,1)S(1)} %bitcast.286), channel_id=1, source_target_pairs={{0,2},{1,3},{2,0},{3,1},{4,6},{5,7},{6,4},{7,5},{8,10},{9,11},{10,... | collective-permute-start | bytes 1572872 | tf_op jit(solution)/shard_map/ppermute | solution.py:12
  84.2 11.6 %collective-permute-start.23 = (bf16[256,1024]{1,0:T(8,128)(2,1)S(1)}, bf16[256,1024]{1,0:T(8,128)(2,1)S(1)}, u32[]{:S(2)}, u32[]{:S(2)}) collective-permute-start(bf16[256,1024]{1,0:T(8,128)(2,1)S(1)} %broadcast_select_fusion.7), channel_id=1, source_target_pairs={{0,4},{1,3},{2,6},{3,1},{4,0},{5,7},{6,2},{7,5},{8,12},{9,11},{10,... | collective-permute-start | bytes 1572872 | tf_op jit(solution)/shard_map/ppermute | solution.py:12
  101.9 13.9 %collective-permute-start.26 = (bf16[256,1024]{1,0:T(8,128)(2,1)S(1)}, bf16[256,1024]{1,0:T(8,128)(2,1)S(1)}, u32[]{:S(2)}, u32[]{:S(2)}) collective-permute-start(bf16[256,1024]{1,0:T(8,128)(2,1)S(1)} %multiply_convert_fusion.4), channel_id=1, source_target_pairs={{0,4},{1,5},{2,6},{3,7},{4,0},{5,1},{6,2},{7,3},{8,12},{9,13},{10,... | collective-permute-start | bytes 1572872 | tf_op jit(solution)/shard_map/ppermute | solution.py:12
  104.7 11.3 %collective-permute-start.25 = (bf16[256,1024]{1,0:T(8,128)(2,1)S(1)}, bf16[256,1024]{1,0:T(8,128)(2,1)S(1)}, u32[]{:S(2)}, u32[]{:S(2)}) collective-permute-start(bf16[256,1024]{1,0:T(8,128)(2,1)S(1)} %multiply_convert_fusion.4), channel_id=1, source_target_pairs={{0,2},{1,3},{2,0},{3,1},{4,6},{5,7},{6,4},{7,5},{8,10},{9,11},{10,... | collective-permute-start | bytes 1572872 | tf_op jit(solution)/shard_map/ppermute | solution.py:12
  116.1 13.7 %collective-permute-start.27 = (bf16[3,256,1024]{2,1,0:T(8,128)(2,1)S(1)}, bf16[3,256,1024]{2,1,0:T(8,128)(2,1)S(1)}, u32[]{:S(2)}, u32[]{:S(2)}) collective-permute-start(bf16[3,256,1024]{2,1,0:T(8,128)(2,1)S(1)} %pad_maximum_fusion.8), channel_id=1, source_target_pairs={{0,1},{1,0},{2,3},{3,2},{4,5},{5,4},{6,7},{7,6},{8,9},{9,8},{10,11... | collective-permute-start | bytes 4718600 | tf_op jit(solution)/shard_map/ppermute | solution.py:12
  149.0 20.8 %collective-permute-start.30 = (bf16[1024,1024]{1,0:T(8,128)(2,1)S(1)}, bf16[1024,1024]{1,0:T(8,128)(2,1)S(1)}, u32[]{:S(2)}, u32[]{:S(2)}) collective-permute-start(bf16[1024,1024]{1,0:T(8,128)(2,1)S(1)} %add_convert_fusion.1), channel_id=1, source_target_pairs={{0,1},{1,0},{2,3},{3,2},{4,5},{5,4},{6,7},{7,6},{8,9},{9,8},{10,11... | collective-permute-start | bytes 6291464 | tf_op jit(solution)/shard_map/ppermute | solution.py:12
  162.1 32.0 %collective-permute-start.34 = (bf16[1024,576]{0,1:T(8,128)(2,1)S(1)}, bf16[1024,576]{0,1:T(8,128)(2,1)S(1)}, u32[]{:S(2)}, u32[]{:S(2)}) collective-permute-start(bf16[1024,576]{0,1:T(8,128)(2,1)S(1)} %convolution_convert_fusion.4), channel_id=1, source_target_pairs={{0,8},{24,16},{1,9},{25,17},{2,10},{26,18},{3,11},{27,19},{4,12},{... | collective-permute-start | bytes 3538952 | tf_op jit(solution)/shard_map/ppermute | solution.py:12
  179.8 12.8 %collective-permute-start.32 = (bf16[256,1024]{1,0:T(8,128)(2,1)S(1)}, bf16[256,1024]{1,0:T(8,128)(2,1)S(1)}, u32[]{:S(2)}, u32[]{:S(2)}) collective-permute-start(bf16[256,1024]{1,0:T(8,128)(2,1)S(1)} %get-tuple-element.238), channel_id=1, source_target_pairs={{0,2},{1,3},{2,0},{3,1},{4,6},{5,7},{6,4},{7,5},{8,10},{9,11},{10,... | collective-permute-start | bytes 1572872 | tf_op jit(solution)/shard_map/ppermute | solution.py:12
  181.4 12.4 %collective-permute-start.33 = (bf16[256,1024]{1,0:T(8,128)(2,1)S(1)}, bf16[256,1024]{1,0:T(8,128)(2,1)S(1)}, u32[]{:S(2)}, u32[]{:S(2)}) collective-permute-start(bf16[256,1024]{1,0:T(8,128)(2,1)S(1)} %get-tuple-element.239), channel_id=1, source_target_pairs={{0,4},{1,5},{2,6},{3,7},{4,0},{5,1},{6,2},{7,3},{8,12},{9,13},{10,... | collective-permute-start | bytes 1572872 | tf_op jit(solution)/shard_map/ppermute | solution.py:12
  196.9 28.3 %collective-permute-start.36 = (bf16[1024,576]{0,1:T(8,128)(2,1)S(1)}, bf16[1024,576]{0,1:T(8,128)(2,1)S(1)}, u32[]{:S(2)}, u32[]{:S(2)}) collective-permute-start(bf16[1024,576]{0,1:T(8,128)(2,1)S(1)} %convolution_convert_fusion.3), channel_id=1, source_target_pairs={{0,8},{24,16},{1,9},{25,17},{2,10},{26,18},{3,11},{27,19},{4,12},{... | collective-permute-start | bytes 3538952 | tf_op jit(solution)/shard_map/ppermute | solution.py:12
  239.4 14.2 %collective-permute-start.38 = (bf16[512,2048]{1,0:T(8,128)(2,1)}, bf16[512,2048]{1,0:T(8,128)(2,1)}, u32[]{:S(2)}, u32[]{:S(2)}) collective-permute-start(bf16[512,2048]{1,0:T(8,128)(2,1)} %pad_maximum_fusion.4), channel_id=1, source_target_pairs={{0,1},{1,0},{2,3},{3,2},{4,5},{5,4},{6,7},{7,6},{8,9},{9,8},{10,11... | collective-permute-start | bytes 6291464 | tf_op jit(solution)/shard_map/ppermute | solution.py:12
  240.9 15.8 %collective-permute-start.49 = (bf16[512,2176]{1,0:T(8,128)(2,1)}, bf16[512,2176]{1,0:T(8,128)(2,1)}, u32[]{:S(2)}, u32[]{:S(2)}) collective-permute-start(bf16[512,2176]{1,0:T(8,128)(2,1)} %pad_maximum_fusion.3), channel_id=1, source_target_pairs={{0,1},{1,0},{2,3},{3,2},{4,5},{5,4},{6,7},{7,6},{8,9},{9,8},{10,11... | collective-permute-start | bytes 6684680 | tf_op jit(solution)/shard_map/ppermute | solution.py:12
  241.4 45.4 %collective-permute-start.44 = (bf16[576,1024]{1,0:T(8,128)(2,1)}, bf16[576,1024]{1,0:T(8,128)(2,1)S(1)}, u32[]{:S(2)}, u32[]{:S(2)}) collective-permute-start(bf16[576,1024]{1,0:T(8,128)(2,1)} %convolution_convert_fusion.5), channel_id=1, source_target_pairs={{0,8},{24,16},{1,9},{25,17},{2,10},{26,18},{3,11},{27,19},{4,12},{... | collective-permute-start | bytes 3538952 | tf_op jit(solution)/shard_map/ppermute | solution.py:12
  248.2 38.7 %collective-permute-start.43 = (bf16[1024,576]{0,1:T(8,128)(2,1)S(1)}, bf16[1024,576]{0,1:T(8,128)(2,1)S(1)}, u32[]{:S(2)}, u32[]{:S(2)}) collective-permute-start(bf16[1024,576]{0,1:T(8,128)(2,1)S(1)} %add_convert_fusion.5), channel_id=1, source_target_pairs={{8,16},{16,8},{9,17},{17,9},{10,18},{18,10},{11,19},{19,11},{12,20... | collective-permute-start | bytes 3538952 | tf_op jit(solution)/shard_map/ppermute | solution.py:12
  249.6 37.3 %collective-permute-start.42 = (bf16[1024,576]{0,1:T(8,128)(2,1)S(1)}, bf16[1024,576]{0,1:T(8,128)(2,1)S(1)}, u32[]{:S(2)}, u32[]{:S(2)}) collective-permute-start(bf16[1024,576]{0,1:T(8,128)(2,1)S(1)} %add_convert_fusion.6), channel_id=1, source_target_pairs={{8,0},{16,24},{9,1},{17,25},{10,2},{18,26},{11,3},{19,27},{12,4},{... | collective-permute-start | bytes 3538952 | tf_op jit(solution)/shard_map/ppermute | solution.py:12
  257.9 15.2 %collective-permute-start.50 = (bf16[128,2176]{1,0:T(8,128)(2,1)S(1)}, bf16[128,2176]{1,0:T(8,128)(2,1)S(1)}, u32[]{:S(2)}, u32[]{:S(2)}) collective-permute-start(bf16[128,2176]{1,0:T(8,128)(2,1)S(1)} %fusion.30), channel_id=1, source_target_pairs={{0,2},{1,5},{2,0},{3,7},{4,6},{5,1},{6,4},{7,3},{8,10},{9,13},{10,... | collective-permute-start | bytes 1671176 | tf_op jit(solution)/shard_map/ppermute | solution.py:12
  266.1 15.6 %collective-permute-start.40 = (bf16[128,2048]{1,0:T(8,128)(2,1)S(1)}, bf16[128,2048]{1,0:T(8,128)(2,1)S(1)}, u32[]{:S(2)}, u32[]{:S(2)}) collective-permute-start(bf16[128,2048]{1,0:T(8,128)(2,1)S(1)} %get-tuple-element.234), channel_id=1, source_target_pairs={{0,2},{1,3},{2,0},{3,1},{4,6},{5,7},{6,4},{7,5},{8,10},{9,11},{10,... | collective-permute-start | bytes 1572872 | tf_op jit(solution)/shard_map/ppermute | solution.py:12
  281.7 25.9 %collective-permute-start.51 = (bf16[128,2176]{1,0:T(8,128)(2,1)}, bf16[128,2176]{1,0:T(8,128)(2,1)}, u32[]{:S(2)}, u32[]{:S(2)}) collective-permute-start(bf16[128,2176]{1,0:T(8,128)(2,1)} %get-tuple-element.232), channel_id=1, source_target_pairs={{0,2},{1,3},{2,0},{3,1},{4,6},{5,7},{6,4},{7,5},{8,10},{9,11},{10,... | collective-permute-start | bytes 1671176 | tf_op jit(solution)/shard_map/ppermute | solution.py:12
  283.2 26.5 %collective-permute-start.52 = (bf16[128,2176]{1,0:T(8,128)(2,1)}, bf16[128,2176]{1,0:T(8,128)(2,1)}, u32[]{:S(2)}, u32[]{:S(2)}) collective-permute-start(bf16[128,2176]{1,0:T(8,128)(2,1)} %get-tuple-element.233), channel_id=1, source_target_pairs={{0,4},{1,5},{2,6},{3,7},{4,0},{5,1},{6,2},{7,3},{8,12},{9,13},{10,... | collective-permute-start | bytes 1671176 | tf_op jit(solution)/shard_map/ppermute | solution.py:12
  287.9 22.0 %collective-permute-start.55 = (bf16[128,2048]{1,0:T(8,128)(2,1)}, bf16[128,2048]{1,0:T(8,128)(2,1)}, u32[]{:S(2)}, u32[]{:S(2)}) collective-permute-start(bf16[128,2048]{1,0:T(8,128)(2,1)} %fusion.58), channel_id=1, source_target_pairs={{0,8},{24,16},{1,9},{25,17},{2,10},{26,18},{3,11},{27,19},{4,12},{... | collective-permute-start | bytes 1572872 | tf_op jit(solution)/shard_map/ppermute | solution.py:12
  304.5 18.5 %collective-permute-start.54 = (bf16[576,1024]{1,0:T(8,128)(2,1)S(1)}, bf16[576,1024]{1,0:T(8,128)(2,1)S(1)}, u32[]{:S(2)}, u32[]{:S(2)}) collective-permute-start(bf16[576,1024]{1,0:T(8,128)(2,1)S(1)} %add_convert_fusion.3), channel_id=1, source_target_pairs={{8,16},{16,8},{9,17},{17,9},{10,18},{18,10},{11,19},{19,11},{12,20... | collective-permute-start | bytes 3538952 | tf_op jit(solution)/shard_map/ppermute | solution.py:12
  305.8 29.0 %collective-permute-start.53 = (bf16[1024,576]{0,1:T(8,128)(2,1)S(1)}, bf16[1024,576]{0,1:T(8,128)(2,1)S(1)}, u32[]{:S(2)}, u32[]{:S(2)}) collective-permute-start(bf16[1024,576]{0,1:T(8,128)(2,1)S(1)} %add_convert_fusion.4), channel_id=1, source_target_pairs={{8,0},{16,24},{9,1},{17,25},{10,2},{18,26},{11,3},{19,27},{12,4},{... | collective-permute-start | bytes 3538952 | tf_op jit(solution)/shard_map/ppermute | solution.py:12
  309.6 12.9 %collective-permute-start.57 = (bf16[2,128,576]{1,2,0:T(8,128)(2,1)S(1)}, bf16[2,128,576]{1,2,0:T(8,128)(2,1)S(1)}, u32[]{:S(2)}, u32[]{:S(2)}) collective-permute-start(bf16[2,128,576]{1,2,0:T(8,128)(2,1)S(1)} %get-tuple-element.255), channel_id=1, source_target_pairs={{0,2},{1,3},{2,0},{3,1},{4,6},{5,7},{6,4},{7,5},{8,10},{9,11},{10,... | collective-permute-start | bytes 884744 | tf_op jit(solution)/shard_map/ppermute | solution.py:12
  309.8 13.2 %collective-permute-start.58 = (bf16[2,128,576]{1,2,0:T(8,128)(2,1)S(1)}, bf16[2,128,576]{1,2,0:T(8,128)(2,1)S(1)}, u32[]{:S(2)}, u32[]{:S(2)}) collective-permute-start(bf16[2,128,576]{1,2,0:T(8,128)(2,1)S(1)} %get-tuple-element.256), channel_id=1, source_target_pairs={{0,4},{1,5},{2,6},{3,7},{4,0},{5,1},{6,2},{7,3},{8,12},{9,13},{10,... | collective-permute-start | bytes 884744 | tf_op jit(solution)/shard_map/ppermute | solution.py:12
  318.5 46.0 %collective-permute-start.45 = (bf16[1024,1024]{1,0:T(8,128)(2,1)}, bf16[1024,1024]{1,0:T(8,128)(2,1)}, u32[]{:S(2)}, u32[]{:S(2)}) collective-permute-start(bf16[1024,1024]{1,0:T(8,128)(2,1)} %convolution_convert_fusion.1), channel_id=1, source_target_pairs={{0,1},{1,0},{2,3},{3,2},{4,5},{5,4},{6,7},{7,6},{8,9},{9,8},{10,11... | collective-permute-start | bytes 6291464 | tf_op jit(solution)/shard_map/ppermute | solution.py:12
  342.2 22.1 %collective-permute-start.61 = (bf16[128,2048]{1,0:T(8,128)(2,1)}, bf16[128,2048]{1,0:T(8,128)(2,1)}, u32[]{:S(2)}, u32[]{:S(2)}) collective-permute-start(bf16[128,2048]{1,0:T(8,128)(2,1)} %add_convert_fusion.11), channel_id=1, source_target_pairs={{8,16},{16,8},{9,17},{17,9},{10,18},{18,10},{11,19},{19,11},{12,20... | collective-permute-start | bytes 1572872 | tf_op jit(solution)/shard_map/ppermute | solution.py:12
  343.7 24.6 %collective-permute-start.62 = (bf16[128,2176]{1,0:T(8,128)(2,1)}, bf16[128,2176]{1,0:T(8,128)(2,1)}, u32[]{:S(2)}, u32[]{:S(2)}) collective-permute-start(bf16[128,2176]{1,0:T(8,128)(2,1)} %fusion.35), channel_id=1, source_target_pairs={{0,8},{24,16},{1,9},{25,17},{2,10},{26,18},{3,11},{27,19},{4,12},{... | collective-permute-start | bytes 1671176 | tf_op jit(solution)/shard_map/ppermute | solution.py:12
  352.7 30.1 %collective-permute-start.60 = (bf16[576,1024]{1,0:T(8,128)(2,1)}, bf16[576,1024]{1,0:T(8,128)(2,1)}, u32[]{:S(2)}, u32[]{:S(2)}) collective-permute-start(bf16[576,1024]{1,0:T(8,128)(2,1)} %add_convert_fusion.2), channel_id=1, source_target_pairs={{8,0},{16,24},{9,1},{17,25},{10,2},{18,26},{11,3},{19,27},{12,4},{... | collective-permute-start | bytes 3538952 | tf_op jit(solution)/shard_map/ppermute | solution.py:12
  364.3 12.8 %collective-permute-start.64 = (bf16[2,128,576]{1,2,0:T(8,128)(2,1)S(1)}, bf16[2,128,576]{1,2,0:T(8,128)(2,1)S(1)}, u32[]{:S(2)}, u32[]{:S(2)}) collective-permute-start(bf16[2,128,576]{1,2,0:T(8,128)(2,1)S(1)} %get-tuple-element.250), channel_id=1, source_target_pairs={{0,2},{1,3},{2,0},{3,1},{4,6},{5,7},{6,4},{7,5},{8,10},{9,11},{10,... | collective-permute-start | bytes 884744 | tf_op jit(solution)/shard_map/ppermute | solution.py:12
  364.6 13.1 %collective-permute-start.65 = (bf16[2,128,576]{1,2,0:T(8,128)(2,1)S(1)}, bf16[2,128,576]{1,2,0:T(8,128)(2,1)S(1)}, u32[]{:S(2)}, u32[]{:S(2)}) collective-permute-start(bf16[2,128,576]{1,2,0:T(8,128)(2,1)S(1)} %get-tuple-element.251), channel_id=1, source_target_pairs={{0,4},{1,5},{2,6},{3,7},{4,0},{5,1},{6,2},{7,3},{8,12},{9,13},{10,... | collective-permute-start | bytes 884744 | tf_op jit(solution)/shard_map/ppermute | solution.py:12
  368.3 29.1 %collective-permute-start.46 = (bf16[256,1024]{1,0:T(8,128)(2,1)}, bf16[256,1024]{1,0:T(8,128)(2,1)}, u32[]{:S(2)}, u32[]{:S(2)}) collective-permute-start(bf16[256,1024]{1,0:T(8,128)(2,1)} %add_convert_fusion.13), channel_id=1, source_target_pairs={{0,2},{1,5},{2,0},{3,7},{4,6},{5,1},{6,4},{7,3},{8,10},{9,13},{10,... | collective-permute-start | bytes 1572872 | tf_op jit(solution)/shard_map/ppermute | solution.py:12
  386.9 15.2 %collective-permute-start.69 = (bf16[128,2048]{1,0:T(8,128)(2,1)}, bf16[128,2048]{1,0:T(8,128)(2,1)}, u32[]{:S(2)}, u32[]{:S(2)}) collective-permute-start(bf16[128,2048]{1,0:T(8,128)(2,1)} %add_convert_fusion.10), channel_id=1, source_target_pairs={{8,0},{16,24},{9,1},{17,25},{10,2},{18,26},{11,3},{19,27},{12,4},{... | collective-permute-start | bytes 1572872 | tf_op jit(solution)/shard_map/ppermute | solution.py:12
  388.2 15.0 %collective-permute-start.67 = (bf16[128,2176]{1,0:T(8,128)(2,1)}, bf16[128,2176]{1,0:T(8,128)(2,1)}, u32[]{:S(2)}, u32[]{:S(2)}) collective-permute-start(bf16[128,2176]{1,0:T(8,128)(2,1)} %add_convert_fusion.9), channel_id=1, source_target_pairs={{8,16},{16,8},{9,17},{17,9},{10,18},{18,10},{11,19},{19,11},{12,20... | collective-permute-start | bytes 1671176 | tf_op jit(solution)/shard_map/ppermute | solution.py:12
  399.4 13.4 %collective-permute-start.47 = (bf16[256,1024]{1,0:T(8,128)(2,1)S(1)}, bf16[256,1024]{1,0:T(8,128)(2,1)S(1)}, u32[]{:S(2)}, u32[]{:S(2)}) collective-permute-start(bf16[256,1024]{1,0:T(8,128)(2,1)S(1)} %get-tuple-element.236), channel_id=1, source_target_pairs={{0,2},{1,3},{2,0},{3,1},{4,6},{5,7},{6,4},{7,5},{8,10},{9,11},{10,... | collective-permute-start | bytes 1572872 | tf_op jit(solution)/shard_map/ppermute | solution.py:12
  401.5 12.7 %collective-permute-start.48 = (bf16[256,1024]{1,0:T(8,128)(2,1)S(1)}, bf16[256,1024]{1,0:T(8,128)(2,1)S(1)}, u32[]{:S(2)}, u32[]{:S(2)}) collective-permute-start(bf16[256,1024]{1,0:T(8,128)(2,1)S(1)} %get-tuple-element.237), channel_id=1, source_target_pairs={{0,4},{1,5},{2,6},{3,7},{4,0},{5,1},{6,2},{7,3},{8,12},{9,13},{10,... | collective-permute-start | bytes 1572872 | tf_op jit(solution)/shard_map/ppermute | solution.py:12
  404.7 17.5 %collective-permute-start.68 = (bf16[128,2176]{1,0:T(8,128)(2,1)S(1)}, bf16[128,2176]{1,0:T(8,128)(2,1)S(1)}, u32[]{:S(2)}, u32[]{:S(2)}) collective-permute-start(bf16[128,2176]{1,0:T(8,128)(2,1)S(1)} %add_convert_fusion.8), channel_id=1, source_target_pairs={{8,0},{16,24},{9,1},{17,25},{10,2},{18,26},{11,3},{19,27},{12,4},{... | collective-permute-start | bytes 1671176 | tf_op jit(solution)/shard_map/ppermute | solution.py:12
  (93 other events, 826.1 us)

commit v3 on v2

v3 whole, which is shorter than its diff:
```python
import jax
import jax.numpy as jnp
from jax import lax
from jax.experimental import pallas as pl
from jax.experimental.layout import Layout, with_layout_constraint
from jax.experimental.pallas import tpu as pltpu
from jax.sharding import PartitionSpec as P

epsilon = 1e-05
bf16 = jnp.bfloat16
f32 = jnp.float32


def along(shard, axis, pairs):
    return lax.ppermute(shard, axis, pairs)


def flip(shard, bits):
    peers = lax.axis_size("fsdp")
    return along(shard, "fsdp", [(i, i ^ bits) for i in range(peers)])


def flip_by_core(shard, even_bits, odd_bits):
    peers = lax.axis_size("fsdp")
    return along(
        shard, "fsdp", [(i, i ^ (odd_bits if i & 1 else even_bits)) for i in range(peers)]
    )


def is_cube():
    return lax.axis_size("fsdp") == 8


def on_odd_core():
    return (lax.axis_index("fsdp") & 1) == 1


def gather_sides(shard):
    if not is_cube():
        return (lax.all_gather(shard, "fsdp", axis=0),) * 2
    return flip(shard, 2), flip(shard, 4)


def gather_rest(shard, from_x, from_y):
    if not is_cube():
        return [from_x]
    across = flip_by_core(jnp.where(on_odd_core(), from_y, from_x), 4, 2)
    mine = jnp.stack([shard, from_x, from_y])
    return [flip(mine, 1), flip(across, 1)[None], mine, across[None]]


def gather(shard):
    return jnp.concatenate(gather_rest(shard, *gather_sides(shard)), axis=0)


def places():
    return [1, 3, 5, 7, 0, 2, 4, 6] if is_cube() else list(range(lax.axis_size("fsdp")))


def scatter_near(theirs, mine):
    if is_cube():
        return flip(theirs, 1)
    peers = lax.axis_size("fsdp")
    whole = jnp.concatenate([theirs, mine], axis=0)
    whole = whole.reshape(peers, whole.shape[0] // peers, -1)
    return lax.psum_scatter(whole, "fsdp", scatter_dimension=0)


def block_sum(mine, near, k):
    size = mine.shape[0] // 4
    rows = slice(k * size, (k + 1) * size)
    return mine[rows].astype(f32) + near[rows].astype(f32)


def scatter_across(mine, near):
    return flip_by_core(block_sum(mine, near, 3).astype(bf16), 2, 4) if is_cube() else near


def scatter_last(mine, near, across):
    if not is_cube():
        return near, near
    odd, zero = on_odd_core(), jnp.zeros((), f32)
    across = across.astype(f32)
    to_x = block_sum(mine, near, 1) + jnp.where(odd, across, zero)
    to_y = block_sum(mine, near, 2) + jnp.where(odd, zero, across)
    return flip(to_x.astype(bf16), 2), flip(to_y.astype(bf16), 4)


def scattered(mine, near, last):
    if not is_cube():
        return near.astype(f32)
    return block_sum(mine, near, 0) + last[0].astype(f32) + last[1].astype(f32)


def exchange_early(blocks):
    if not is_cube():
        return [lax.all_to_all(blocks, "fsdp", 0, 0)]
    chip, odd = lax.axis_index("fsdp") >> 1, on_odd_core()
    pairs = blocks.reshape((4, 2) + blocks.shape[1:])
    to_even, to_odd = pairs[:, 0], pairs[:, 1]
    kept = jnp.where(odd, to_odd, to_even)
    came = flip(jnp.where(odd, to_even, to_odd), 1)
    both = jnp.stack([jnp.where(odd, came, kept), jnp.where(odd, kept, came)], axis=1)
    return [both] + [
        flip(lax.dynamic_index_in_dim(both, chip ^ k, 0, keepdims=False), 2 * k)
        for k in (1, 2, 3)
    ]


def exchanged_early(parts):
    if not is_cube():
        return parts[0]
    chip, result = lax.axis_index("fsdp") >> 1, parts[0]
    for k in (1, 2, 3):
        result = lax.dynamic_update_index_in_dim(result, parts[k], chip ^ k, 0)
    return result.reshape((8,) + result.shape[2:])


def exchange_chips(blocks):
    if not is_cube():
        return [lax.all_to_all(blocks, "fsdp", 0, 0)]
    chip = lax.axis_index("fsdp") >> 1
    pairs = blocks.reshape((4, 2) + blocks.shape[1:])
    return [pairs] + [
        flip(lax.dynamic_index_in_dim(pairs, chip ^ k, 0, keepdims=False), 2 * k)
        for k in (1, 2, 3)
    ]


def exchange_cores(parts):
    if not is_cube():
        return parts[0]
    chip, odd = lax.axis_index("fsdp") >> 1, on_odd_core()
    came = parts[0]
    for k in (1, 2, 3):
        came = lax.dynamic_update_index_in_dim(came, parts[k], chip ^ k, 0)
    to_even, to_odd = came[:, 0], came[:, 1]
    kept = jnp.where(odd, to_odd, to_even)
    other = flip(jnp.where(odd, to_even, to_odd), 1)
    both = jnp.stack([jnp.where(odd, other, kept), jnp.where(odd, kept, other)], axis=1)
    return both.reshape((8,) + both.shape[2:])


def relabel(columns, back=False):
    peers = lax.axis_size("fsdp")
    if not is_cube():
        return columns
    size = columns.shape[-1] // peers
    me = lax.axis_index("fsdp")
    blocks = [columns[..., k * size : (k + 1) * size] for k in range(peers)]
    if back:
        blocks = [blocks[places().index(j)] for j in range(peers)]
    for bit in (1, 2, 4):
        swap = (me & bit) != 0
        blocks = [jnp.where(swap, blocks[k ^ bit], blocks[k]) for k in range(peers)]
    if not back:
        blocks = [blocks[j] for j in places()]
    return jnp.concatenate(blocks, axis=-1)


def in_line():
    return lax.axis_size("dp") == 4


def inward(term):
    if not in_line():
        return lax.psum(term, "dp")
    return along(term, "dp", [(0, 1), (3, 2)])


def between(pair):
    return along(pair, "dp", [(1, 2), (2, 1)]) if in_line() else pair


def outward(total):
    return along(total, "dp", [(1, 0), (2, 3)]) if in_line() else total


def inward_outward(term, total):
    if not in_line():
        return lax.psum(term, "dp"), total
    came = along(jnp.where(in_middle(), total, term), "dp", [(0, 1), (3, 2), (1, 0), (2, 3)])
    return jnp.where(in_middle(), came, jnp.zeros((), bf16)), came


def in_middle():
    return (lax.axis_index("dp") == 1) | (lax.axis_index("dp") == 2)


def add_pair(one, other):
    return (one.astype(f32) + other.astype(f32)).astype(bf16) if in_line() else other


def settle(total, came):
    if not in_line():
        return total
    return jnp.where(in_middle(), total, came)


def together(*values):
    return lax.optimization_barrier(values)


def from_behind(shard, axis, by):
    peers = lax.axis_size(axis)
    pairs = [(i, i + by) for i in range(peers) if 0 <= i + by < peers]
    return lax.ppermute(shard, axis, pairs)


def inverse_rms(values):
    return lax.rsqrt(jnp.mean(values * values, axis=-1, keepdims=True) + epsilon)


def norm_back(values, scale, gain, incoming):
    normed = values * scale
    gain_grad = jnp.sum(incoming * normed, axis=0)
    weighted = incoming * gain
    projection = jnp.mean(weighted * normed, axis=-1, keepdims=True)
    return (scale * (weighted - normed * projection), gain_grad)


def times(left, right):
    return jnp.dot(left, right, preferred_element_type=f32)


def over_tokens(left, right):
    return lax.dot_general(left, right, (((0,), (0,)), ((), ())), preferred_element_type=f32)


def against_rows(left, right):
    return lax.dot_general(left, right, (((1,), (1,)), ((), ())), preferred_element_type=f32)


def gated(gate_pre, up_pre, grad_activ):
    sigmoid_gate = jax.nn.sigmoid(gate_pre)
    silu_gate = gate_pre * sigmoid_gate
    activ = (silu_gate * up_pre).astype(bf16)
    grad_gate = (grad_activ * up_pre * (sigmoid_gate + silu_gate * (1.0 - sigmoid_gate))).astype(
        bf16
    )
    return activ, grad_gate, (grad_activ * silu_gate).astype(bf16)


def feed_forward_kernel(
    tokens_ref, grad_ref, gate_ref, up_ref, down_ref,
    activ_ref, grad_gate_ref, grad_up_ref, *out_refs,
):
    step, steps = pl.program_id(0), pl.num_programs(0)
    tokens, grad_out = tokens_ref[...], grad_ref[...]
    activ, grad_gate, grad_up = gated(
        against_rows(gate_ref[...], tokens),
        against_rows(up_ref[...], tokens),
        against_rows(down_ref[...], grad_out),
    )
    activ_ref[...], grad_gate_ref[...], grad_up_ref[...] = activ, grad_gate, grad_up
    back = over_tokens(grad_gate, gate_ref[...]) + over_tokens(grad_up, up_ref[...])
    back, final = back.astype(bf16), over_tokens(activ, down_ref[...]).astype(bf16)

    @pl.when(step < steps // 2)
    def _():
        out_refs[0][...] = back
        out_refs[2][...] = final

    @pl.when(step >= steps // 2)
    def _():
        out_refs[1][...] = back
        out_refs[3][...] = final


def feed_forward(tokens, grad_out, own_gate, own_up, own_down):
    count, width = tokens.shape
    hidden = own_gate.shape[0]
    half, tile = count // 2, 512
    if not is_cube() or half % tile or width % 128 or hidden % 16:
        activ, grad_gate, grad_up = gated(
            against_rows(own_gate, tokens),
            against_rows(own_up, tokens),
            against_rows(own_down, grad_out),
        )
        back = over_tokens(grad_gate, own_gate) + over_tokens(grad_up, own_up)
        back, final = back.astype(bf16), over_tokens(activ, own_down).astype(bf16)
        return activ, grad_gate, grad_up, back[:half], back[half:], final[:half], final[half:]
    steps = count // tile
    rows = pl.BlockSpec((tile, width), lambda i: (i, 0))
    whole = pl.BlockSpec((hidden, width), lambda i: (0, 0))
    columns = pl.BlockSpec((hidden, tile), lambda i: (0, i))
    first = pl.BlockSpec((tile, width), lambda i: (jnp.minimum(i, steps // 2 - 1), 0))
    second = pl.BlockSpec((tile, width), lambda i: (jnp.maximum(i - steps // 2, 0), 0))
    return pl.pallas_call(
        feed_forward_kernel,
        grid=(steps,),
        in_specs=[rows, rows, whole, whole, whole],
        out_specs=[columns] * 3 + [first, second] * 2,
        out_shape=[jax.ShapeDtypeStruct((hidden, count), bf16)] * 3
        + [jax.ShapeDtypeStruct((half, width), bf16)] * 4,
        compiler_params=pltpu.CompilerParams(vmem_limit_bytes=48 << 20),
        cost_estimate=pl.CostEstimate(
            flops=12 * count * width * hidden,
            bytes_accessed=2 * (4 * count * width + 3 * hidden * (width + count)),
            transcendentals=count * hidden,
        ),
    )(tokens, grad_out, own_gate, own_up, own_down)


def per_device(inputs, norm_in, w_in, taps, w_out, norm_mid, w_gate, w_up, w_down, cotangent):
    micros, rows_held, width = inputs.shape
    peers = lax.axis_size("fsdp")
    reach = taps.shape[0] - 1
    owned = w_in.shape[0]
    hidden = w_down.shape[0]
    all_rows = micros * rows_held

    gate_up = [jnp.transpose(w).reshape(peers, hidden, owned) for w in (w_gate, w_up)]
    groups = lax.axis_size("dp")
    if groups % 2 == 0:
        one_way = (lax.axis_index("dp") & 1) == 0
        gate_up = jnp.where(one_way, gate_up[0], gate_up[1])
    else:
        gate_up = jnp.concatenate(gate_up, axis=1)
    gate_up = exchange_early(gate_up)
    full_in = gather(w_in).reshape(width, 3 * width)
    smalls = jnp.concatenate([norm_in[None], norm_mid[None], taps], axis=0)
    smalls = jnp.pad(smalls, ((0, 8 - (reach + 3)), (0, 0)))
    smalls = jnp.transpose(gather(smalls)[:, : reach + 3], (1, 0, 2))
    smalls = relabel(smalls.reshape(reach + 3, width), back=True).astype(f32)
    gain_in, gain_mid, tap_values = smalls[0], smalls[1], smalls[2:]
    full_out = gather(w_out).reshape(width, width)
    grad_out = cotangent.reshape(all_rows, width)
    grad_out_all = gather(grad_out).reshape(peers * all_rows, width)
    gate_up = jnp.transpose(exchanged_early(gate_up), (1, 0, 2)).reshape(-1, width)
    if groups % 2 == 0:
        other = along(gate_up, "dp", [(i, i ^ 1) for i in range(groups)])
        own_gate = jnp.where(one_way, gate_up, other)
        own_up = jnp.where(one_way, other, gate_up)
    else:
        own_gate, own_up = gate_up[:hidden], gate_up[hidden:]

    resid = inputs.reshape(all_rows, width).astype(f32)
    scale_in = inverse_rms(resid)
    normed_in = relabel((resid * scale_in * gain_in).astype(bf16))
    projected = times(normed_in, full_in)
    gate_b = projected[:, :width]
    gate_c = projected[:, width : 2 * width]
    values = projected[:, 2 * width :]
    mixed = (gate_b * values).astype(bf16).reshape(micros, rows_held, width)
    earlier = from_behind(mixed[:, rows_held - reach :], "fsdp", 1)
    extended = jnp.concatenate([earlier, mixed], axis=1).astype(f32)
    convolved = jnp.zeros((micros, rows_held, width), f32)
    for offset in range(reach + 1):
        convolved = convolved + tap_values[offset] * extended[:, offset : offset + rows_held]
    convolved = convolved.reshape(all_rows, width)
    gated = relabel((gate_c * convolved).astype(bf16))
    middle = resid + times(gated, full_out)
    scale_mid = inverse_rms(middle)
    normed_mid = (middle * scale_mid * gain_mid).astype(bf16)

    normed_all = gather(normed_mid).reshape(peers * all_rows, width)
    activ, grad_gate, grad_up, theirs, ours, final_theirs, final_ours = feed_forward(
        normed_all, grad_out_all, own_gate, own_up, w_down
    )
    near = scatter_near(theirs, ours)

    term_gate = times(grad_gate, normed_all).astype(bf16)
    came_gate = inward(term_gate)
    near, grad_up, activ, term_gate = together(near, grad_up, activ, term_gate)
    across = scatter_across(ours, near)
    grad_normed_mid = scattered(ours, near, scatter_last(ours, near, across))
    term_up = times(grad_up, normed_all).astype(bf16)
    term_down = times(activ, grad_out_all).astype(bf16)
    grad_normed_mid, came_gate, term_up, term_down = together(
        grad_normed_mid, came_gate, term_up, term_down
    )
    came_up = inward(term_up)
    pair_gate = add_pair(term_gate, came_gate)
    far_gate = between(pair_gate)

    back_mid, gain_mid_grad = norm_back(middle, scale_mid, gain_mid, grad_normed_mid)
    grad_middle = grad_out.astype(f32) + back_mid
    grad_branch = grad_middle.astype(bf16)
    grad_gated = relabel(against_rows(grad_branch, full_out), back=True)
    grad_c = grad_gated * convolved
    grad_conv = (grad_gated * gate_c).astype(bf16).reshape(micros, rows_held, width)
    later = from_behind(grad_conv[:, :reach], "fsdp", -1)
    ext_grad = jnp.concatenate([grad_conv, later], axis=1).astype(f32)
    grad_mixed = jnp.zeros((micros, rows_held, width), f32)
    tap_terms = []
    for offset in range(reach + 1):
        grad_mixed = (
            grad_mixed + tap_values[offset] * ext_grad[:, reach - offset : reach - offset + rows_held]
        )
        tap_terms.append(
            jnp.sum(extended[:, offset : offset + rows_held] * ext_grad[:, :rows_held], axis=(0, 1))
        )
    grad_mixed = grad_mixed.reshape(all_rows, width)
    grad_proj = [
        (grad_mixed * values).astype(bf16),
        grad_c.astype(bf16),
        (grad_mixed * gate_b).astype(bf16),
    ]

    half = width // 2
    normed_theirs, normed_ours = normed_in[:, :half], normed_in[:, half:]
    grad_b_v = jnp.concatenate([grad_proj[0], grad_proj[2]], axis=1)
    terms_out_c = [
        jnp.concatenate(
            [over_tokens(p, grad_branch).astype(bf16), over_tokens(q, grad_proj[1]).astype(bf16)],
            axis=1,
        )
        for p, q in ((gated[:, :half], normed_theirs), (gated[:, half:], normed_ours))
    ]
    terms_b_v = [over_tokens(p, grad_b_v).astype(bf16) for p in (normed_theirs, normed_ours)]
    grad_normed_in = relabel(
        against_rows(jnp.concatenate(grad_proj, axis=1), full_in), back=True
    )
    back_in, gain_in_grad = norm_back(resid, scale_in, gain_in, grad_normed_in)
    grad_inputs = (grad_middle + back_in).reshape(micros, rows_held, width)
    smalls = relabel(jnp.stack([gain_in_grad, gain_mid_grad] + tap_terms))
    smalls = jnp.pad(jnp.transpose(smalls), ((0, 0), (0, 128 - (reach + 3)))).astype(bf16)
    terms_b_v = [
        jnp.concatenate([terms_b_v[0], smalls[:half]], axis=1),
        jnp.concatenate([terms_b_v[1], smalls[half:]], axis=1),
    ]
    near_out_c = scatter_near(*terms_out_c)
    across_out_c = scatter_across(terms_out_c[1], near_out_c)
    across_out_c, terms_b_v[0], far_gate, came_up, term_down = together(
        across_out_c, terms_b_v[0], far_gate, came_up, term_down
    )

    total_gate = add_pair(pair_gate, far_gate)
    both = inward_outward(term_down, total_gate)
    pair_up = add_pair(term_up, came_up)
    far_up = between(pair_up)
    last_out_c = scatter_last(terms_out_c[1], near_out_c, across_out_c)
    near_b_v = scatter_near(*terms_b_v)
    across_b_v = scatter_across(terms_b_v[1], near_b_v)

    came_down, out_gate, far_up, across_b_v, *last_out_c = together(
        *both, far_up, across_b_v, *last_out_c
    )
    rows_out_c = scattered(terms_out_c[1], near_out_c, last_out_c).astype(bf16)
    came_out_c = inward(rows_out_c)
    pair_down = add_pair(term_down, came_down)
    far_down = between(pair_down)
    total_up = add_pair(pair_up, far_up)
    out_up = outward(total_up)
    last_b_v = scatter_last(terms_b_v[1], near_b_v, across_b_v)

    came_out_c, out_up, far_down, final_theirs, *last_b_v = together(
        came_out_c, out_up, far_down, final_theirs, *last_b_v
    )
    rows_b_v = scattered(terms_b_v[1], near_b_v, last_b_v).astype(bf16)
    came_b_v = inward(rows_b_v)
    pair_out_c = add_pair(rows_out_c, came_out_c)
    far_out_c = between(pair_out_c)
    total_down = add_pair(pair_down, far_down)
    out_down = outward(total_down)
    mine = exchange_chips(
        jnp.concatenate(
            [
                jnp.transpose(settle(t, o).reshape(hidden, peers, owned), (1, 0, 2))
                for t, o in ((total_gate, out_gate), (total_up, out_up))
            ],
            axis=1,
        )
    )

    came_b_v, far_out_c, out_down, final_theirs, *mine = together(
        came_b_v, far_out_c, out_down, final_theirs, *mine
    )
    pair_b_v = add_pair(rows_b_v, came_b_v)
    far_b_v = between(pair_b_v)
    total_out_c = add_pair(pair_out_c, far_out_c)
    out_out_c = outward(total_out_c)
    near_final = scatter_near(final_theirs, final_ours)
    across_final = scatter_across(final_ours, near_final)
    grad_w_down = settle(total_down, out_down).astype(f32)
    mine = exchange_cores(mine)
    by_rows = Layout(major_to_minor=(0, 1))
    grad_w_gate, grad_w_up = [
        with_layout_constraint(
            jnp.transpose(part.reshape(peers * hidden, owned)).astype(f32), by_rows
        )
        for part in (mine[:, :hidden], mine[:, hidden:])
    ]

    far_b_v, out_out_c, across_final, grad_w_down, grad_w_gate, grad_w_up = together(
        far_b_v, out_out_c, across_final, grad_w_down, grad_w_gate, grad_w_up
    )
    total_b_v = add_pair(pair_b_v, far_b_v)
    out_b_v = outward(total_b_v)
    last_final = scatter_last(final_ours, near_final, across_final)
    final = scattered(final_ours, near_final, last_final)
    block_out = (middle + final).astype(bf16).reshape(micros, rows_held, width)
    out_b_v, block_out = together(out_b_v, block_out)
    total_out_c = settle(total_out_c, out_out_c).astype(f32)
    total_b_v = settle(total_b_v, out_b_v).astype(f32)
    grad_w_out = total_out_c[:, :width]
    grad_w_in = jnp.concatenate(
        [total_b_v[:, :width], total_out_c[:, width:], total_b_v[:, width : 2 * width]], axis=1
    )
    smalls = jnp.transpose(total_b_v[:, 2 * width : 2 * width + reach + 3])
    return (
        block_out,
        grad_inputs,
        smalls[0],
        grad_w_in,
        smalls[2:],
        grad_w_out,
        smalls[1],
        grad_w_gate,
        grad_w_up,
        grad_w_down,
    )


def solution(mesh):
    return jax.shard_map(
        per_device,
        mesh=mesh,
        in_specs=(
            P("dp", "fsdp", None),
            P("fsdp"),
            P("fsdp", None),
            P(None, "fsdp"),
            P("fsdp", None),
            P("fsdp"),
            P("fsdp", None),
            P("fsdp", None),
            P("fsdp", None),
            P("dp", "fsdp", None),
        ),
        out_specs=(
            P("dp", "fsdp", None),
            P("dp", "fsdp", None),
            P("fsdp"),
            P("fsdp", None),
            P(None, "fsdp"),
            P("fsdp", None),
            P("fsdp"),
            P("fsdp", None),
            P("fsdp", None),
            P("fsdp", None),
        ),
        check_vma=False,
    )
```

time: 433 us -> 383 us (0.88)
  the two profiles are of different devices: /device:TPU:0 before, /device:TPU:8 now
where the time goes in v3:
time: 383 us; the launch traced here: 376 us
  waiting for transfers between devices  160 us (42%)
  starting transfers between devices  79.4 us (21%)
  other arithmetic  62.3 us (16%)
  matrix products  25.1 us (7%)
  Pallas kernels  24.4 us (6%)
  local copies, waits for them, and re-layouts  22.4 us (6%)
    ppermute x64, waiting for transfers between devices, along(): return lax.ppermute(shard, axis, pairs)  159 us
    ppermute x64, starting transfers between devices, along(): return lax.ppermute(shard, axis, pairs)  75.4 us
    pallas_call x1, Pallas kernels, feed_forward(): pl.pallas_call(feed_forward_kernel, grid=(steps,), in_specs=[rows, rows,...  24.4 us
    dot_general x5, matrix products, times(): return jnp.dot(left, right, preferred_element_type=f32)  15.6 us
    unnamed x143, local copies, waits for them, and re-layouts  13.6 us
    convert_element_type x9, other arithmetic, add_pair(): (one.astype(f32) + other.astype(f32)).astype(bf16)  8.29 us
  transfers between devices with their start and end apart: 66, of which 31 were waited for; matrix products, arithmetic and copies ran while one was open for 24% of the time, Pallas kernels for 0%

profile of v3, /device:TPU:8, one launch (start us, length us, event | category | flops | bytes accessed | tf_op | source)
XLA Modules:
  0.0 375.9 jit_solution(14656315712665416197)
XLA Ops:
  8.3 2.4 copy.72
  19.7 3.4 collective-permute-start.4
  37.4 9.7 %collective-permute-done.6 = bf16[128,3072]{1,0:T(8,128)(2,1)S(1)} collective-permute-done((bf16[128,3072]{1,0:T(8,128)(2,1)}, bf16[128,3072]{1,0:T(8,128)(2,1)S(1)}, u32[]{:S(2)}, u32[]{:S(2)}) %collective-permute-start.6) | collective-permute-done | bytes 786464 | tf_op jit(solution)/shard_map/ppermute | solution.py:15
  48.6 2.9 collective-permute-done.5
  51.8 2.5 collective-permute-start.7
  54.3 3.5 collective-permute-done.27
  59.9 2.2 collective-permute-start.15
  62.1 5.8 %collective-permute-done.29 = bf16[2,576,128]{2,1,0:T(8,128)(2,1)S(1)} collective-permute-done((bf16[2,576,128]{2,1,0:T(8,128)(2,1)S(1)}, bf16[2,576,128]{2,1,0:T(8,128)(2,1)S(1)}, u32[]{:S(2)}, u32[]{:S(2)}) %collective-permute-start.29) | collective-permute-done | bytes 294944 | tf_op jit(solution)/shard_map/ppermute | solution.py:15
  70.7 12.0 %collective-permute-done.8 = bf16[128,3072]{1,0:T(8,128)(2,1)S(1)} collective-permute-done((bf16[128,3072]{1,0:T(8,128)(2,1)S(1)}, bf16[128,3072]{1,0:T(8,128)(2,1)S(1)}, u32[]{:S(2)}, u32[]{:S(2)}) %collective-permute-start.8) | collective-permute-done | bytes 786464 | tf_op jit(solution)/shard_map/ppermute | solution.py:15
  88.0 2.4 collective-permute-start.10
  95.1 2.6 collective-permute-start.16
  99.5 10.2 %collective-permute-done.16 = bf16[256,1024]{1,0:T(8,128)(2,1)S(1)} collective-permute-done((bf16[256,1024]{1,0:T(8,128)(2,1)S(1)}, bf16[256,1024]{1,0:T(8,128)(2,1)S(1)}, u32[]{:S(2)}, u32[]{:S(2)}) %collective-permute-start.16) | collective-permute-done | bytes 524320 | tf_op jit(solution)/shard_map/ppermute | solution.py:15
  113.0 8.2 %collective-permute-done.19 = bf16[256,1024]{1,0:T(8,128)(2,1)S(1)} collective-permute-done((bf16[256,1024]{1,0:T(8,128)(2,1)S(1)}, bf16[256,1024]{1,0:T(8,128)(2,1)S(1)}, u32[]{:S(2)}, u32[]{:S(2)}) %collective-permute-start.19) | collective-permute-done | bytes 524320 | tf_op jit(solution)/shard_map/ppermute | solution.py:15
  123.4 2.0 copy-done.21
  125.4 24.4 %shard_map.177 = (bf16[576,2048]{1,0:T(8,128)(2,1)}, bf16[576,2048]{1,0:T(8,128)(2,1)}, bf16[576,2048]{1,0:T(8,128)(2,1)}, bf16[1024,1024]{1,0:T(8,128)(2,1)S(1)...) custom-call(bf16[2048,1024]{1,0:T(8,128)(2,1)} %bitcast.276, ...), custom_call_target="tpu_custom_call" | custom-call | flops 14495514624 | bytes 27394048 | tf_op jit(solution)/shard_map/pallas_call | solution.py:289
  149.9 5.6 %convolution_convert_fusion.4 = bf16[576,1024]{1,0:T(8,128)(2,1)S(1)} fusion(bf16[576,2048]{1,0:T(8,128)(2,1)} %get-tuple-element.62, bf16[2048,1024]{1,0:T(8,128)(2,1)} %bitcast.277), kind=kOutput, calls=%fused_computation.44 | convolution fusion | flops 2416508928 | bytes 7733248 | tf_op jit(solution)/shard_map/dot_general | solution.py:223
  158.0 3.6 convolution_convert_fusion.2
  161.7 5.2 %collective-permute-done.32 = bf16[256,1024]{1,0:T(8,128)(2,1)S(1)} collective-permute-done((bf16[256,1024]{1,0:T(8,128)(2,1)S(1)}, bf16[256,1024]{1,0:T(8,128)(2,1)S(1)}, u32[]{:S(2)}, u32[]{:S(2)}) %collective-permute-start.32) | collective-permute-done | bytes 524320 | tf_op jit(solution)/shard_map/ppermute | solution.py:15
  168.9 3.6 convolution_convert_fusion.3
  172.5 8.3 %collective-permute-done.33 = bf16[256,1024]{1,0:T(8,128)(2,1)S(1)} collective-permute-done((bf16[256,1024]{1,0:T(8,128)(2,1)S(1)}, bf16[256,1024]{1,0:T(8,128)(2,1)S(1)}, u32[]{:S(2)}, u32[]{:S(2)}) %collective-permute-start.33) | collective-permute-done | bytes 524320 | tf_op jit(solution)/shard_map/ppermute | solution.py:15
  181.2 4.5 %collective-permute-done.35 = bf16[576,1024]{1,0:T(8,128)(2,1)S(1)} collective-permute-done((bf16[576,1024]{1,0:T(8,128)(2,1)S(1)}, bf16[576,1024]{1,0:T(8,128)(2,1)S(1)}, u32[]{:S(2)}, u32[]{:S(2)}) %collective-permute-start.35) | collective-permute-done | bytes 1179680 | tf_op jit(solution)/shard_map/ppermute | solution.py:15
  189.1 3.5 collective-permute-start.39
  208.8 2.1 convolution_convert_fusion
  214.5 4.2 %collective-permute-done.39 = bf16[576,1024]{1,0:T(8,128)(2,1)} collective-permute-done((bf16[576,1024]{1,0:T(8,128)(2,1)}, bf16[576,1024]{1,0:T(8,128)(2,1)}, u32[]{:S(2)}, u32[]{:S(2)}) %collective-permute-start.39) | collective-permute-done | bytes 1179680 | tf_op jit(solution)/shard_map/ppermute | solution.py:15
  218.7 3.2 collective-permute-done.40
  222.0 2.0 convolution_convert_fusion.1
  224.1 2.4 broadcast_select_fusion.1
  226.5 3.2 collective-permute-start.42
  229.7 2.1 add_convert_fusion.3
  231.8 2.5 collective-permute-start.43
  239.7 16.5 %collective-permute-done.42 = bf16[576,1024]{1,0:T(8,128)(2,1)S(1)} collective-permute-done((bf16[576,1024]{1,0:T(8,128)(2,1)S(1)}, bf16[576,1024]{1,0:T(8,128)(2,1)S(1)}, u32[]{:S(2)}, u32[]{:S(2)}) %collective-permute-start.42) | collective-permute-done | bytes 1179680 | tf_op jit(solution)/shard_map/ppermute | solution.py:15
  256.4 5.5 %collective-permute-done.43 = bf16[576,1024]{1,0:T(8,128)(2,1)S(1)} collective-permute-done((bf16[576,1024]{1,0:T(8,128)(2,1)S(1)}, bf16[576,1024]{1,0:T(8,128)(2,1)S(1)}, u32[]{:S(2)}, u32[]{:S(2)}) %collective-permute-start.43) | collective-permute-done | bytes 1179680 | tf_op jit(solution)/shard_map/ppermute | solution.py:15
  264.2 2.6 collective-permute-start.49
  272.6 13.0 %collective-permute-done.47 = bf16[128,2048]{1,0:T(8,128)(2,1)S(1)} collective-permute-done((bf16[128,2048]{1,0:T(8,128)(2,1)S(1)}, bf16[128,2048]{1,0:T(8,128)(2,1)S(1)}, u32[]{:S(2)}, u32[]{:S(2)}) %collective-permute-start.47) | collective-permute-done | bytes 524320 | tf_op jit(solution)/shard_map/ppermute | solution.py:15
  285.6 3.6 collective-permute-done.48
  289.2 4.2 %collective-permute-done.49 = bf16[576,1024]{1,0:T(8,128)(2,1)S(1)} collective-permute-done((bf16[576,1024]{1,0:T(8,128)(2,1)S(1)}, bf16[576,1024]{1,0:T(8,128)(2,1)S(1)}, u32[]{:S(2)}, u32[]{:S(2)}) %collective-permute-start.49) | collective-permute-done | bytes 1179680 | tf_op jit(solution)/shard_map/ppermute | solution.py:15
  294.0 2.4 collective-permute-start.53
  297.7 2.4 bitcast_bitcast_fusion
  305.3 2.9 collective-permute-done.53
  310.7 11.4 %collective-permute-done.52 = bf16[128,2176]{1,0:T(8,128)(2,1)S(1)} collective-permute-done((bf16[128,2176]{1,0:T(8,128)(2,1)S(1)}, bf16[128,2176]{1,0:T(8,128)(2,1)S(1)}, u32[]{:S(2)}, u32[]{:S(2)}) %collective-permute-start.52) | collective-permute-done | bytes 557088 | tf_op jit(solution)/shard_map/ppermute | solution.py:15
  322.1 5.0 %collective-permute-done.56 = bf16[2,1152,128]{2,1,0:T(8,128)(2,1)S(1)} collective-permute-done((bf16[2,1152,128]{2,1,0:T(8,128)(2,1)S(1)}, bf16[2,1152,128]{2,1,0:T(8,128)(2,1)S(1)}, u32[]{:S(2)}, u32[]{:S(2)}) %collective-permute-start.56) | collective-permute-done | bytes 589856 | tf_op jit(solution)/shard_map/ppermute | solution.py:15
  328.5 2.1 collective-permute-start.59
  331.5 3.5 collective-permute-start.58
  340.6 2.0 add_convert_fusion.11
  345.0 1.9 copy.88
  347.0 3.2 copy.87
  360.7 9.2 %collective-permute-done.64 = bf16[256,1024]{1,0:T(8,128)(2,1)S(1)} collective-permute-done((bf16[256,1024]{1,0:T(8,128)(2,1)S(1)}, bf16[256,1024]{1,0:T(8,128)(2,1)S(1)}, u32[]{:S(2)}, u32[]{:S(2)}) %collective-permute-start.64) | collective-permute-done | bytes 524320 | tf_op jit(solution)/shard_map/ppermute | solution.py:15
  370.5 2.3 add_convert_fusion.10
  (397 shorter events, 129.7 us)
Async XLA Ops:
  1.5 13.0 %collective-permute-start = (bf16[8,128]{1,0:T(8,128)(2,1)S(1)}, bf16[8,128]{1,0:T(8,128)(2,1)S(1)}, u32[]{:S(2)}, u32[]{:S(2)}) collective-permute-start(bf16[8,128]{1,0:T(8,128)(2,1)S(1)} %fusion.62), channel_id=1, source_target_pairs={{0,2},{1,3},{2,0},{3,1},{4,6},{5,7},{6,4},{7,5},{8,10},{9,11},{10,... | collective-permute-start | bytes 6152 | tf_op jit(solution)/shard_map/ppermute | solution.py:15
  3.0 11.5 %collective-permute-start.1 = (bf16[8,128]{1,0:T(8,128)(2,1)S(1)}, bf16[8,128]{1,0:T(8,128)(2,1)S(1)}, u32[]{:S(2)}, u32[]{:S(2)}) collective-permute-start(bf16[8,128]{1,0:T(8,128)(2,1)S(1)} %fusion.62), channel_id=1, source_target_pairs={{0,4},{1,5},{2,6},{3,7},{4,0},{5,1},{6,2},{7,3},{8,12},{9,13},{10,... | collective-permute-start | bytes 6152 | tf_op jit(solution)/shard_map/ppermute | solution.py:15
  4.5 26.6 %collective-permute-start.12 = (bf16[128,1024]{1,0:T(8,128)(2,1)}, bf16[128,1024]{1,0:T(8,128)(2,1)S(1)}, u32[]{:S(2)}, u32[]{:S(2)}) collective-permute-start(bf16[128,1024]{1,0:T(8,128)(2,1)} %param.14), channel_id=1, source_target_pairs={{0,4},{1,5},{2,6},{3,7},{4,0},{5,1},{6,2},{7,3},{8,12},{9,13},{10,... | collective-permute-start | bytes 786440 | tf_op jit(solution)/shard_map/ppermute | solution.py:15
  5.0 26.6 %collective-permute-start.11 = (bf16[128,1024]{1,0:T(8,128)(2,1)}, bf16[128,1024]{1,0:T(8,128)(2,1)}, u32[]{:S(2)}, u32[]{:S(2)}) collective-permute-start(bf16[128,1024]{1,0:T(8,128)(2,1)} %param.14), channel_id=1, source_target_pairs={{0,2},{1,3},{2,0},{3,1},{4,6},{5,7},{6,4},{7,5},{8,10},{9,11},{10,... | collective-permute-start | bytes 786440 | tf_op jit(solution)/shard_map/ppermute | solution.py:15
  5.6 28.1 %collective-permute-start.21 = (bf16[256,1024]{1,0:T(8,128)(2,1)}, bf16[256,1024]{1,0:T(8,128)(2,1)S(1)}, u32[]{:S(2)}, u32[]{:S(2)}) collective-permute-start(bf16[256,1024]{1,0:T(8,128)(2,1)} %bitcast.254), channel_id=1, source_target_pairs={{0,2},{1,3},{2,0},{3,1},{4,6},{5,7},{6,4},{7,5},{8,10},{9,11},{10,... | collective-permute-start | bytes 1572872 | tf_op jit(solution)/shard_map/ppermute | solution.py:15
  18.2 17.1 %collective-permute-start.22 = (bf16[256,1024]{1,0:T(8,128)(2,1)S(1)}, bf16[256,1024]{1,0:T(8,128)(2,1)S(1)}, u32[]{:S(2)}, u32[]{:S(2)}) collective-permute-start(bf16[256,1024]{1,0:T(8,128)(2,1)S(1)} %bitcast.255), channel_id=1, source_target_pairs={{0,4},{1,5},{2,6},{3,7},{4,0},{5,1},{6,2},{7,3},{8,12},{9,13},{10,... | collective-permute-start | bytes 1572872 | tf_op jit(solution)/shard_map/ppermute | solution.py:15
  23.9 23.2 %collective-permute-start.6 = (bf16[128,3072]{1,0:T(8,128)(2,1)}, bf16[128,3072]{1,0:T(8,128)(2,1)S(1)}, u32[]{:S(2)}, u32[]{:S(2)}) collective-permute-start(bf16[128,3072]{1,0:T(8,128)(2,1)} %param.12), channel_id=1, source_target_pairs={{0,4},{1,5},{2,6},{3,7},{4,0},{5,1},{6,2},{7,3},{8,12},{9,13},{10,... | collective-permute-start | bytes 2359304 | tf_op jit(solution)/shard_map/ppermute | solution.py:15
  31.1 20.4 %collective-permute-start.5 = (bf16[128,3072]{1,0:T(8,128)(2,1)S(1)}, bf16[128,3072]{1,0:T(8,128)(2,1)S(1)}, u32[]{:S(2)}, u32[]{:S(2)}) collective-permute-start(bf16[128,3072]{1,0:T(8,128)(2,1)S(1)} %copy-done.9), channel_id=1, source_target_pairs={{0,2},{1,3},{2,0},{3,1},{4,6},{5,7},{6,4},{7,5},{8,10},{9,11},{10,... | collective-permute-start | bytes 2359304 | tf_op jit(solution)/shard_map/ppermute | solution.py:15
  33.7 25.7 %collective-permute-start.14 = (bf16[128,1024]{1,0:T(8,128)(2,1)S(1)}, bf16[128,1024]{1,0:T(8,128)(2,1)S(1)}, u32[]{:S(2)}, u32[]{:S(2)}) collective-permute-start(bf16[128,1024]{1,0:T(8,128)(2,1)S(1)} %broadcast_select_fusion.9), channel_id=1, source_target_pairs={{0,4},{1,3},{2,6},{3,1},{4,0},{5,7},{6,2},{7,5},{8,12},{9,11},{10,... | collective-permute-start | bytes 786440 | tf_op jit(solution)/shard_map/ppermute | solution.py:15
  35.3 34.7 %collective-permute-start.13 = (bf16[3,128,1024]{2,1,0:T(8,128)(2,1)S(1)}, bf16[3,128,1024]{2,1,0:T(8,128)(2,1)S(1)}, u32[]{:S(2)}, u32[]{:S(2)}) collective-permute-start(bf16[3,128,1024]{2,1,0:T(8,128)(2,1)S(1)} %pad_maximum_fusion.10), channel_id=1, source_target_pairs={{0,1},{1,0},{2,3},{3,2},{4,5},{5,4},{6,7},{7,6},{8,9},{9,8},{10,11... | collective-permute-start | bytes 2359304 | tf_op jit(solution)/shard_map/ppermute | solution.py:15
  36.3 21.5 %collective-permute-start.27 = (bf16[2,576,128]{2,1,0:T(8,128)(2,1)S(1)}, bf16[2,576,128]{2,1,0:T(8,128)(2,1)S(1)}, u32[]{:S(2)}, u32[]{:S(2)}) collective-permute-start(bf16[2,576,128]{2,1,0:T(8,128)(2,1)S(1)} %get-tuple-element.279), channel_id=1, source_target_pairs={{0,2},{1,3},{2,0},{3,1},{4,6},{5,7},{6,4},{7,5},{8,10},{9,11},{10,... | collective-permute-start | bytes 884744 | tf_op jit(solution)/shard_map/ppermute | solution.py:15
  47.1 12.8 %collective-permute-start.28 = (bf16[2,576,128]{2,1,0:T(8,128)(2,1)S(1)}, bf16[2,576,128]{2,1,0:T(8,128)(2,1)S(1)}, u32[]{:S(2)}, u32[]{:S(2)}) collective-permute-start(bf16[2,576,128]{2,1,0:T(8,128)(2,1)S(1)} %get-tuple-element.280), channel_id=1, source_target_pairs={{0,4},{1,5},{2,6},{3,7},{4,0},{5,1},{6,2},{7,3},{8,12},{9,13},{10,... | collective-permute-start | bytes 884744 | tf_op jit(solution)/shard_map/ppermute | solution.py:15
  51.8 32.1 %collective-permute-start.7 = (bf16[3,128,3072]{2,1,0:T(8,128)(2,1)S(1)}, bf16[3,128,3072]{2,1,0:T(8,128)(2,1)S(1)}, u32[]{:S(2)}, u32[]{:S(2)}) collective-permute-start(bf16[3,128,3072]{2,1,0:T(8,128)(2,1)S(1)} %pad_maximum_fusion), channel_id=1, source_target_pairs={{0,1},{1,0},{2,3},{3,2},{4,5},{5,4},{6,7},{7,6},{8,9},{9,8},{10,11... | collective-permute-start | bytes 7077896 | tf_op jit(solution)/shard_map/ppermute | solution.py:15
  59.4 40.0 %collective-permute-start.24 = (bf16[256,1024]{1,0:T(8,128)(2,1)S(1)}, bf16[256,1024]{1,0:T(8,128)(2,1)S(1)}, u32[]{:S(2)}, u32[]{:S(2)}) collective-permute-start(bf16[256,1024]{1,0:T(8,128)(2,1)S(1)} %broadcast_select_fusion.7), channel_id=1, source_target_pairs={{0,4},{1,3},{2,6},{3,1},{4,0},{5,7},{6,2},{7,5},{8,12},{9,11},{10,... | collective-permute-start | bytes 1572872 | tf_op jit(solution)/shard_map/ppermute | solution.py:15
  68.0 14.7 %collective-permute-start.8 = (bf16[128,3072]{1,0:T(8,128)(2,1)S(1)}, bf16[128,3072]{1,0:T(8,128)(2,1)S(1)}, u32[]{:S(2)}, u32[]{:S(2)}) collective-permute-start(bf16[128,3072]{1,0:T(8,128)(2,1)S(1)} %broadcast_select_fusion.5), channel_id=1, source_target_pairs={{0,4},{1,3},{2,6},{3,1},{4,0},{5,7},{6,2},{7,5},{8,12},{9,11},{10,... | collective-permute-start | bytes 2359304 | tf_op jit(solution)/shard_map/ppermute | solution.py:15
  70.0 41.7 %collective-permute-start.23 = (bf16[3,256,1024]{2,1,0:T(8,128)(2,1)S(1)}, bf16[3,256,1024]{2,1,0:T(8,128)(2,1)S(1)}, u32[]{:S(2)}, u32[]{:S(2)}) collective-permute-start(bf16[3,256,1024]{2,1,0:T(8,128)(2,1)S(1)} %pad_maximum_fusion.7), channel_id=1, source_target_pairs={{0,1},{1,0},{2,3},{3,2},{4,5},{5,4},{6,7},{7,6},{8,9},{9,8},{10,11... | collective-permute-start | bytes 4718600 | tf_op jit(solution)/shard_map/ppermute | solution.py:15
  70.1 41.4 %collective-permute-start.30 = (bf16[576,1024]{1,0:T(8,128)(2,1)S(1)}, bf16[576,1024]{1,0:T(8,128)(2,1)S(1)}, u32[]{:S(2)}, u32[]{:S(2)}) collective-permute-start(bf16[576,1024]{1,0:T(8,128)(2,1)S(1)} %bitcast.266), channel_id=1, source_target_pairs={{0,8},{8,0},{16,24},{24,16},{1,9},{9,1},{17,25},{25,17},{2,10},{10... | collective-permute-start | bytes 3538952 | tf_op jit(solution)/shard_map/ppermute | solution.py:15
  95.1 14.7 %collective-permute-start.16 = (bf16[256,1024]{1,0:T(8,128)(2,1)S(1)}, bf16[256,1024]{1,0:T(8,128)(2,1)S(1)}, u32[]{:S(2)}, u32[]{:S(2)}) collective-permute-start(bf16[256,1024]{1,0:T(8,128)(2,1)S(1)} %multiply_convert_fusion.1), channel_id=1, source_target_pairs={{0,2},{1,3},{2,0},{3,1},{4,6},{5,7},{6,4},{7,5},{8,10},{9,11},{10,... | collective-permute-start | bytes 1572872 | tf_op jit(solution)/shard_map/ppermute | solution.py:15
  97.7 13.5 %collective-permute-start.17 = (bf16[256,1024]{1,0:T(8,128)(2,1)S(1)}, bf16[256,1024]{1,0:T(8,128)(2,1)S(1)}, u32[]{:S(2)}, u32[]{:S(2)}) collective-permute-start(bf16[256,1024]{1,0:T(8,128)(2,1)S(1)} %multiply_convert_fusion.1), channel_id=1, source_target_pairs={{0,4},{1,5},{2,6},{3,7},{4,0},{5,1},{6,2},{7,3},{8,12},{9,13},{10,... | collective-permute-start | bytes 1572872 | tf_op jit(solution)/shard_map/ppermute | solution.py:15
  99.4 12.9 %collective-permute-start.25 = (bf16[256,1024]{1,0:T(8,128)(2,1)S(1)}, bf16[256,1024]{1,0:T(8,128)(2,1)S(1)}, u32[]{:S(2)}, u32[]{:S(2)}) collective-permute-start(bf16[256,1024]{1,0:T(8,128)(2,1)S(1)} %collective-permute-done.24), channel_id=1, source_target_pairs={{0,1},{1,0},{2,3},{3,2},{4,5},{5,4},{6,7},{7,6},{8,9},{9,8},{10,11... | collective-permute-start | bytes 1572872 | tf_op jit(solution)/shard_map/ppermute | solution.py:15
  155.6 30.1 %collective-permute-start.35 = (bf16[576,1024]{1,0:T(8,128)(2,1)S(1)}, bf16[576,1024]{1,0:T(8,128)(2,1)S(1)}, u32[]{:S(2)}, u32[]{:S(2)}) collective-permute-start(bf16[576,1024]{1,0:T(8,128)(2,1)S(1)} %convolution_convert_fusion.4), channel_id=1, source_target_pairs={{0,8},{24,16},{1,9},{25,17},{2,10},{26,18},{3,11},{27,19},{4,12},{... | collective-permute-start | bytes 3538952 | tf_op jit(solution)/shard_map/ppermute | solution.py:15
  167.4 13.4 %collective-permute-start.33 = (bf16[256,1024]{1,0:T(8,128)(2,1)S(1)}, bf16[256,1024]{1,0:T(8,128)(2,1)S(1)}, u32[]{:S(2)}, u32[]{:S(2)}) collective-permute-start(bf16[256,1024]{1,0:T(8,128)(2,1)S(1)} %get-tuple-element.263), channel_id=1, source_target_pairs={{0,2},{1,3},{2,0},{3,1},{4,6},{5,7},{6,4},{7,5},{8,10},{9,11},{10,... | collective-permute-start | bytes 1572872 | tf_op jit(solution)/shard_map/ppermute | solution.py:15
  167.8 13.1 %collective-permute-start.34 = (bf16[256,1024]{1,0:T(8,128)(2,1)S(1)}, bf16[256,1024]{1,0:T(8,128)(2,1)S(1)}, u32[]{:S(2)}, u32[]{:S(2)}) collective-permute-start(bf16[256,1024]{1,0:T(8,128)(2,1)S(1)} %get-tuple-element.264), channel_id=1, source_target_pairs={{0,4},{1,5},{2,6},{3,7},{4,0},{5,1},{6,2},{7,3},{8,12},{9,13},{10,... | collective-permute-start | bytes 1572872 | tf_op jit(solution)/shard_map/ppermute | solution.py:15
  189.1 29.6 %collective-permute-start.39 = (bf16[576,1024]{1,0:T(8,128)(2,1)}, bf16[576,1024]{1,0:T(8,128)(2,1)}, u32[]{:S(2)}, u32[]{:S(2)}) collective-permute-start(bf16[576,1024]{1,0:T(8,128)(2,1)} %add_convert_fusion.5), channel_id=1, source_target_pairs={{8,16},{16,8},{9,17},{17,9},{10,18},{18,10},{11,19},{19,11},{12,20... | collective-permute-start | bytes 3538952 | tf_op jit(solution)/shard_map/ppermute | solution.py:15
  192.6 29.4 %collective-permute-start.40 = (bf16[576,1024]{1,0:T(8,128)(2,1)}, bf16[576,1024]{1,0:T(8,128)(2,1)}, u32[]{:S(2)}, u32[]{:S(2)}) collective-permute-start(bf16[576,1024]{1,0:T(8,128)(2,1)} %convolution_convert_fusion.3), channel_id=1, source_target_pairs={{0,8},{24,16},{1,9},{25,17},{2,10},{26,18},{3,11},{27,19},{4,12},{... | collective-permute-start | bytes 3538952 | tf_op jit(solution)/shard_map/ppermute | solution.py:15
  198.8 12.1 %collective-permute-start.37 = (bf16[512,2048]{1,0:T(8,128)(2,1)}, bf16[512,2048]{1,0:T(8,128)(2,1)}, u32[]{:S(2)}, u32[]{:S(2)}) collective-permute-start(bf16[512,2048]{1,0:T(8,128)(2,1)} %pad_maximum_fusion.4), channel_id=1, source_target_pairs={{0,1},{1,0},{2,3},{3,2},{4,5},{5,4},{6,7},{7,6},{8,9},{9,8},{10,11... | collective-permute-start | bytes 6291464 | tf_op jit(solution)/shard_map/ppermute | solution.py:15
  222.0 12.3 %collective-permute-start.41 = (bf16[512,2176]{1,0:T(8,128)(2,1)}, bf16[512,2176]{1,0:T(8,128)(2,1)}, u32[]{:S(2)}, u32[]{:S(2)}) collective-permute-start(bf16[512,2176]{1,0:T(8,128)(2,1)} %pad_maximum_fusion.3), channel_id=1, source_target_pairs={{0,1},{1,0},{2,3},{3,2},{4,5},{5,4},{6,7},{7,6},{8,9},{9,8},{10,11... | collective-permute-start | bytes 6684680 | tf_op jit(solution)/shard_map/ppermute | solution.py:15
  226.5 29.8 %collective-permute-start.42 = (bf16[576,1024]{1,0:T(8,128)(2,1)S(1)}, bf16[576,1024]{1,0:T(8,128)(2,1)S(1)}, u32[]{:S(2)}, u32[]{:S(2)}) collective-permute-start(bf16[576,1024]{1,0:T(8,128)(2,1)S(1)} %broadcast_select_fusion.1), channel_id=1, source_target_pairs={{0,8},{24,16},{8,0},{16,24},{1,9},{25,17},{9,1},{17,25},{2,10},{26... | collective-permute-start | bytes 3538952 | tf_op jit(solution)/shard_map/ppermute | solution.py:15
  231.8 30.1 %collective-permute-start.43 = (bf16[576,1024]{1,0:T(8,128)(2,1)S(1)}, bf16[576,1024]{1,0:T(8,128)(2,1)S(1)}, u32[]{:S(2)}, u32[]{:S(2)}) collective-permute-start(bf16[576,1024]{1,0:T(8,128)(2,1)S(1)} %add_convert_fusion.3), channel_id=1, source_target_pairs={{8,16},{16,8},{9,17},{17,9},{10,18},{18,10},{11,19},{19,11},{12,20... | collective-permute-start | bytes 3538952 | tf_op jit(solution)/shard_map/ppermute | solution.py:15
  235.5 26.4 %collective-permute-start.44 = (bf16[128,2176]{1,0:T(8,128)(2,1)S(1)}, bf16[128,2176]{1,0:T(8,128)(2,1)S(1)}, u32[]{:S(2)}, u32[]{:S(2)}) collective-permute-start(bf16[128,2176]{1,0:T(8,128)(2,1)S(1)} %add_convert_fusion.9), channel_id=1, source_target_pairs={{0,2},{1,5},{2,0},{3,7},{4,6},{5,1},{6,4},{7,3},{8,10},{9,13},{10,... | collective-permute-start | bytes 1671176 | tf_op jit(solution)/shard_map/ppermute | solution.py:15
  237.8 18.6 %collective-permute-start.46 = (bf16[128,2048]{1,0:T(8,128)(2,1)S(1)}, bf16[128,2048]{1,0:T(8,128)(2,1)S(1)}, u32[]{:S(2)}, u32[]{:S(2)}) collective-permute-start(bf16[128,2048]{1,0:T(8,128)(2,1)S(1)} %get-tuple-element.261), channel_id=1, source_target_pairs={{0,4},{1,5},{2,6},{3,7},{4,0},{5,1},{6,2},{7,3},{8,12},{9,13},{10,... | collective-permute-start | bytes 1572872 | tf_op jit(solution)/shard_map/ppermute | solution.py:15
  238.8 17.6 %collective-permute-start.45 = (bf16[128,2048]{1,0:T(8,128)(2,1)S(1)}, bf16[128,2048]{1,0:T(8,128)(2,1)S(1)}, u32[]{:S(2)}, u32[]{:S(2)}) collective-permute-start(bf16[128,2048]{1,0:T(8,128)(2,1)S(1)} %get-tuple-element.262), channel_id=1, source_target_pairs={{0,2},{1,3},{2,0},{3,1},{4,6},{5,7},{6,4},{7,5},{8,10},{9,11},{10,... | collective-permute-start | bytes 1572872 | tf_op jit(solution)/shard_map/ppermute | solution.py:15
  262.8 26.3 %collective-permute-start.48 = (bf16[576,1024]{1,0:T(8,128)(2,1)S(1)}, bf16[576,1024]{1,0:T(8,128)(2,1)S(1)}, u32[]{:S(2)}, u32[]{:S(2)}) collective-permute-start(bf16[576,1024]{1,0:T(8,128)(2,1)S(1)} %add_convert_fusion.2), channel_id=1, source_target_pairs={{8,0},{16,24},{9,1},{17,25},{10,2},{18,26},{11,3},{19,27},{12,4},{... | collective-permute-start | bytes 3538952 | tf_op jit(solution)/shard_map/ppermute | solution.py:15
  264.2 29.2 %collective-permute-start.49 = (bf16[576,1024]{1,0:T(8,128)(2,1)S(1)}, bf16[576,1024]{1,0:T(8,128)(2,1)S(1)}, u32[]{:S(2)}, u32[]{:S(2)}) collective-permute-start(bf16[576,1024]{1,0:T(8,128)(2,1)S(1)} %add_convert_fusion.1), channel_id=1, source_target_pairs={{8,16},{16,8},{9,17},{17,9},{10,18},{18,10},{11,19},{19,11},{12,20... | collective-permute-start | bytes 3538952 | tf_op jit(solution)/shard_map/ppermute | solution.py:15
  268.5 17.1 %collective-permute-start.51 = (bf16[128,2176]{1,0:T(8,128)(2,1)S(1)}, bf16[128,2176]{1,0:T(8,128)(2,1)S(1)}, u32[]{:S(2)}, u32[]{:S(2)}) collective-permute-start(bf16[128,2176]{1,0:T(8,128)(2,1)S(1)} %get-tuple-element.257), channel_id=1, source_target_pairs={{0,4},{1,5},{2,6},{3,7},{4,0},{5,1},{6,2},{7,3},{8,12},{9,13},{10,... | collective-permute-start | bytes 1671176 | tf_op jit(solution)/shard_map/ppermute | solution.py:15
  268.8 16.8 %collective-permute-start.50 = (bf16[128,2176]{1,0:T(8,128)(2,1)S(1)}, bf16[128,2176]{1,0:T(8,128)(2,1)S(1)}, u32[]{:S(2)}, u32[]{:S(2)}) collective-permute-start(bf16[128,2176]{1,0:T(8,128)(2,1)S(1)} %get-tuple-element.258), channel_id=1, source_target_pairs={{0,2},{1,3},{2,0},{3,1},{4,6},{5,7},{6,4},{7,5},{8,10},{9,11},{10,... | collective-permute-start | bytes 1671176 | tf_op jit(solution)/shard_map/ppermute | solution.py:15
  271.3 14.3 %collective-permute-start.47 = (bf16[128,2048]{1,0:T(8,128)(2,1)S(1)}, bf16[128,2048]{1,0:T(8,128)(2,1)S(1)}, u32[]{:S(2)}, u32[]{:S(2)}) collective-permute-start(bf16[128,2048]{1,0:T(8,128)(2,1)S(1)} %add_convert_fusion.14), channel_id=1, source_target_pairs={{0,8},{24,16},{1,9},{25,17},{2,10},{26,18},{3,11},{27,19},{4,12},{... | collective-permute-start | bytes 1572872 | tf_op jit(solution)/shard_map/ppermute | solution.py:15
  294.0 14.2 %collective-permute-start.53 = (bf16[128,2048]{1,0:T(8,128)(2,1)S(1)}, bf16[128,2048]{1,0:T(8,128)(2,1)S(1)}, u32[]{:S(2)}, u32[]{:S(2)}) collective-permute-start(bf16[128,2048]{1,0:T(8,128)(2,1)S(1)} %add_convert_fusion.13), channel_id=1, source_target_pairs={{8,16},{16,8},{9,17},{17,9},{10,18},{18,10},{11,19},{19,11},{12,20... | collective-permute-start | bytes 1572872 | tf_op jit(solution)/shard_map/ppermute | solution.py:15
  296.3 30.7 %collective-permute-start.54 = (bf16[576,1024]{1,0:T(8,128)(2,1)S(1)}, bf16[576,1024]{1,0:T(8,128)(2,1)S(1)}, u32[]{:S(2)}, u32[]{:S(2)}) collective-permute-start(bf16[576,1024]{1,0:T(8,128)(2,1)S(1)} %add_convert_fusion), channel_id=1, source_target_pairs={{8,0},{16,24},{9,1},{17,25},{10,2},{18,26},{11,3},{19,27},{12,4},{... | collective-permute-start | bytes 3538952 | tf_op jit(solution)/shard_map/ppermute | solution.py:15
  300.4 21.7 %collective-permute-start.57 = (bf16[2,1152,128]{2,1,0:T(8,128)(2,1)S(1)}, bf16[2,1152,128]{2,1,0:T(8,128)(2,1)S(1)}, u32[]{:S(2)}, u32[]{:S(2)}) collective-permute-start(bf16[2,1152,128]{2,1,0:T(8,128)(2,1)S(1)} %get-tuple-element.271), channel_id=1, source_target_pairs={{0,6},{1,7},{2,4},{3,5},{4,2},{5,3},{6,0},{7,1},{8,14},{9,15},{10,... | collective-permute-start | bytes 1769480 | tf_op jit(solution)/shard_map/ppermute | solution.py:15
  301.3 25.8 %collective-permute-start.56 = (bf16[2,1152,128]{2,1,0:T(8,128)(2,1)S(1)}, bf16[2,1152,128]{2,1,0:T(8,128)(2,1)S(1)}, u32[]{:S(2)}, u32[]{:S(2)}) collective-permute-start(bf16[2,1152,128]{2,1,0:T(8,128)(2,1)S(1)} %get-tuple-element.272), channel_id=1, source_target_pairs={{0,4},{1,5},{2,6},{3,7},{4,0},{5,1},{6,2},{7,3},{8,12},{9,13},{10,... | collective-permute-start | bytes 1769480 | tf_op jit(solution)/shard_map/ppermute | solution.py:15
  302.4 24.7 %collective-permute-start.55 = (bf16[2,1152,128]{2,1,0:T(8,128)(2,1)S(1)}, bf16[2,1152,128]{2,1,0:T(8,128)(2,1)S(1)}, u32[]{:S(2)}, u32[]{:S(2)}) collective-permute-start(bf16[2,1152,128]{2,1,0:T(8,128)(2,1)S(1)} %get-tuple-element.273), channel_id=1, source_target_pairs={{0,2},{1,3},{2,0},{3,1},{4,6},{5,7},{6,4},{7,5},{8,10},{9,11},{10,... | collective-permute-start | bytes 1769480 | tf_op jit(solution)/shard_map/ppermute | solution.py:15
  308.2 14.0 %collective-permute-start.52 = (bf16[128,2176]{1,0:T(8,128)(2,1)S(1)}, bf16[128,2176]{1,0:T(8,128)(2,1)S(1)}, u32[]{:S(2)}, u32[]{:S(2)}) collective-permute-start(bf16[128,2176]{1,0:T(8,128)(2,1)S(1)} %add_convert_fusion.8), channel_id=1, source_target_pairs={{0,8},{24,16},{1,9},{25,17},{2,10},{26,18},{3,11},{27,19},{4,12},{... | collective-permute-start | bytes 1671176 | tf_op jit(solution)/shard_map/ppermute | solution.py:15
  328.5 21.7 %collective-permute-start.59 = (bf16[128,2048]{1,0:T(8,128)(2,1)}, bf16[128,2048]{1,0:T(8,128)(2,1)}, u32[]{:S(2)}, u32[]{:S(2)}) collective-permute-start(bf16[128,2048]{1,0:T(8,128)(2,1)} %add_convert_fusion.12), channel_id=1, source_target_pairs={{8,0},{16,24},{9,1},{17,25},{10,2},{18,26},{11,3},{19,27},{12,4},{... | collective-permute-start | bytes 1572872 | tf_op jit(solution)/shard_map/ppermute | solution.py:15
  331.5 18.7 %collective-permute-start.58 = (bf16[128,2176]{1,0:T(8,128)(2,1)}, bf16[128,2176]{1,0:T(8,128)(2,1)}, u32[]{:S(2)}, u32[]{:S(2)}) collective-permute-start(bf16[128,2176]{1,0:T(8,128)(2,1)} %add_convert_fusion.7), channel_id=1, source_target_pairs={{8,16},{16,8},{9,17},{17,9},{10,18},{18,10},{11,19},{19,11},{12,20... | collective-permute-start | bytes 1671176 | tf_op jit(solution)/shard_map/ppermute | solution.py:15
  353.5 19.3 %collective-permute-start.63 = (bf16[128,2176]{1,0:T(8,128)(2,1)S(1)}, bf16[128,2176]{1,0:T(8,128)(2,1)S(1)}, u32[]{:S(2)}, u32[]{:S(2)}) collective-permute-start(bf16[128,2176]{1,0:T(8,128)(2,1)S(1)} %add_convert_fusion.6), channel_id=1, source_target_pairs={{8,0},{16,24},{9,1},{17,25},{10,2},{18,26},{11,3},{19,27},{12,4},{... | collective-permute-start | bytes 1671176 | tf_op jit(solution)/shard_map/ppermute | solution.py:15
  356.7 13.3 %collective-permute-start.64 = (bf16[256,1024]{1,0:T(8,128)(2,1)S(1)}, bf16[256,1024]{1,0:T(8,128)(2,1)S(1)}, u32[]{:S(2)}, u32[]{:S(2)}) collective-permute-start(bf16[256,1024]{1,0:T(8,128)(2,1)S(1)} %get-tuple-element.259), channel_id=1, source_target_pairs={{0,2},{1,3},{2,0},{3,1},{4,6},{5,7},{6,4},{7,5},{8,10},{9,11},{10,... | collective-permute-start | bytes 1572872 | tf_op jit(solution)/shard_map/ppermute | solution.py:15
  357.6 12.9 %collective-permute-start.65 = (bf16[256,1024]{1,0:T(8,128)(2,1)S(1)}, bf16[256,1024]{1,0:T(8,128)(2,1)S(1)}, u32[]{:S(2)}, u32[]{:S(2)}) collective-permute-start(bf16[256,1024]{1,0:T(8,128)(2,1)S(1)} %get-tuple-element.260), channel_id=1, source_target_pairs={{0,4},{1,5},{2,6},{3,7},{4,0},{5,1},{6,2},{7,3},{8,12},{9,13},{10,... | collective-permute-start | bytes 1572872 | tf_op jit(solution)/shard_map/ppermute | solution.py:15
  (73 other events, 419.1 us)

commit v4 on v3

--- a/solution.py
+++ b/solution.py
@@ -92,15 +92,21 @@
     return block_sum(mine, near, 0) + last[0].astype(f32) + last[1].astype(f32)
 
 
-def exchange_early(blocks):
-    if not is_cube():
-        return [lax.all_to_all(blocks, "fsdp", 0, 0)]
-    chip, odd = lax.axis_index("fsdp") >> 1, on_odd_core()
+def exchange_early_cores(blocks):
+    if not is_cube():
+        return blocks
+    odd = on_odd_core()
     pairs = blocks.reshape((4, 2) + blocks.shape[1:])
     to_even, to_odd = pairs[:, 0], pairs[:, 1]
     kept = jnp.where(odd, to_odd, to_even)
     came = flip(jnp.where(odd, to_even, to_odd), 1)
-    both = jnp.stack([jnp.where(odd, came, kept), jnp.where(odd, kept, came)], axis=1)
+    return jnp.stack([jnp.where(odd, came, kept), jnp.where(odd, kept, came)], axis=1)
+
+
+def exchange_early_chips(both):
+    if not is_cube():
+        return [lax.all_to_all(both, "fsdp", 0, 0)]
+    chip = lax.axis_index("fsdp") >> 1
     return [both] + [
         flip(lax.dynamic_index_in_dim(both, chip ^ k, 0, keepdims=False), 2 * k)
         for k in (1, 2, 3)
@@ -317,16 +323,23 @@
         gate_up = jnp.where(one_way, gate_up[0], gate_up[1])
     else:
         gate_up = jnp.concatenate(gate_up, axis=1)
-    gate_up = exchange_early(gate_up)
-    full_in = gather(w_in).reshape(width, 3 * width)
+    grad_out = cotangent.reshape(all_rows, width)
+    gate_up = exchange_early_cores(gate_up)
+    in_x, in_y, w_out = together(*gather_sides(w_in), w_out)
+    in_parts = gather_rest(w_in, in_x, in_y)
+    out_x, out_y, in_parts[-1], gate_up = together(
+        *gather_sides(w_out), in_parts[-1], gate_up
+    )
+    out_parts = gather_rest(w_out, out_x, out_y)
+    grad_out_now, *gate_up = together(grad_out, *exchange_early_chips(gate_up))
+    full_in = jnp.concatenate(in_parts, axis=0).reshape(width, 3 * width)
     smalls = jnp.concatenate([norm_in[None], norm_mid[None], taps], axis=0)
     smalls = jnp.pad(smalls, ((0, 8 - (reach + 3)), (0, 0)))
     smalls = jnp.transpose(gather(smalls)[:, : reach + 3], (1, 0, 2))
     smalls = relabel(smalls.reshape(reach + 3, width), back=True).astype(f32)
     gain_in, gain_mid, tap_values = smalls[0], smalls[1], smalls[2:]
-    full_out = gather(w_out).reshape(width, width)
-    grad_out = cotangent.reshape(all_rows, width)
-    grad_out_all = gather(grad_out).reshape(peers * all_rows, width)
+    full_out = jnp.concatenate(out_parts, axis=0).reshape(width, width)
+    grad_out_x, grad_out_y = gather_sides(grad_out_now)
     gate_up = jnp.transpose(exchanged_early(gate_up), (1, 0, 2)).reshape(-1, width)
     if groups % 2 == 0:
         other = along(gate_up, "dp", [(i, i ^ 1) for i in range(groups)])
@@ -354,7 +367,10 @@
     scale_mid = inverse_rms(middle)
     normed_mid = (middle * scale_mid * gain_mid).astype(bf16)
 
+    normed_mid, grad_out_x, grad_out_y = together(normed_mid, grad_out_x, grad_out_y)
     normed_all = gather(normed_mid).reshape(peers * all_rows, width)
+    grad_out_all = jnp.concatenate(gather_rest(grad_out_now, grad_out_x, grad_out_y), axis=0)
+    grad_out_all = grad_out_all.reshape(peers * all_rows, width)
     activ, grad_gate, grad_up, theirs, ours, final_theirs, final_ours = feed_forward(
         normed_all, grad_out_all, own_gate, own_up, w_down
     )
@@ -400,7 +416,6 @@
 
     half = width // 2
     normed_theirs, normed_ours = normed_in[:, :half], normed_in[:, half:]
-    grad_b_v = jnp.concatenate([grad_proj[0], grad_proj[2]], axis=1)
     terms_out_c = [
         jnp.concatenate(
             [over_tokens(p, grad_branch).astype(bf16), over_tokens(q, grad_proj[1]).astype(bf16)],
@@ -408,6 +423,10 @@
         )
         for p, q in ((gated[:, :half], normed_theirs), (gated[:, half:], normed_ours))
     ]
+    near_out_c = scatter_near(*terms_out_c)
+    near_out_c, grad_proj[0], grad_proj[2] = together(near_out_c, grad_proj[0], grad_proj[2])
+    across_out_c = scatter_across(terms_out_c[1], near_out_c)
+    grad_b_v = jnp.concatenate([grad_proj[0], grad_proj[2]], axis=1)
     terms_b_v = [over_tokens(p, grad_b_v).astype(bf16) for p in (normed_theirs, normed_ours)]
     grad_normed_in = relabel(
         against_rows(jnp.concatenate(grad_proj, axis=1), full_in), back=True
@@ -420,10 +439,9 @@
         jnp.concatenate([terms_b_v[0], smalls[:half]], axis=1),
         jnp.concatenate([terms_b_v[1], smalls[half:]], axis=1),
     ]
-    near_out_c = scatter_near(*terms_out_c)
-    across_out_c = scatter_across(terms_out_c[1], near_out_c)
-    across_out_c, terms_b_v[0], far_gate, came_up, term_down = together(
-        across_out_c, terms_b_v[0], far_gate, came_up, term_down
+    near_final = scatter_near(final_theirs, final_ours)
+    across_out_c, *terms_b_v, far_gate, came_up, term_down, near_final = together(
+        across_out_c, *terms_b_v, far_gate, came_up, term_down, near_final
     )
 
     total_gate = add_pair(pair_gate, far_gate)
@@ -444,9 +462,10 @@
     total_up = add_pair(pair_up, far_up)
     out_up = outward(total_up)
     last_b_v = scatter_last(terms_b_v[1], near_b_v, across_b_v)
-
-    came_out_c, out_up, far_down, final_theirs, *last_b_v = together(
-        came_out_c, out_up, far_down, final_theirs, *last_b_v
+    across_final = scatter_across(final_ours, near_final)
+
+    came_out_c, out_up, far_down, across_final, *last_b_v = together(
+        came_out_c, out_up, far_down, across_final, *last_b_v
     )
     rows_b_v = scattered(terms_b_v[1], near_b_v, last_b_v).astype(bf16)
     came_b_v = inward(rows_b_v)
@@ -464,15 +483,14 @@
         )
     )
 
-    came_b_v, far_out_c, out_down, final_theirs, *mine = together(
-        came_b_v, far_out_c, out_down, final_theirs, *mine
+    came_b_v, far_out_c, out_down, across_final, *mine = together(
+        came_b_v, far_out_c, out_down, across_final, *mine
     )
     pair_b_v = add_pair(rows_b_v, came_b_v)
     far_b_v = between(pair_b_v)
     total_out_c = add_pair(pair_out_c, far_out_c)
     out_out_c = outward(total_out_c)
-    near_final = scatter_near(final_theirs, final_ours)
-    across_final = scatter_across(final_ours, near_final)
+    last_final = scatter_last(final_ours, near_final, across_final)
     grad_w_down = settle(total_down, out_down).astype(f32)
     mine = exchange_cores(mine)
     by_rows = Layout(major_to_minor=(0, 1))
@@ -483,13 +501,12 @@
         for part in (mine[:, :hidden], mine[:, hidden:])
     ]
 
-    far_b_v, out_out_c, across_final, grad_w_down, grad_w_gate, grad_w_up = together(
-        far_b_v, out_out_c, across_final, grad_w_down, grad_w_gate, grad_w_up
+    far_b_v, out_out_c, last_x, last_y, grad_w_down, grad_w_gate, grad_w_up = together(
+        far_b_v, out_out_c, *last_final, grad_w_down, grad_w_gate, grad_w_up
     )
     total_b_v = add_pair(pair_b_v, far_b_v)
     out_b_v = outward(total_b_v)
-    last_final = scatter_last(final_ours, near_final, across_final)
-    final = scattered(final_ours, near_final, last_final)
+    final = scattered(final_ours, near_final, (last_x, last_y))
     block_out = (middle + final).astype(bf16).reshape(micros, rows_held, width)
     out_b_v, block_out = together(out_b_v, block_out)
     total_out_c = settle(total_out_c, out_out_c).astype(f32)

time: 383 us -> 368 us (0.961)
  the two profiles are of different devices: /device:TPU:8 before, /device:TPU:0 now
where the time goes in v4:
time: 368 us; the launch traced here: 362 us
  waiting for transfers between devices  144 us (39%)
  starting transfers between devices  86.6 us (24%)
  other arithmetic  61 us (17%)
  Pallas kernels  24.4 us (7%)
  matrix products  21.6 us (6%)
  local copies, waits for them, and re-layouts  21.2 us (6%)
    ppermute x64, waiting for transfers between devices, along(): return lax.ppermute(shard, axis, pairs)  143 us
    ppermute x64, starting transfers between devices, along(): return lax.ppermute(shard, axis, pairs)  83.3 us
    pallas_call x1, Pallas kernels, feed_forward(): pl.pallas_call(feed_forward_kernel, grid=(steps,), in_specs=[rows, rows,...  24.4 us
    dot_general x5, matrix products, times(): return jnp.dot(left, right, preferred_element_type=f32)  15.7 us
    unnamed x139, local copies, waits for them, and re-layouts  10.8 us
    unnamed x44, other arithmetic  10.1 us
    convert_element_type x9, other arithmetic, add_pair(): (one.astype(f32) + other.astype(f32)).astype(bf16)  8.33 us
  transfers between devices with their start and end apart: 66, of which 30 were waited for; matrix products, arithmetic and copies ran while one was open for 24% of the time, Pallas kernels for 0%

profile of v4, /device:TPU:0, one launch (start us, length us, event | category | flops | bytes accessed | tf_op | source)
XLA Modules:
  0.0 361.9 jit_solution(8859700385568487213)
XLA Ops:
  1.5 3.0 collective-permute-start
  6.6 2.4 copy.72
  13.0 2.0 collective-permute-start.3
  15.8 9.2 %collective-permute-done.3 = bf16[8,128]{1,0:T(8,128)(2,1)S(1)} collective-permute-done((bf16[8,128]{1,0:T(8,128)(2,1)S(1)}, bf16[8,128]{1,0:T(8,128)(2,1)S(1)}, u32[]{:S(2)}, u32[]{:S(2)}) %collective-permute-start.3) | collective-permute-done | bytes 2080 | tf_op jit(solution)/shard_map/ppermute | solution.py:15
  35.1 13.3 %collective-permute-done.11 = bf16[128,1024]{1,0:T(8,128)(2,1)S(1)} collective-permute-done((bf16[128,1024]{1,0:T(8,128)(2,1)S(1)}, bf16[128,1024]{1,0:T(8,128)(2,1)S(1)}, u32[]{:S(2)}, u32[]{:S(2)}) %collective-permute-start.11) | collective-permute-done | bytes 262176 | tf_op jit(solution)/shard_map/ppermute | solution.py:15
  51.4 11.3 %collective-permute-done.15 = bf16[128,1024]{1,0:T(8,128)(2,1)S(1)} collective-permute-done((bf16[128,1024]{1,0:T(8,128)(2,1)S(1)}, bf16[128,1024]{1,0:T(8,128)(2,1)S(1)}, u32[]{:S(2)}, u32[]{:S(2)}) %collective-permute-start.15) | collective-permute-done | bytes 262176 | tf_op jit(solution)/shard_map/ppermute | solution.py:15
  64.7 2.9 collective-permute-done.18
  67.6 1.8 collective-permute-done.17
  71.0 1.8 fusion.70
  73.7 1.8 collective-permute-start.13
  78.1 3.9 %collective-permute-done.21 = bf16[256,1024]{1,0:T(8,128)(2,1)S(1)} collective-permute-done((bf16[256,1024]{1,0:T(8,128)(2,1)S(1)}, bf16[256,1024]{1,0:T(8,128)(2,1)S(1)}, u32[]{:S(2)}, u32[]{:S(2)}) %collective-permute-start.21) | collective-permute-done | bytes 524320 | tf_op jit(solution)/shard_map/ppermute | solution.py:15
  83.2 1.6 collective-permute-start.30
  87.8 11.1 %collective-permute-done.23 = bf16[256,1024]{1,0:T(8,128)(2,1)S(1)} collective-permute-done((bf16[256,1024]{1,0:T(8,128)(2,1)S(1)}, bf16[256,1024]{1,0:T(8,128)(2,1)S(1)}, u32[]{:S(2)}, u32[]{:S(2)}) %collective-permute-start.23) | collective-permute-done | bytes 524320 | tf_op jit(solution)/shard_map/ppermute | solution.py:15
  98.9 2.2 collective-permute-done.22
  101.8 2.7 collective-permute-done.28
  106.0 5.6 %collective-permute-done.30 = bf16[576,1024]{1,0:T(8,128)(2,1)S(1)} collective-permute-done((bf16[576,1024]{1,0:T(8,128)(2,1)S(1)}, bf16[576,1024]{1,0:T(8,128)(2,1)S(1)}, u32[]{:S(2)}, u32[]{:S(2)}) %collective-permute-start.30) | collective-permute-done | bytes 1179680 | tf_op jit(solution)/shard_map/ppermute | solution.py:15
  114.3 1.8 copy-done.23
  116.1 24.4 %shard_map.177 = (bf16[576,2048]{1,0:T(8,128)(2,1)}, bf16[576,2048]{1,0:T(8,128)(2,1)}, bf16[576,2048]{1,0:T(8,128)(2,1)}, bf16[1024,1024]{1,0:T(8,128)(2,1)S(1)...) custom-call(bf16[2048,1024]{1,0:T(8,128)(2,1)} %bitcast.278, ...), custom_call_target="tpu_custom_call" | custom-call | flops 14495514624 | bytes 27394048 | tf_op jit(solution)/shard_map/pallas_call | solution.py:295
  140.5 5.6 %convolution_convert_fusion.4 = bf16[576,1024]{1,0:T(8,128)(2,1)S(1)} fusion(bf16[576,2048]{1,0:T(8,128)(2,1)} %get-tuple-element.98, bf16[2048,1024]{1,0:T(8,128)(2,1)} %bitcast.279), kind=kOutput, calls=%fused_computation.32 | convolution fusion | flops 2416508928 | bytes 7733248 | tf_op jit(solution)/shard_map/dot_general | solution.py:229
  146.2 3.8 %collective-permute-start.35 = (bf16[576,1024]{1,0:T(8,128)(2,1)S(1)}, bf16[576,1024]{1,0:T(8,128)(2,1)S(1)}, u32[]{:S(2)}, u32[]{:S(2)}) collective-permute-start(bf16[576,1024]{1,0:T(8,128)(2,1)S(1)} %convolution_convert_fusion.4), channel_id=1, source_target_pairs={{0,8},{24,16},{1,9},{25,17},{2,10},{26,18},{3,11},{27,19},{4,12},{... | collective-permute-start | bytes 3538952 | tf_op jit(solution)/shard_map/ppermute | solution.py:15
  151.1 3.7 %convolution_convert_fusion.2 = bf16[576,1024]{1,0:T(8,128)(2,1)} fusion(bf16[576,2048]{1,0:T(8,128)(2,1)S(1)} %copy-done.49, bf16[2048,1024]{1,0:T(8,128)(2,1)S(1)} %bitcast.277), kind=kOutput, calls=%fused_computation.30 | convolution fusion | flops 2416508928 | bytes 7733248 | tf_op jit(solution)/shard_map/dot_general | solution.py:229
  154.8 4.6 %collective-permute-done.32 = bf16[256,1024]{1,0:T(8,128)(2,1)S(1)} collective-permute-done((bf16[256,1024]{1,0:T(8,128)(2,1)S(1)}, bf16[256,1024]{1,0:T(8,128)(2,1)S(1)}, u32[]{:S(2)}, u32[]{:S(2)}) %collective-permute-start.32) | collective-permute-done | bytes 524320 | tf_op jit(solution)/shard_map/ppermute | solution.py:15
  162.1 3.7 %convolution_convert_fusion.3 = bf16[576,1024]{1,0:T(8,128)(2,1)} fusion(bf16[576,2048]{1,0:T(8,128)(2,1)S(1)} %copy-done.48, bf16[2048,1024]{1,0:T(8,128)(2,1)S(1)} %bitcast.280), kind=kOutput, calls=%fused_computation.31 | convolution fusion | flops 2416508928 | bytes 7733248 | tf_op jit(solution)/shard_map/dot_general | solution.py:229
  165.8 7.3 %collective-permute-done.33 = bf16[256,1024]{1,0:T(8,128)(2,1)S(1)} collective-permute-done((bf16[256,1024]{1,0:T(8,128)(2,1)S(1)}, bf16[256,1024]{1,0:T(8,128)(2,1)S(1)}, u32[]{:S(2)}, u32[]{:S(2)}) %collective-permute-start.33) | collective-permute-done | bytes 524320 | tf_op jit(solution)/shard_map/ppermute | solution.py:15
  181.9 1.7 collective-permute-start.39
  183.6 7.3 %collective-permute-start.40 = (bf16[576,1024]{1,0:T(8,128)(2,1)}, bf16[576,1024]{1,0:T(8,128)(2,1)}, u32[]{:S(2)}, u32[]{:S(2)}) collective-permute-start(bf16[576,1024]{1,0:T(8,128)(2,1)} %convolution_convert_fusion.3), channel_id=1, source_target_pairs={{0,8},{24,16},{1,9},{25,17},{2,10},{26,18},{3,11},{27,19},{4,12},{... | collective-permute-start | bytes 3538952 | tf_op jit(solution)/shard_map/ppermute | solution.py:15
  197.3 1.8 fusion
  210.5 2.5 pad_maximum_fusion.3
  213.0 2.2 collective-permute-done.40
  215.2 2.9 broadcast_select_fusion.1
  218.1 2.2 collective-permute-start.43
  220.3 2.1 add_convert_fusion.3
  230.7 16.2 %collective-permute-done.43 = bf16[576,1024]{1,0:T(8,128)(2,1)S(1)} collective-permute-done((bf16[576,1024]{1,0:T(8,128)(2,1)S(1)}, bf16[576,1024]{1,0:T(8,128)(2,1)S(1)}, u32[]{:S(2)}, u32[]{:S(2)}) %collective-permute-start.43) | collective-permute-done | bytes 1179680 | tf_op jit(solution)/shard_map/ppermute | solution.py:15
  251.2 1.7 fusion.11
  256.1 7.7 %collective-permute-start.48 = (bf16[128,2048]{1,0:T(8,128)(2,1)S(1)}, bf16[128,2048]{1,0:T(8,128)(2,1)S(1)}, u32[]{:S(2)}, u32[]{:S(2)}) collective-permute-start(bf16[128,2048]{1,0:T(8,128)(2,1)S(1)} %add_convert_fusion.14), channel_id=1, source_target_pairs={{0,8},{24,16},{1,9},{25,17},{2,10},{26,18},{3,11},{27,19},{4,12},{... | collective-permute-start | bytes 1572872 | tf_op jit(solution)/shard_map/ppermute | solution.py:15
  263.8 2.1 bitcast_bitcast_fusion.1
  265.9 8.1 %collective-permute-done.48 = bf16[128,2048]{1,0:T(8,128)(2,1)S(1)} collective-permute-done((bf16[128,2048]{1,0:T(8,128)(2,1)S(1)}, bf16[128,2048]{1,0:T(8,128)(2,1)S(1)}, u32[]{:S(2)}, u32[]{:S(2)}) %collective-permute-start.48) | collective-permute-done | bytes 524320 | tf_op jit(solution)/shard_map/ppermute | solution.py:15
  274.0 6.9 %collective-permute-done.49 = bf16[576,1024]{1,0:T(8,128)(2,1)S(1)} collective-permute-done((bf16[576,1024]{1,0:T(8,128)(2,1)S(1)}, bf16[576,1024]{1,0:T(8,128)(2,1)S(1)}, u32[]{:S(2)}, u32[]{:S(2)}) %collective-permute-start.49) | collective-permute-done | bytes 1179680 | tf_op jit(solution)/shard_map/ppermute | solution.py:15
  289.1 13.0 %collective-permute-start.54 = (bf16[128,2176]{1,0:T(8,128)(2,1)S(1)}, bf16[128,2176]{1,0:T(8,128)(2,1)S(1)}, u32[]{:S(2)}, u32[]{:S(2)}) collective-permute-start(bf16[128,2176]{1,0:T(8,128)(2,1)S(1)} %add_convert_fusion.8), channel_id=1, source_target_pairs={{0,8},{24,16},{1,9},{25,17},{2,10},{26,18},{3,11},{27,19},{4,12},{... | collective-permute-start | bytes 1671176 | tf_op jit(solution)/shard_map/ppermute | solution.py:15
  303.4 8.6 %collective-permute-done.54 = bf16[128,2176]{1,0:T(8,128)(2,1)S(1)} collective-permute-done((bf16[128,2176]{1,0:T(8,128)(2,1)S(1)}, bf16[128,2176]{1,0:T(8,128)(2,1)S(1)}, u32[]{:S(2)}, u32[]{:S(2)}) %collective-permute-start.54) | collective-permute-done | bytes 557088 | tf_op jit(solution)/shard_map/ppermute | solution.py:15
  312.2 1.7 collective-permute-done.56
  319.0 2.7 fusion.23
  326.3 1.6 bitcast_convert_fusion.1
  327.9 1.9 copy.88
  329.9 3.0 copy.87
  332.9 3.4 collective-permute-done.63
  342.2 2.7 add_convert_fusion.10
  344.9 13.6 %collective-permute-done.65 = bf16[128,2176]{1,0:T(8,128)(2,1)S(1)} collective-permute-done((bf16[128,2176]{1,0:T(8,128)(2,1)S(1)}, bf16[128,2176]{1,0:T(8,128)(2,1)S(1)}, u32[]{:S(2)}, u32[]{:S(2)}) %collective-permute-start.65) | collective-permute-done | bytes 557088 | tf_op jit(solution)/shard_map/ppermute | solution.py:15
  (393 shorter events, 109.9 us)
Async XLA Ops:
  1.5 11.5 %collective-permute-start = (bf16[8,128]{1,0:T(8,128)(2,1)S(1)}, bf16[8,128]{1,0:T(8,128)(2,1)S(1)}, u32[]{:S(2)}, u32[]{:S(2)}) collective-permute-start(bf16[8,128]{1,0:T(8,128)(2,1)S(1)} %fusion.53), channel_id=1, source_target_pairs={{0,2},{1,3},{2,0},{3,1},{4,6},{5,7},{6,4},{7,5},{8,10},{9,11},{10,... | collective-permute-start | bytes 6152 | tf_op jit(solution)/shard_map/ppermute | solution.py:15
  6.0 24.7 %collective-permute-start.6 = (bf16[128,3072]{1,0:T(8,128)(2,1)}, bf16[128,3072]{1,0:T(8,128)(2,1)S(1)}, u32[]{:S(2)}, u32[]{:S(2)}) collective-permute-start(bf16[128,3072]{1,0:T(8,128)(2,1)} %param.12), channel_id=1, source_target_pairs={{0,4},{1,5},{2,6},{3,7},{4,0},{5,1},{6,2},{7,3},{8,12},{9,13},{10,... | collective-permute-start | bytes 2359304 | tf_op jit(solution)/shard_map/ppermute | solution.py:15
  6.5 24.2 %collective-permute-start.5 = (bf16[128,3072]{1,0:T(8,128)(2,1)}, bf16[128,3072]{1,0:T(8,128)(2,1)S(1)}, u32[]{:S(2)}, u32[]{:S(2)}) collective-permute-start(bf16[128,3072]{1,0:T(8,128)(2,1)} %param.12), channel_id=1, source_target_pairs={{0,2},{1,3},{2,0},{3,1},{4,6},{5,7},{6,4},{7,5},{8,10},{9,11},{10,... | collective-permute-start | bytes 2359304 | tf_op jit(solution)/shard_map/ppermute | solution.py:15
  12.7 18.7 %collective-permute-start.12 = (bf16[4,576,128]{2,1,0:T(8,128)(2,1)}, bf16[4,576,128]{2,1,0:T(8,128)(2,1)}, u32[]{:S(2)}, u32[]{:S(2)}) collective-permute-start(bf16[4,576,128]{2,1,0:T(8,128)(2,1)} %select_bitcast_fusion.4), channel_id=1, source_target_pairs={{0,1},{1,0},{2,3},{3,2},{4,5},{5,4},{6,7},{7,6},{8,9},{9,8},{10,11... | collective-permute-start | bytes 1769480 | tf_op jit(solution)/shard_map/ppermute | solution.py:15
  13.0 12.0 %collective-permute-start.3 = (bf16[8,128]{1,0:T(8,128)(2,1)S(1)}, bf16[8,128]{1,0:T(8,128)(2,1)S(1)}, u32[]{:S(2)}, u32[]{:S(2)}) collective-permute-start(bf16[8,128]{1,0:T(8,128)(2,1)S(1)} %broadcast_select_fusion.82), channel_id=1, source_target_pairs={{0,4},{1,3},{2,6},{3,1},{4,0},{5,7},{6,2},{7,5},{8,12},{9,11},{10,... | collective-permute-start | bytes 6152 | tf_op jit(solution)/shard_map/ppermute | solution.py:15
  30.8 17.7 %collective-permute-start.8 = (bf16[128,3072]{1,0:T(8,128)(2,1)S(1)}, bf16[128,3072]{1,0:T(8,128)(2,1)S(1)}, u32[]{:S(2)}, u32[]{:S(2)}) collective-permute-start(bf16[128,3072]{1,0:T(8,128)(2,1)S(1)} %broadcast_select_fusion.5), channel_id=1, source_target_pairs={{0,4},{1,3},{2,6},{3,1},{4,0},{5,7},{6,2},{7,5},{8,12},{9,11},{10,... | collective-permute-start | bytes 2359304 | tf_op jit(solution)/shard_map/ppermute | solution.py:15
  32.7 15.8 %collective-permute-start.11 = (bf16[128,1024]{1,0:T(8,128)(2,1)S(1)}, bf16[128,1024]{1,0:T(8,128)(2,1)S(1)}, u32[]{:S(2)}, u32[]{:S(2)}) collective-permute-start(bf16[128,1024]{1,0:T(8,128)(2,1)S(1)} %copy-done.19), channel_id=1, source_target_pairs={{0,4},{1,5},{2,6},{3,7},{4,0},{5,1},{6,2},{7,3},{8,12},{9,13},{10,... | collective-permute-start | bytes 786440 | tf_op jit(solution)/shard_map/ppermute | solution.py:15
  34.3 14.2 %collective-permute-start.10 = (bf16[128,1024]{1,0:T(8,128)(2,1)S(1)}, bf16[128,1024]{1,0:T(8,128)(2,1)S(1)}, u32[]{:S(2)}, u32[]{:S(2)}) collective-permute-start(bf16[128,1024]{1,0:T(8,128)(2,1)S(1)} %copy-done.19), channel_id=1, source_target_pairs={{0,2},{1,3},{2,0},{3,1},{4,6},{5,7},{6,4},{7,5},{8,10},{9,11},{10,... | collective-permute-start | bytes 786440 | tf_op jit(solution)/shard_map/ppermute | solution.py:15
  35.1 35.4 %collective-permute-start.7 = (bf16[3,128,3072]{2,1,0:T(8,128)(2,1)S(1)}, bf16[3,128,3072]{2,1,0:T(8,128)(2,1)S(1)}, u32[]{:S(2)}, u32[]{:S(2)}) collective-permute-start(bf16[3,128,3072]{2,1,0:T(8,128)(2,1)S(1)} %pad_maximum_fusion), channel_id=1, source_target_pairs={{0,1},{1,0},{2,3},{3,2},{4,5},{5,4},{6,7},{7,6},{8,9},{9,8},{10,11... | collective-permute-start | bytes 7077896 | tf_op jit(solution)/shard_map/ppermute | solution.py:15
  48.5 14.1 %collective-permute-start.15 = (bf16[128,1024]{1,0:T(8,128)(2,1)S(1)}, bf16[128,1024]{1,0:T(8,128)(2,1)S(1)}, u32[]{:S(2)}, u32[]{:S(2)}) collective-permute-start(bf16[128,1024]{1,0:T(8,128)(2,1)S(1)} %broadcast_select_fusion.9), channel_id=1, source_target_pairs={{0,4},{1,3},{2,6},{3,1},{4,0},{5,7},{6,2},{7,5},{8,12},{9,11},{10,... | collective-permute-start | bytes 786440 | tf_op jit(solution)/shard_map/ppermute | solution.py:15
  49.2 20.8 %collective-permute-start.14 = (bf16[3,128,1024]{2,1,0:T(8,128)(2,1)S(1)}, bf16[3,128,1024]{2,1,0:T(8,128)(2,1)S(1)}, u32[]{:S(2)}, u32[]{:S(2)}) collective-permute-start(bf16[3,128,1024]{2,1,0:T(8,128)(2,1)S(1)} %pad_maximum_fusion.10), channel_id=1, source_target_pairs={{0,1},{1,0},{2,3},{3,2},{4,5},{5,4},{6,7},{7,6},{8,9},{9,8},{10,11... | collective-permute-start | bytes 2359304 | tf_op jit(solution)/shard_map/ppermute | solution.py:15
  49.4 15.4 %collective-permute-start.19 = (bf16[2,576,128]{2,1,0:T(8,128)(2,1)S(1)}, bf16[2,576,128]{2,1,0:T(8,128)(2,1)S(1)}, u32[]{:S(2)}, u32[]{:S(2)}) collective-permute-start(bf16[2,576,128]{2,1,0:T(8,128)(2,1)S(1)} %get-tuple-element.320), channel_id=1, source_target_pairs={{0,6},{1,7},{2,4},{3,5},{4,2},{5,3},{6,0},{7,1},{8,14},{9,15},{10,... | collective-permute-start | bytes 884744 | tf_op jit(solution)/shard_map/ppermute | solution.py:15
  50.9 16.7 %collective-permute-start.18 = (bf16[2,576,128]{2,1,0:T(8,128)(2,1)S(1)}, bf16[2,576,128]{2,1,0:T(8,128)(2,1)S(1)}, u32[]{:S(2)}, u32[]{:S(2)}) collective-permute-start(bf16[2,576,128]{2,1,0:T(8,128)(2,1)S(1)} %get-tuple-element.321), channel_id=1, source_target_pairs={{0,4},{1,5},{2,6},{3,7},{4,0},{5,1},{6,2},{7,3},{8,12},{9,13},{10,... | collective-permute-start | bytes 884744 | tf_op jit(solution)/shard_map/ppermute | solution.py:15
  69.4 12.6 %collective-permute-start.21 = (bf16[256,1024]{1,0:T(8,128)(2,1)S(1)}, bf16[256,1024]{1,0:T(8,128)(2,1)S(1)}, u32[]{:S(2)}, u32[]{:S(2)}) collective-permute-start(bf16[256,1024]{1,0:T(8,128)(2,1)S(1)} %bitcast.253), channel_id=1, source_target_pairs={{0,4},{1,5},{2,6},{3,7},{4,0},{5,1},{6,2},{7,3},{8,12},{9,13},{10,... | collective-permute-start | bytes 1572872 | tf_op jit(solution)/shard_map/ppermute | solution.py:15
  70.0 12.5 %collective-permute-start.20 = (bf16[256,1024]{1,0:T(8,128)(2,1)S(1)}, bf16[256,1024]{1,0:T(8,128)(2,1)S(1)}, u32[]{:S(2)}, u32[]{:S(2)}) collective-permute-start(bf16[256,1024]{1,0:T(8,128)(2,1)S(1)} %bitcast.254), channel_id=1, source_target_pairs={{0,2},{1,3},{2,0},{3,1},{4,6},{5,7},{6,4},{7,5},{8,10},{9,11},{10,... | collective-permute-start | bytes 1572872 | tf_op jit(solution)/shard_map/ppermute | solution.py:15
  82.6 29.3 %collective-permute-start.27 = (bf16[3,256,1024]{2,1,0:T(8,128)(2,1)S(1)}, bf16[3,256,1024]{2,1,0:T(8,128)(2,1)S(1)}, u32[]{:S(2)}, u32[]{:S(2)}) collective-permute-start(bf16[3,256,1024]{2,1,0:T(8,128)(2,1)S(1)} %pad_maximum_fusion.7), channel_id=1, source_target_pairs={{0,1},{1,0},{2,3},{3,2},{4,5},{5,4},{6,7},{7,6},{8,9},{9,8},{10,11... | collective-permute-start | bytes 4718600 | tf_op jit(solution)/shard_map/ppermute | solution.py:15
  83.2 28.4 %collective-permute-start.30 = (bf16[576,1024]{1,0:T(8,128)(2,1)S(1)}, bf16[576,1024]{1,0:T(8,128)(2,1)S(1)}, u32[]{:S(2)}, u32[]{:S(2)}) collective-permute-start(bf16[576,1024]{1,0:T(8,128)(2,1)S(1)} %bitcast.267), channel_id=1, source_target_pairs={{0,8},{8,0},{16,24},{24,16},{1,9},{9,1},{17,25},{25,17},{2,10},{10... | collective-permute-start | bytes 3538952 | tf_op jit(solution)/shard_map/ppermute | solution.py:15
  84.8 14.0 %collective-permute-start.23 = (bf16[256,1024]{1,0:T(8,128)(2,1)S(1)}, bf16[256,1024]{1,0:T(8,128)(2,1)S(1)}, u32[]{:S(2)}, u32[]{:S(2)}) collective-permute-start(bf16[256,1024]{1,0:T(8,128)(2,1)S(1)} %multiply_convert_fusion.1), channel_id=1, source_target_pairs={{0,4},{1,5},{2,6},{3,7},{4,0},{5,1},{6,2},{7,3},{8,12},{9,13},{10,... | collective-permute-start | bytes 1572872 | tf_op jit(solution)/shard_map/ppermute | solution.py:15
  86.3 14.8 %collective-permute-start.22 = (bf16[256,1024]{1,0:T(8,128)(2,1)S(1)}, bf16[256,1024]{1,0:T(8,128)(2,1)S(1)}, u32[]{:S(2)}, u32[]{:S(2)}) collective-permute-start(bf16[256,1024]{1,0:T(8,128)(2,1)S(1)} %multiply_convert_fusion.1), channel_id=1, source_target_pairs={{0,2},{1,3},{2,0},{3,1},{4,6},{5,7},{6,4},{7,5},{8,10},{9,11},{10,... | collective-permute-start | bytes 1572872 | tf_op jit(solution)/shard_map/ppermute | solution.py:15
  86.9 17.6 %collective-permute-start.28 = (bf16[256,1024]{1,0:T(8,128)(2,1)S(1)}, bf16[256,1024]{1,0:T(8,128)(2,1)S(1)}, u32[]{:S(2)}, u32[]{:S(2)}) collective-permute-start(bf16[256,1024]{1,0:T(8,128)(2,1)S(1)} %broadcast_select_fusion.7), channel_id=1, source_target_pairs={{0,4},{1,3},{2,6},{3,1},{4,0},{5,7},{6,2},{7,5},{8,12},{9,11},{10,... | collective-permute-start | bytes 1572872 | tf_op jit(solution)/shard_map/ppermute | solution.py:15
  146.2 29.2 %collective-permute-start.35 = (bf16[576,1024]{1,0:T(8,128)(2,1)S(1)}, bf16[576,1024]{1,0:T(8,128)(2,1)S(1)}, u32[]{:S(2)}, u32[]{:S(2)}) collective-permute-start(bf16[576,1024]{1,0:T(8,128)(2,1)S(1)} %convolution_convert_fusion.4), channel_id=1, source_target_pairs={{0,8},{24,16},{1,9},{25,17},{2,10},{26,18},{3,11},{27,19},{4,12},{... | collective-permute-start | bytes 3538952 | tf_op jit(solution)/shard_map/ppermute | solution.py:15
  160.0 13.1 %collective-permute-start.33 = (bf16[256,1024]{1,0:T(8,128)(2,1)S(1)}, bf16[256,1024]{1,0:T(8,128)(2,1)S(1)}, u32[]{:S(2)}, u32[]{:S(2)}) collective-permute-start(bf16[256,1024]{1,0:T(8,128)(2,1)S(1)} %get-tuple-element.305), channel_id=1, source_target_pairs={{0,2},{1,3},{2,0},{3,1},{4,6},{5,7},{6,4},{7,5},{8,10},{9,11},{10,... | collective-permute-start | bytes 1572872 | tf_op jit(solution)/shard_map/ppermute | solution.py:15
  160.9 12.8 %collective-permute-start.34 = (bf16[256,1024]{1,0:T(8,128)(2,1)S(1)}, bf16[256,1024]{1,0:T(8,128)(2,1)S(1)}, u32[]{:S(2)}, u32[]{:S(2)}) collective-permute-start(bf16[256,1024]{1,0:T(8,128)(2,1)S(1)} %get-tuple-element.306), channel_id=1, source_target_pairs={{0,4},{1,5},{2,6},{3,7},{4,0},{5,1},{6,2},{7,3},{8,12},{9,13},{10,... | collective-permute-start | bytes 1572872 | tf_op jit(solution)/shard_map/ppermute | solution.py:15
  179.7 15.4 %collective-permute-start.36 = (bf16[512,2048]{1,0:T(8,128)(2,1)S(1)}, bf16[512,2048]{1,0:T(8,128)(2,1)S(1)}, u32[]{:S(2)}, u32[]{:S(2)}) collective-permute-start(bf16[512,2048]{1,0:T(8,128)(2,1)S(1)} %pad_maximum_fusion.5), channel_id=1, source_target_pairs={{0,1},{1,0},{2,3},{3,2},{4,5},{5,4},{6,7},{7,6},{8,9},{9,8},{10,11... | collective-permute-start | bytes 6291464 | tf_op jit(solution)/shard_map/ppermute | solution.py:15
  179.9 33.2 %collective-permute-start.41 = (bf16[1024,1024]{1,0:T(8,128)(2,1)}, bf16[1024,1024]{1,0:T(8,128)(2,1)}, u32[]{:S(2)}, u32[]{:S(2)}) collective-permute-start(bf16[1024,1024]{1,0:T(8,128)(2,1)} %get-tuple-element.110), channel_id=1, source_target_pairs={{0,1},{1,0},{2,3},{3,2},{4,5},{5,4},{6,7},{7,6},{8,9},{9,8},{10,11... | collective-permute-start | bytes 6291464 | tf_op jit(solution)/shard_map/ppermute | solution.py:15
  181.9 31.1 %collective-permute-start.39 = (bf16[576,1024]{1,0:T(8,128)(2,1)}, bf16[576,1024]{1,0:T(8,128)(2,1)}, u32[]{:S(2)}, u32[]{:S(2)}) collective-permute-start(bf16[576,1024]{1,0:T(8,128)(2,1)} %add_convert_fusion.5), channel_id=1, source_target_pairs={{8,16},{16,8},{9,17},{17,9},{10,18},{18,10},{11,19},{19,11},{12,20... | collective-permute-start | bytes 3538952 | tf_op jit(solution)/shard_map/ppermute | solution.py:15
  183.6 31.7 %collective-permute-start.40 = (bf16[576,1024]{1,0:T(8,128)(2,1)}, bf16[576,1024]{1,0:T(8,128)(2,1)}, u32[]{:S(2)}, u32[]{:S(2)}) collective-permute-start(bf16[576,1024]{1,0:T(8,128)(2,1)} %convolution_convert_fusion.3), channel_id=1, source_target_pairs={{0,8},{24,16},{1,9},{25,17},{2,10},{26,18},{3,11},{27,19},{4,12},{... | collective-permute-start | bytes 3538952 | tf_op jit(solution)/shard_map/ppermute | solution.py:15
  196.0 19.2 %collective-permute-start.38 = (bf16[128,2048]{1,0:T(8,128)(2,1)}, bf16[128,2048]{1,0:T(8,128)(2,1)}, u32[]{:S(2)}, u32[]{:S(2)}) collective-permute-start(bf16[128,2048]{1,0:T(8,128)(2,1)} %add_convert_fusion.15), channel_id=1, source_target_pairs={{0,2},{1,5},{2,0},{3,7},{4,6},{5,1},{6,4},{7,3},{8,10},{9,13},{10,... | collective-permute-start | bytes 1572872 | tf_op jit(solution)/shard_map/ppermute | solution.py:15
  218.1 28.8 %collective-permute-start.43 = (bf16[576,1024]{1,0:T(8,128)(2,1)S(1)}, bf16[576,1024]{1,0:T(8,128)(2,1)S(1)}, u32[]{:S(2)}, u32[]{:S(2)}) collective-permute-start(bf16[576,1024]{1,0:T(8,128)(2,1)S(1)} %broadcast_select_fusion.1), channel_id=1, source_target_pairs={{0,8},{24,16},{8,0},{16,24},{1,9},{25,17},{9,1},{17,25},{2,10},{26... | collective-permute-start | bytes 3538952 | tf_op jit(solution)/shard_map/ppermute | solution.py:15
  222.4 25.5 %collective-permute-start.44 = (bf16[576,1024]{1,0:T(8,128)(2,1)S(1)}, bf16[576,1024]{1,0:T(8,128)(2,1)S(1)}, u32[]{:S(2)}, u32[]{:S(2)}) collective-permute-start(bf16[576,1024]{1,0:T(8,128)(2,1)S(1)} %add_convert_fusion.3), channel_id=1, source_target_pairs={{8,16},{16,8},{9,17},{17,9},{10,18},{18,10},{11,19},{19,11},{12,20... | collective-permute-start | bytes 3538952 | tf_op jit(solution)/shard_map/ppermute | solution.py:15
  224.4 23.5 %collective-permute-start.45 = (bf16[128,2176]{1,0:T(8,128)(2,1)S(1)}, bf16[128,2176]{1,0:T(8,128)(2,1)S(1)}, u32[]{:S(2)}, u32[]{:S(2)}) collective-permute-start(bf16[128,2176]{1,0:T(8,128)(2,1)S(1)} %add_convert_fusion.9), channel_id=1, source_target_pairs={{0,2},{1,5},{2,0},{3,7},{4,6},{5,1},{6,4},{7,3},{8,10},{9,13},{10,... | collective-permute-start | bytes 1671176 | tf_op jit(solution)/shard_map/ppermute | solution.py:15
  226.8 21.1 %collective-permute-start.47 = (bf16[128,2048]{1,0:T(8,128)(2,1)S(1)}, bf16[128,2048]{1,0:T(8,128)(2,1)S(1)}, u32[]{:S(2)}, u32[]{:S(2)}) collective-permute-start(bf16[128,2048]{1,0:T(8,128)(2,1)S(1)} %get-tuple-element.303), channel_id=1, source_target_pairs={{0,4},{1,5},{2,6},{3,7},{4,0},{5,1},{6,2},{7,3},{8,12},{9,13},{10,... | collective-permute-start | bytes 1572872 | tf_op jit(solution)/shard_map/ppermute | solution.py:15
  228.1 19.8 %collective-permute-start.46 = (bf16[128,2048]{1,0:T(8,128)(2,1)S(1)}, bf16[128,2048]{1,0:T(8,128)(2,1)S(1)}, u32[]{:S(2)}, u32[]{:S(2)}) collective-permute-start(bf16[128,2048]{1,0:T(8,128)(2,1)S(1)} %get-tuple-element.304), channel_id=1, source_target_pairs={{0,2},{1,3},{2,0},{3,1},{4,6},{5,7},{6,4},{7,5},{8,10},{9,11},{10,... | collective-permute-start | bytes 1572872 | tf_op jit(solution)/shard_map/ppermute | solution.py:15
  248.9 32.1 %collective-permute-start.49 = (bf16[576,1024]{1,0:T(8,128)(2,1)S(1)}, bf16[576,1024]{1,0:T(8,128)(2,1)S(1)}, u32[]{:S(2)}, u32[]{:S(2)}) collective-permute-start(bf16[576,1024]{1,0:T(8,128)(2,1)S(1)} %add_convert_fusion.2), channel_id=1, source_target_pairs={{8,0},{16,24},{9,1},{17,25},{10,2},{18,26},{11,3},{19,27},{12,4},{... | collective-permute-start | bytes 3538952 | tf_op jit(solution)/shard_map/ppermute | solution.py:15
  250.2 30.8 %collective-permute-start.50 = (bf16[576,1024]{1,0:T(8,128)(2,1)S(1)}, bf16[576,1024]{1,0:T(8,128)(2,1)S(1)}, u32[]{:S(2)}, u32[]{:S(2)}) collective-permute-start(bf16[576,1024]{1,0:T(8,128)(2,1)S(1)} %add_convert_fusion.1), channel_id=1, source_target_pairs={{8,16},{16,8},{9,17},{17,9},{10,18},{18,10},{11,19},{19,11},{12,20... | collective-permute-start | bytes 3538952 | tf_op jit(solution)/shard_map/ppermute | solution.py:15
  252.8 21.2 %collective-permute-start.53 = (bf16[128,2176]{1,0:T(8,128)(2,1)S(1)}, bf16[128,2176]{1,0:T(8,128)(2,1)S(1)}, u32[]{:S(2)}, u32[]{:S(2)}) collective-permute-start(bf16[128,2176]{1,0:T(8,128)(2,1)S(1)} %get-tuple-element.299), channel_id=1, source_target_pairs={{0,4},{1,5},{2,6},{3,7},{4,0},{5,1},{6,2},{7,3},{8,12},{9,13},{10,... | collective-permute-start | bytes 1671176 | tf_op jit(solution)/shard_map/ppermute | solution.py:15
  254.1 19.9 %collective-permute-start.52 = (bf16[128,2176]{1,0:T(8,128)(2,1)S(1)}, bf16[128,2176]{1,0:T(8,128)(2,1)S(1)}, u32[]{:S(2)}, u32[]{:S(2)}) collective-permute-start(bf16[128,2176]{1,0:T(8,128)(2,1)S(1)} %get-tuple-element.300), channel_id=1, source_target_pairs={{0,2},{1,3},{2,0},{3,1},{4,6},{5,7},{6,4},{7,5},{8,10},{9,11},{10,... | collective-permute-start | bytes 1671176 | tf_op jit(solution)/shard_map/ppermute | solution.py:15
  256.1 17.8 %collective-permute-start.48 = (bf16[128,2048]{1,0:T(8,128)(2,1)S(1)}, bf16[128,2048]{1,0:T(8,128)(2,1)S(1)}, u32[]{:S(2)}, u32[]{:S(2)}) collective-permute-start(bf16[128,2048]{1,0:T(8,128)(2,1)S(1)} %add_convert_fusion.14), channel_id=1, source_target_pairs={{0,8},{24,16},{1,9},{25,17},{2,10},{26,18},{3,11},{27,19},{4,12},{... | collective-permute-start | bytes 1572872 | tf_op jit(solution)/shard_map/ppermute | solution.py:15
  282.6 31.3 %collective-permute-start.56 = (bf16[576,1024]{1,0:T(8,128)(2,1)S(1)}, bf16[576,1024]{1,0:T(8,128)(2,1)S(1)}, u32[]{:S(2)}, u32[]{:S(2)}) collective-permute-start(bf16[576,1024]{1,0:T(8,128)(2,1)S(1)} %add_convert_fusion), channel_id=1, source_target_pairs={{8,0},{16,24},{9,1},{17,25},{10,2},{18,26},{11,3},{19,27},{12,4},{... | collective-permute-start | bytes 3538952 | tf_op jit(solution)/shard_map/ppermute | solution.py:15
  284.2 27.8 %collective-permute-start.59 = (bf16[2,1152,128]{2,1,0:T(8,128)(2,1)S(1)}, bf16[2,1152,128]{2,1,0:T(8,128)(2,1)S(1)}, u32[]{:S(2)}, u32[]{:S(2)}) collective-permute-start(bf16[2,1152,128]{2,1,0:T(8,128)(2,1)S(1)} %get-tuple-element.313), channel_id=1, source_target_pairs={{0,6},{1,7},{2,4},{3,5},{4,2},{5,3},{6,0},{7,1},{8,14},{9,15},{10,... | collective-permute-start | bytes 1769480 | tf_op jit(solution)/shard_map/ppermute | solution.py:15
  285.7 26.5 %collective-permute-start.58 = (bf16[2,1152,128]{2,1,0:T(8,128)(2,1)S(1)}, bf16[2,1152,128]{2,1,0:T(8,128)(2,1)S(1)}, u32[]{:S(2)}, u32[]{:S(2)}) collective-permute-start(bf16[2,1152,128]{2,1,0:T(8,128)(2,1)S(1)} %get-tuple-element.314), channel_id=1, source_target_pairs={{0,4},{1,5},{2,6},{3,7},{4,0},{5,1},{6,2},{7,3},{8,12},{9,13},{10,... | collective-permute-start | bytes 1769480 | tf_op jit(solution)/shard_map/ppermute | solution.py:15
  286.5 25.6 %collective-permute-start.57 = (bf16[2,1152,128]{2,1,0:T(8,128)(2,1)S(1)}, bf16[2,1152,128]{2,1,0:T(8,128)(2,1)S(1)}, u32[]{:S(2)}, u32[]{:S(2)}) collective-permute-start(bf16[2,1152,128]{2,1,0:T(8,128)(2,1)S(1)} %get-tuple-element.315), channel_id=1, source_target_pairs={{0,2},{1,3},{2,0},{3,1},{4,6},{5,7},{6,4},{7,5},{8,10},{9,11},{10,... | collective-permute-start | bytes 1769480 | tf_op jit(solution)/shard_map/ppermute | solution.py:15
  289.1 22.9 %collective-permute-start.54 = (bf16[128,2176]{1,0:T(8,128)(2,1)S(1)}, bf16[128,2176]{1,0:T(8,128)(2,1)S(1)}, u32[]{:S(2)}, u32[]{:S(2)}) collective-permute-start(bf16[128,2176]{1,0:T(8,128)(2,1)S(1)} %add_convert_fusion.8), channel_id=1, source_target_pairs={{0,8},{24,16},{1,9},{25,17},{2,10},{26,18},{3,11},{27,19},{4,12},{... | collective-permute-start | bytes 1671176 | tf_op jit(solution)/shard_map/ppermute | solution.py:15
  314.8 18.1 %collective-permute-start.61 = (bf16[128,2048]{1,0:T(8,128)(2,1)}, bf16[128,2048]{1,0:T(8,128)(2,1)}, u32[]{:S(2)}, u32[]{:S(2)}) collective-permute-start(bf16[128,2048]{1,0:T(8,128)(2,1)} %add_convert_fusion.11), channel_id=1, source_target_pairs={{8,0},{16,24},{9,1},{17,25},{10,2},{18,26},{11,3},{19,27},{12,4},{... | collective-permute-start | bytes 1572872 | tf_op jit(solution)/shard_map/ppermute | solution.py:15
  317.5 20.0 %collective-permute-start.60 = (bf16[128,2176]{1,0:T(8,128)(2,1)}, bf16[128,2176]{1,0:T(8,128)(2,1)}, u32[]{:S(2)}, u32[]{:S(2)}) collective-permute-start(bf16[128,2176]{1,0:T(8,128)(2,1)} %add_convert_fusion.7), channel_id=1, source_target_pairs={{8,16},{16,8},{9,17},{17,9},{10,18},{18,10},{11,19},{19,11},{12,20... | collective-permute-start | bytes 1671176 | tf_op jit(solution)/shard_map/ppermute | solution.py:15
  321.7 14.6 %collective-permute-start.63 = (bf16[256,1024]{1,0:T(8,128)(2,1)}, bf16[256,1024]{1,0:T(8,128)(2,1)}, u32[]{:S(2)}, u32[]{:S(2)}) collective-permute-start(bf16[256,1024]{1,0:T(8,128)(2,1)} %get-tuple-element.301), channel_id=1, source_target_pairs={{0,4},{1,5},{2,6},{3,7},{4,0},{5,1},{6,2},{7,3},{8,12},{9,13},{10,... | collective-permute-start | bytes 1572872 | tf_op jit(solution)/shard_map/ppermute | solution.py:15
  323.2 14.4 %collective-permute-start.62 = (bf16[256,1024]{1,0:T(8,128)(2,1)}, bf16[256,1024]{1,0:T(8,128)(2,1)}, u32[]{:S(2)}, u32[]{:S(2)}) collective-permute-start(bf16[256,1024]{1,0:T(8,128)(2,1)} %get-tuple-element.302), channel_id=1, source_target_pairs={{0,2},{1,3},{2,0},{3,1},{4,6},{5,7},{6,4},{7,5},{8,10},{9,11},{10,... | collective-permute-start | bytes 1572872 | tf_op jit(solution)/shard_map/ppermute | solution.py:15
  340.0 18.5 %collective-permute-start.65 = (bf16[128,2176]{1,0:T(8,128)(2,1)S(1)}, bf16[128,2176]{1,0:T(8,128)(2,1)S(1)}, u32[]{:S(2)}, u32[]{:S(2)}) collective-permute-start(bf16[128,2176]{1,0:T(8,128)(2,1)S(1)} %add_convert_fusion.6), channel_id=1, source_target_pairs={{8,0},{16,24},{9,1},{17,25},{10,2},{18,26},{11,3},{19,27},{12,4},{... | collective-permute-start | bytes 1671176 | tf_op jit(solution)/shard_map/ppermute | solution.py:15
  (70 other events, 480.3 us)

commit v5 on v4

--- a/solution.py
+++ b/solution.py
@@ -383,9 +383,7 @@
     grad_normed_mid = scattered(ours, near, scatter_last(ours, near, across))
     term_up = times(grad_up, normed_all).astype(bf16)
     term_down = times(activ, grad_out_all).astype(bf16)
-    grad_normed_mid, came_gate, term_up, term_down = together(
-        grad_normed_mid, came_gate, term_up, term_down
-    )
+    grad_normed_mid, term_up, term_down = together(grad_normed_mid, term_up, term_down)
     came_up = inward(term_up)
     pair_gate = add_pair(term_gate, came_gate)
     far_gate = between(pair_gate)

time: 368 us -> 364 us (0.989)
  transfers between devices with their start and end apart: 66 -> 66, of which waited for: 30 -> 29; matrix products, arithmetic and copies ran while one was open for 24% -> 25% of each run, Pallas kernels for 0% -> 0%
where the time goes in v5:
time: 364 us; the launch traced here: 358 us
  waiting for transfers between devices  142 us (39%)
  starting transfers between devices  84.6 us (23%)
  other arithmetic  61 us (17%)
  Pallas kernels  24.4 us (7%)
  matrix products  21.6 us (6%)
  local copies, waits for them, and re-layouts  21.3 us (6%)
    ppermute x64, waiting for transfers between devices, along(): return lax.ppermute(shard, axis, pairs)  141 us
    ppermute x64, starting transfers between devices, along(): return lax.ppermute(shard, axis, pairs)  81.3 us
    pallas_call x1, Pallas kernels, feed_forward(): pl.pallas_call(feed_forward_kernel, grid=(steps,), in_specs=[rows, rows,...  24.4 us
    dot_general x5, matrix products, times(): return jnp.dot(left, right, preferred_element_type=f32)  15.7 us
    unnamed x139, local copies, waits for them, and re-layouts  10.9 us
    unnamed x44, other arithmetic  10.1 us
    convert_element_type x9, other arithmetic, add_pair(): (one.astype(f32) + other.astype(f32)).astype(bf16)  8.33 us
  transfers between devices with their start and end apart: 66, of which 29 were waited for; matrix products, arithmetic and copies ran while one was open for 25% of the time, Pallas kernels for 0%

profile of v5, /device:TPU:0, one launch (start us, length us, event | category | flops | bytes accessed | tf_op | source)
XLA Modules:
  0.0 357.8 jit_solution(1789797543034612000)
XLA Ops:
  1.5 3.0 collective-permute-start
  6.6 2.4 copy.72
  13.0 2.0 collective-permute-start.3
  15.8 9.2 %collective-permute-done.3 = bf16[8,128]{1,0:T(8,128)(2,1)S(1)} collective-permute-done((bf16[8,128]{1,0:T(8,128)(2,1)S(1)}, bf16[8,128]{1,0:T(8,128)(2,1)S(1)}, u32[]{:S(2)}, u32[]{:S(2)}) %collective-permute-start.3) | collective-permute-done | bytes 2080 | tf_op jit(solution)/shard_map/ppermute | solution.py:15
  35.1 13.3 %collective-permute-done.11 = bf16[128,1024]{1,0:T(8,128)(2,1)S(1)} collective-permute-done((bf16[128,1024]{1,0:T(8,128)(2,1)S(1)}, bf16[128,1024]{1,0:T(8,128)(2,1)S(1)}, u32[]{:S(2)}, u32[]{:S(2)}) %collective-permute-start.11) | collective-permute-done | bytes 262176 | tf_op jit(solution)/shard_map/ppermute | solution.py:15
  51.4 11.3 %collective-permute-done.15 = bf16[128,1024]{1,0:T(8,128)(2,1)S(1)} collective-permute-done((bf16[128,1024]{1,0:T(8,128)(2,1)S(1)}, bf16[128,1024]{1,0:T(8,128)(2,1)S(1)}, u32[]{:S(2)}, u32[]{:S(2)}) %collective-permute-start.15) | collective-permute-done | bytes 262176 | tf_op jit(solution)/shard_map/ppermute | solution.py:15
  64.7 2.9 collective-permute-done.18
  67.6 1.8 collective-permute-done.17
  71.0 1.8 fusion.70
  73.7 1.8 collective-permute-start.13
  78.1 3.9 %collective-permute-done.21 = bf16[256,1024]{1,0:T(8,128)(2,1)S(1)} collective-permute-done((bf16[256,1024]{1,0:T(8,128)(2,1)S(1)}, bf16[256,1024]{1,0:T(8,128)(2,1)S(1)}, u32[]{:S(2)}, u32[]{:S(2)}) %collective-permute-start.21) | collective-permute-done | bytes 524320 | tf_op jit(solution)/shard_map/ppermute | solution.py:15
  83.2 1.6 collective-permute-start.30
  87.8 11.1 %collective-permute-done.23 = bf16[256,1024]{1,0:T(8,128)(2,1)S(1)} collective-permute-done((bf16[256,1024]{1,0:T(8,128)(2,1)S(1)}, bf16[256,1024]{1,0:T(8,128)(2,1)S(1)}, u32[]{:S(2)}, u32[]{:S(2)}) %collective-permute-start.23) | collective-permute-done | bytes 524320 | tf_op jit(solution)/shard_map/ppermute | solution.py:15
  98.9 2.2 collective-permute-done.22
  101.8 2.7 collective-permute-done.28
  106.0 5.6 %collective-permute-done.30 = bf16[576,1024]{1,0:T(8,128)(2,1)S(1)} collective-permute-done((bf16[576,1024]{1,0:T(8,128)(2,1)S(1)}, bf16[576,1024]{1,0:T(8,128)(2,1)S(1)}, u32[]{:S(2)}, u32[]{:S(2)}) %collective-permute-start.30) | collective-permute-done | bytes 1179680 | tf_op jit(solution)/shard_map/ppermute | solution.py:15
  114.3 1.8 copy-done.23
  116.1 24.4 %shard_map.177 = (bf16[576,2048]{1,0:T(8,128)(2,1)}, bf16[576,2048]{1,0:T(8,128)(2,1)}, bf16[576,2048]{1,0:T(8,128)(2,1)}, bf16[1024,1024]{1,0:T(8,128)(2,1)S(1)...) custom-call(bf16[2048,1024]{1,0:T(8,128)(2,1)} %bitcast.278, ...), custom_call_target="tpu_custom_call" | custom-call | flops 14495514624 | bytes 27394048 | tf_op jit(solution)/shard_map/pallas_call | solution.py:295
  140.5 5.6 %convolution_convert_fusion.4 = bf16[576,1024]{1,0:T(8,128)(2,1)S(1)} fusion(bf16[576,2048]{1,0:T(8,128)(2,1)} %get-tuple-element.97, bf16[2048,1024]{1,0:T(8,128)(2,1)} %bitcast.279), kind=kOutput, calls=%fused_computation.32 | convolution fusion | flops 2416508928 | bytes 7733248 | tf_op jit(solution)/shard_map/dot_general | solution.py:229
  146.2 3.8 %collective-permute-start.38 = (bf16[576,1024]{1,0:T(8,128)(2,1)S(1)}, bf16[576,1024]{1,0:T(8,128)(2,1)S(1)}, u32[]{:S(2)}, u32[]{:S(2)}) collective-permute-start(bf16[576,1024]{1,0:T(8,128)(2,1)S(1)} %convolution_convert_fusion.4), channel_id=1, source_target_pairs={{0,8},{24,16},{1,9},{25,17},{2,10},{26,18},{3,11},{27,19},{4,12},{... | collective-permute-start | bytes 3538952 | tf_op jit(solution)/shard_map/ppermute | solution.py:15
  151.1 3.7 %convolution_convert_fusion.2 = bf16[576,1024]{1,0:T(8,128)(2,1)} fusion(bf16[576,2048]{1,0:T(8,128)(2,1)S(1)} %copy-done.49, bf16[2048,1024]{1,0:T(8,128)(2,1)S(1)} %bitcast.277), kind=kOutput, calls=%fused_computation.30 | convolution fusion | flops 2416508928 | bytes 7733248 | tf_op jit(solution)/shard_map/dot_general | solution.py:229
  154.8 4.6 %collective-permute-done.32 = bf16[256,1024]{1,0:T(8,128)(2,1)S(1)} collective-permute-done((bf16[256,1024]{1,0:T(8,128)(2,1)S(1)}, bf16[256,1024]{1,0:T(8,128)(2,1)S(1)}, u32[]{:S(2)}, u32[]{:S(2)}) %collective-permute-start.32) | collective-permute-done | bytes 524320 | tf_op jit(solution)/shard_map/ppermute | solution.py:15
  162.1 3.7 %convolution_convert_fusion.3 = bf16[576,1024]{1,0:T(8,128)(2,1)} fusion(bf16[576,2048]{1,0:T(8,128)(2,1)S(1)} %copy-done.48, bf16[2048,1024]{1,0:T(8,128)(2,1)S(1)} %bitcast.280), kind=kOutput, calls=%fused_computation.31 | convolution fusion | flops 2416508928 | bytes 7733248 | tf_op jit(solution)/shard_map/dot_general | solution.py:229
  165.8 7.3 %collective-permute-done.33 = bf16[256,1024]{1,0:T(8,128)(2,1)S(1)} collective-permute-done((bf16[256,1024]{1,0:T(8,128)(2,1)S(1)}, bf16[256,1024]{1,0:T(8,128)(2,1)S(1)}, u32[]{:S(2)}, u32[]{:S(2)}) %collective-permute-start.33) | collective-permute-done | bytes 524320 | tf_op jit(solution)/shard_map/ppermute | solution.py:15
  180.5 1.7 collective-permute-start.39
  182.2 4.4 %collective-permute-start.40 = (bf16[576,1024]{1,0:T(8,128)(2,1)}, bf16[576,1024]{1,0:T(8,128)(2,1)}, u32[]{:S(2)}, u32[]{:S(2)}) collective-permute-start(bf16[576,1024]{1,0:T(8,128)(2,1)} %convolution_convert_fusion.3), channel_id=1, source_target_pairs={{0,8},{24,16},{1,9},{25,17},{2,10},{26,18},{3,11},{27,19},{4,12},{... | collective-permute-start | bytes 3538952 | tf_op jit(solution)/shard_map/ppermute | solution.py:15
  193.2 1.8 fusion
  206.4 2.5 pad_maximum_fusion.3
  208.9 2.1 collective-permute-done.40
  211.0 2.9 broadcast_select_fusion.1
  213.9 2.2 collective-permute-start.43
  216.1 2.1 add_convert_fusion.3
  226.3 16.5 %collective-permute-done.43 = bf16[576,1024]{1,0:T(8,128)(2,1)S(1)} collective-permute-done((bf16[576,1024]{1,0:T(8,128)(2,1)S(1)}, bf16[576,1024]{1,0:T(8,128)(2,1)S(1)}, u32[]{:S(2)}, u32[]{:S(2)}) %collective-permute-start.43) | collective-permute-done | bytes 1179680 | tf_op jit(solution)/shard_map/ppermute | solution.py:15
  247.3 1.7 fusion.11
  251.9 8.3 %collective-permute-start.48 = (bf16[128,2048]{1,0:T(8,128)(2,1)S(1)}, bf16[128,2048]{1,0:T(8,128)(2,1)S(1)}, u32[]{:S(2)}, u32[]{:S(2)}) collective-permute-start(bf16[128,2048]{1,0:T(8,128)(2,1)S(1)} %add_convert_fusion.14), channel_id=1, source_target_pairs={{0,8},{24,16},{1,9},{25,17},{2,10},{26,18},{3,11},{27,19},{4,12},{... | collective-permute-start | bytes 1572872 | tf_op jit(solution)/shard_map/ppermute | solution.py:15
  260.2 2.1 bitcast_bitcast_fusion.1
  262.3 8.1 %collective-permute-done.48 = bf16[128,2048]{1,0:T(8,128)(2,1)S(1)} collective-permute-done((bf16[128,2048]{1,0:T(8,128)(2,1)S(1)}, bf16[128,2048]{1,0:T(8,128)(2,1)S(1)}, u32[]{:S(2)}, u32[]{:S(2)}) %collective-permute-start.48) | collective-permute-done | bytes 524320 | tf_op jit(solution)/shard_map/ppermute | solution.py:15
  270.4 6.3 %collective-permute-done.49 = bf16[576,1024]{1,0:T(8,128)(2,1)S(1)} collective-permute-done((bf16[576,1024]{1,0:T(8,128)(2,1)S(1)}, bf16[576,1024]{1,0:T(8,128)(2,1)S(1)}, u32[]{:S(2)}, u32[]{:S(2)}) %collective-permute-start.49) | collective-permute-done | bytes 1179680 | tf_op jit(solution)/shard_map/ppermute | solution.py:15
  280.0 2.1 collective-permute-start.59
  284.8 13.0 %collective-permute-start.54 = (bf16[128,2176]{1,0:T(8,128)(2,1)S(1)}, bf16[128,2176]{1,0:T(8,128)(2,1)S(1)}, u32[]{:S(2)}, u32[]{:S(2)}) collective-permute-start(bf16[128,2176]{1,0:T(8,128)(2,1)S(1)} %add_convert_fusion.8), channel_id=1, source_target_pairs={{0,8},{24,16},{1,9},{25,17},{2,10},{26,18},{3,11},{27,19},{4,12},{... | collective-permute-start | bytes 1671176 | tf_op jit(solution)/shard_map/ppermute | solution.py:15
  299.1 8.6 %collective-permute-done.54 = bf16[128,2176]{1,0:T(8,128)(2,1)S(1)} collective-permute-done((bf16[128,2176]{1,0:T(8,128)(2,1)S(1)}, bf16[128,2176]{1,0:T(8,128)(2,1)S(1)}, u32[]{:S(2)}, u32[]{:S(2)}) %collective-permute-start.54) | collective-permute-done | bytes 557088 | tf_op jit(solution)/shard_map/ppermute | solution.py:15
  307.9 1.7 collective-permute-done.56
  314.8 2.7 fusion.23
  324.3 1.9 copy.88
  326.2 3.0 copy.87
  329.3 2.9 collective-permute-done.63
  337.7 2.7 add_convert_fusion.10
  340.5 13.9 %collective-permute-done.65 = bf16[128,2176]{1,0:T(8,128)(2,1)S(1)} collective-permute-done((bf16[128,2176]{1,0:T(8,128)(2,1)S(1)}, bf16[128,2176]{1,0:T(8,128)(2,1)S(1)}, u32[]{:S(2)}, u32[]{:S(2)}) %collective-permute-start.65) | collective-permute-done | bytes 557088 | tf_op jit(solution)/shard_map/ppermute | solution.py:15
  (393 shorter events, 108.3 us)
Async XLA Ops:
  1.5 11.5 %collective-permute-start = (bf16[8,128]{1,0:T(8,128)(2,1)S(1)}, bf16[8,128]{1,0:T(8,128)(2,1)S(1)}, u32[]{:S(2)}, u32[]{:S(2)}) collective-permute-start(bf16[8,128]{1,0:T(8,128)(2,1)S(1)} %fusion.53), channel_id=1, source_target_pairs={{0,2},{1,3},{2,0},{3,1},{4,6},{5,7},{6,4},{7,5},{8,10},{9,11},{10,... | collective-permute-start | bytes 6152 | tf_op jit(solution)/shard_map/ppermute | solution.py:15
  6.0 24.7 %collective-permute-start.6 = (bf16[128,3072]{1,0:T(8,128)(2,1)}, bf16[128,3072]{1,0:T(8,128)(2,1)S(1)}, u32[]{:S(2)}, u32[]{:S(2)}) collective-permute-start(bf16[128,3072]{1,0:T(8,128)(2,1)} %param.12), channel_id=1, source_target_pairs={{0,4},{1,5},{2,6},{3,7},{4,0},{5,1},{6,2},{7,3},{8,12},{9,13},{10,... | collective-permute-start | bytes 2359304 | tf_op jit(solution)/shard_map/ppermute | solution.py:15
  6.5 24.2 %collective-permute-start.5 = (bf16[128,3072]{1,0:T(8,128)(2,1)}, bf16[128,3072]{1,0:T(8,128)(2,1)S(1)}, u32[]{:S(2)}, u32[]{:S(2)}) collective-permute-start(bf16[128,3072]{1,0:T(8,128)(2,1)} %param.12), channel_id=1, source_target_pairs={{0,2},{1,3},{2,0},{3,1},{4,6},{5,7},{6,4},{7,5},{8,10},{9,11},{10,... | collective-permute-start | bytes 2359304 | tf_op jit(solution)/shard_map/ppermute | solution.py:15
  12.7 18.7 %collective-permute-start.12 = (bf16[4,576,128]{2,1,0:T(8,128)(2,1)}, bf16[4,576,128]{2,1,0:T(8,128)(2,1)}, u32[]{:S(2)}, u32[]{:S(2)}) collective-permute-start(bf16[4,576,128]{2,1,0:T(8,128)(2,1)} %select_bitcast_fusion.4), channel_id=1, source_target_pairs={{0,1},{1,0},{2,3},{3,2},{4,5},{5,4},{6,7},{7,6},{8,9},{9,8},{10,11... | collective-permute-start | bytes 1769480 | tf_op jit(solution)/shard_map/ppermute | solution.py:15
  13.0 12.0 %collective-permute-start.3 = (bf16[8,128]{1,0:T(8,128)(2,1)S(1)}, bf16[8,128]{1,0:T(8,128)(2,1)S(1)}, u32[]{:S(2)}, u32[]{:S(2)}) collective-permute-start(bf16[8,128]{1,0:T(8,128)(2,1)S(1)} %broadcast_select_fusion.82), channel_id=1, source_target_pairs={{0,4},{1,3},{2,6},{3,1},{4,0},{5,7},{6,2},{7,5},{8,12},{9,11},{10,... | collective-permute-start | bytes 6152 | tf_op jit(solution)/shard_map/ppermute | solution.py:15
  30.8 17.7 %collective-permute-start.8 = (bf16[128,3072]{1,0:T(8,128)(2,1)S(1)}, bf16[128,3072]{1,0:T(8,128)(2,1)S(1)}, u32[]{:S(2)}, u32[]{:S(2)}) collective-permute-start(bf16[128,3072]{1,0:T(8,128)(2,1)S(1)} %broadcast_select_fusion.5), channel_id=1, source_target_pairs={{0,4},{1,3},{2,6},{3,1},{4,0},{5,7},{6,2},{7,5},{8,12},{9,11},{10,... | collective-permute-start | bytes 2359304 | tf_op jit(solution)/shard_map/ppermute | solution.py:15
  32.7 15.8 %collective-permute-start.11 = (bf16[128,1024]{1,0:T(8,128)(2,1)S(1)}, bf16[128,1024]{1,0:T(8,128)(2,1)S(1)}, u32[]{:S(2)}, u32[]{:S(2)}) collective-permute-start(bf16[128,1024]{1,0:T(8,128)(2,1)S(1)} %copy-done.19), channel_id=1, source_target_pairs={{0,4},{1,5},{2,6},{3,7},{4,0},{5,1},{6,2},{7,3},{8,12},{9,13},{10,... | collective-permute-start | bytes 786440 | tf_op jit(solution)/shard_map/ppermute | solution.py:15
  34.3 14.2 %collective-permute-start.10 = (bf16[128,1024]{1,0:T(8,128)(2,1)S(1)}, bf16[128,1024]{1,0:T(8,128)(2,1)S(1)}, u32[]{:S(2)}, u32[]{:S(2)}) collective-permute-start(bf16[128,1024]{1,0:T(8,128)(2,1)S(1)} %copy-done.19), channel_id=1, source_target_pairs={{0,2},{1,3},{2,0},{3,1},{4,6},{5,7},{6,4},{7,5},{8,10},{9,11},{10,... | collective-permute-start | bytes 786440 | tf_op jit(solution)/shard_map/ppermute | solution.py:15
  35.1 35.4 %collective-permute-start.7 = (bf16[3,128,3072]{2,1,0:T(8,128)(2,1)S(1)}, bf16[3,128,3072]{2,1,0:T(8,128)(2,1)S(1)}, u32[]{:S(2)}, u32[]{:S(2)}) collective-permute-start(bf16[3,128,3072]{2,1,0:T(8,128)(2,1)S(1)} %pad_maximum_fusion), channel_id=1, source_target_pairs={{0,1},{1,0},{2,3},{3,2},{4,5},{5,4},{6,7},{7,6},{8,9},{9,8},{10,11... | collective-permute-start | bytes 7077896 | tf_op jit(solution)/shard_map/ppermute | solution.py:15
  48.5 14.1 %collective-permute-start.15 = (bf16[128,1024]{1,0:T(8,128)(2,1)S(1)}, bf16[128,1024]{1,0:T(8,128)(2,1)S(1)}, u32[]{:S(2)}, u32[]{:S(2)}) collective-permute-start(bf16[128,1024]{1,0:T(8,128)(2,1)S(1)} %broadcast_select_fusion.9), channel_id=1, source_target_pairs={{0,4},{1,3},{2,6},{3,1},{4,0},{5,7},{6,2},{7,5},{8,12},{9,11},{10,... | collective-permute-start | bytes 786440 | tf_op jit(solution)/shard_map/ppermute | solution.py:15
  49.2 20.8 %collective-permute-start.14 = (bf16[3,128,1024]{2,1,0:T(8,128)(2,1)S(1)}, bf16[3,128,1024]{2,1,0:T(8,128)(2,1)S(1)}, u32[]{:S(2)}, u32[]{:S(2)}) collective-permute-start(bf16[3,128,1024]{2,1,0:T(8,128)(2,1)S(1)} %pad_maximum_fusion.10), channel_id=1, source_target_pairs={{0,1},{1,0},{2,3},{3,2},{4,5},{5,4},{6,7},{7,6},{8,9},{9,8},{10,11... | collective-permute-start | bytes 2359304 | tf_op jit(solution)/shard_map/ppermute | solution.py:15
  49.4 15.4 %collective-permute-start.19 = (bf16[2,576,128]{2,1,0:T(8,128)(2,1)S(1)}, bf16[2,576,128]{2,1,0:T(8,128)(2,1)S(1)}, u32[]{:S(2)}, u32[]{:S(2)}) collective-permute-start(bf16[2,576,128]{2,1,0:T(8,128)(2,1)S(1)} %get-tuple-element.318), channel_id=1, source_target_pairs={{0,6},{1,7},{2,4},{3,5},{4,2},{5,3},{6,0},{7,1},{8,14},{9,15},{10,... | collective-permute-start | bytes 884744 | tf_op jit(solution)/shard_map/ppermute | solution.py:15
  50.9 16.7 %collective-permute-start.18 = (bf16[2,576,128]{2,1,0:T(8,128)(2,1)S(1)}, bf16[2,576,128]{2,1,0:T(8,128)(2,1)S(1)}, u32[]{:S(2)}, u32[]{:S(2)}) collective-permute-start(bf16[2,576,128]{2,1,0:T(8,128)(2,1)S(1)} %get-tuple-element.319), channel_id=1, source_target_pairs={{0,4},{1,5},{2,6},{3,7},{4,0},{5,1},{6,2},{7,3},{8,12},{9,13},{10,... | collective-permute-start | bytes 884744 | tf_op jit(solution)/shard_map/ppermute | solution.py:15
  69.4 12.6 %collective-permute-start.21 = (bf16[256,1024]{1,0:T(8,128)(2,1)S(1)}, bf16[256,1024]{1,0:T(8,128)(2,1)S(1)}, u32[]{:S(2)}, u32[]{:S(2)}) collective-permute-start(bf16[256,1024]{1,0:T(8,128)(2,1)S(1)} %bitcast.253), channel_id=1, source_target_pairs={{0,4},{1,5},{2,6},{3,7},{4,0},{5,1},{6,2},{7,3},{8,12},{9,13},{10,... | collective-permute-start | bytes 1572872 | tf_op jit(solution)/shard_map/ppermute | solution.py:15
  70.0 12.5 %collective-permute-start.20 = (bf16[256,1024]{1,0:T(8,128)(2,1)S(1)}, bf16[256,1024]{1,0:T(8,128)(2,1)S(1)}, u32[]{:S(2)}, u32[]{:S(2)}) collective-permute-start(bf16[256,1024]{1,0:T(8,128)(2,1)S(1)} %bitcast.254), channel_id=1, source_target_pairs={{0,2},{1,3},{2,0},{3,1},{4,6},{5,7},{6,4},{7,5},{8,10},{9,11},{10,... | collective-permute-start | bytes 1572872 | tf_op jit(solution)/shard_map/ppermute | solution.py:15
  82.6 29.3 %collective-permute-start.27 = (bf16[3,256,1024]{2,1,0:T(8,128)(2,1)S(1)}, bf16[3,256,1024]{2,1,0:T(8,128)(2,1)S(1)}, u32[]{:S(2)}, u32[]{:S(2)}) collective-permute-start(bf16[3,256,1024]{2,1,0:T(8,128)(2,1)S(1)} %pad_maximum_fusion.7), channel_id=1, source_target_pairs={{0,1},{1,0},{2,3},{3,2},{4,5},{5,4},{6,7},{7,6},{8,9},{9,8},{10,11... | collective-permute-start | bytes 4718600 | tf_op jit(solution)/shard_map/ppermute | solution.py:15
  83.2 28.4 %collective-permute-start.30 = (bf16[576,1024]{1,0:T(8,128)(2,1)S(1)}, bf16[576,1024]{1,0:T(8,128)(2,1)S(1)}, u32[]{:S(2)}, u32[]{:S(2)}) collective-permute-start(bf16[576,1024]{1,0:T(8,128)(2,1)S(1)} %bitcast.267), channel_id=1, source_target_pairs={{0,8},{8,0},{16,24},{24,16},{1,9},{9,1},{17,25},{25,17},{2,10},{10... | collective-permute-start | bytes 3538952 | tf_op jit(solution)/shard_map/ppermute | solution.py:15
  84.8 14.0 %collective-permute-start.23 = (bf16[256,1024]{1,0:T(8,128)(2,1)S(1)}, bf16[256,1024]{1,0:T(8,128)(2,1)S(1)}, u32[]{:S(2)}, u32[]{:S(2)}) collective-permute-start(bf16[256,1024]{1,0:T(8,128)(2,1)S(1)} %multiply_convert_fusion.1), channel_id=1, source_target_pairs={{0,4},{1,5},{2,6},{3,7},{4,0},{5,1},{6,2},{7,3},{8,12},{9,13},{10,... | collective-permute-start | bytes 1572872 | tf_op jit(solution)/shard_map/ppermute | solution.py:15
  86.3 14.8 %collective-permute-start.22 = (bf16[256,1024]{1,0:T(8,128)(2,1)S(1)}, bf16[256,1024]{1,0:T(8,128)(2,1)S(1)}, u32[]{:S(2)}, u32[]{:S(2)}) collective-permute-start(bf16[256,1024]{1,0:T(8,128)(2,1)S(1)} %multiply_convert_fusion.1), channel_id=1, source_target_pairs={{0,2},{1,3},{2,0},{3,1},{4,6},{5,7},{6,4},{7,5},{8,10},{9,11},{10,... | collective-permute-start | bytes 1572872 | tf_op jit(solution)/shard_map/ppermute | solution.py:15
  86.9 17.6 %collective-permute-start.28 = (bf16[256,1024]{1,0:T(8,128)(2,1)S(1)}, bf16[256,1024]{1,0:T(8,128)(2,1)S(1)}, u32[]{:S(2)}, u32[]{:S(2)}) collective-permute-start(bf16[256,1024]{1,0:T(8,128)(2,1)S(1)} %broadcast_select_fusion.7), channel_id=1, source_target_pairs={{0,4},{1,3},{2,6},{3,1},{4,0},{5,7},{6,2},{7,5},{8,12},{9,11},{10,... | collective-permute-start | bytes 1572872 | tf_op jit(solution)/shard_map/ppermute | solution.py:15
  146.2 32.9 %collective-permute-start.38 = (bf16[576,1024]{1,0:T(8,128)(2,1)S(1)}, bf16[576,1024]{1,0:T(8,128)(2,1)S(1)}, u32[]{:S(2)}, u32[]{:S(2)}) collective-permute-start(bf16[576,1024]{1,0:T(8,128)(2,1)S(1)} %convolution_convert_fusion.4), channel_id=1, source_target_pairs={{0,8},{24,16},{1,9},{25,17},{2,10},{26,18},{3,11},{27,19},{4,12},{... | collective-permute-start | bytes 3538952 | tf_op jit(solution)/shard_map/ppermute | solution.py:15
  160.0 13.1 %collective-permute-start.33 = (bf16[256,1024]{1,0:T(8,128)(2,1)S(1)}, bf16[256,1024]{1,0:T(8,128)(2,1)S(1)}, u32[]{:S(2)}, u32[]{:S(2)}) collective-permute-start(bf16[256,1024]{1,0:T(8,128)(2,1)S(1)} %get-tuple-element.303), channel_id=1, source_target_pairs={{0,2},{1,3},{2,0},{3,1},{4,6},{5,7},{6,4},{7,5},{8,10},{9,11},{10,... | collective-permute-start | bytes 1572872 | tf_op jit(solution)/shard_map/ppermute | solution.py:15
  160.9 12.8 %collective-permute-start.34 = (bf16[256,1024]{1,0:T(8,128)(2,1)S(1)}, bf16[256,1024]{1,0:T(8,128)(2,1)S(1)}, u32[]{:S(2)}, u32[]{:S(2)}) collective-permute-start(bf16[256,1024]{1,0:T(8,128)(2,1)S(1)} %get-tuple-element.304), channel_id=1, source_target_pairs={{0,4},{1,5},{2,6},{3,7},{4,0},{5,1},{6,2},{7,3},{8,12},{9,13},{10,... | collective-permute-start | bytes 1572872 | tf_op jit(solution)/shard_map/ppermute | solution.py:15
  178.4 12.5 %collective-permute-start.35 = (bf16[512,2048]{1,0:T(8,128)(2,1)S(1)}, bf16[512,2048]{1,0:T(8,128)(2,1)S(1)}, u32[]{:S(2)}, u32[]{:S(2)}) collective-permute-start(bf16[512,2048]{1,0:T(8,128)(2,1)S(1)} %pad_maximum_fusion.5), channel_id=1, source_target_pairs={{0,1},{1,0},{2,3},{3,2},{4,5},{5,4},{6,7},{7,6},{8,9},{9,8},{10,11... | collective-permute-start | bytes 6291464 | tf_op jit(solution)/shard_map/ppermute | solution.py:15
  178.5 30.4 %collective-permute-start.41 = (bf16[1024,1024]{1,0:T(8,128)(2,1)}, bf16[1024,1024]{1,0:T(8,128)(2,1)}, u32[]{:S(2)}, u32[]{:S(2)}) collective-permute-start(bf16[1024,1024]{1,0:T(8,128)(2,1)} %get-tuple-element.108), channel_id=1, source_target_pairs={{0,1},{1,0},{2,3},{3,2},{4,5},{5,4},{6,7},{7,6},{8,9},{9,8},{10,11... | collective-permute-start | bytes 6291464 | tf_op jit(solution)/shard_map/ppermute | solution.py:15
  180.5 28.3 %collective-permute-start.39 = (bf16[576,1024]{1,0:T(8,128)(2,1)}, bf16[576,1024]{1,0:T(8,128)(2,1)}, u32[]{:S(2)}, u32[]{:S(2)}) collective-permute-start(bf16[576,1024]{1,0:T(8,128)(2,1)} %add_convert_fusion.5), channel_id=1, source_target_pairs={{8,16},{16,8},{9,17},{17,9},{10,18},{18,10},{11,19},{19,11},{12,20... | collective-permute-start | bytes 3538952 | tf_op jit(solution)/shard_map/ppermute | solution.py:15
  182.2 28.8 %collective-permute-start.40 = (bf16[576,1024]{1,0:T(8,128)(2,1)}, bf16[576,1024]{1,0:T(8,128)(2,1)}, u32[]{:S(2)}, u32[]{:S(2)}) collective-permute-start(bf16[576,1024]{1,0:T(8,128)(2,1)} %convolution_convert_fusion.3), channel_id=1, source_target_pairs={{0,8},{24,16},{1,9},{25,17},{2,10},{26,18},{3,11},{27,19},{4,12},{... | collective-permute-start | bytes 3538952 | tf_op jit(solution)/shard_map/ppermute | solution.py:15
  191.8 19.2 %collective-permute-start.37 = (bf16[128,2048]{1,0:T(8,128)(2,1)}, bf16[128,2048]{1,0:T(8,128)(2,1)}, u32[]{:S(2)}, u32[]{:S(2)}) collective-permute-start(bf16[128,2048]{1,0:T(8,128)(2,1)} %add_convert_fusion.15), channel_id=1, source_target_pairs={{0,2},{1,5},{2,0},{3,7},{4,6},{5,1},{6,4},{7,3},{8,10},{9,13},{10,... | collective-permute-start | bytes 1572872 | tf_op jit(solution)/shard_map/ppermute | solution.py:15
  213.9 28.8 %collective-permute-start.43 = (bf16[576,1024]{1,0:T(8,128)(2,1)S(1)}, bf16[576,1024]{1,0:T(8,128)(2,1)S(1)}, u32[]{:S(2)}, u32[]{:S(2)}) collective-permute-start(bf16[576,1024]{1,0:T(8,128)(2,1)S(1)} %broadcast_select_fusion.1), channel_id=1, source_target_pairs={{0,8},{24,16},{8,0},{16,24},{1,9},{25,17},{9,1},{17,25},{2,10},{26... | collective-permute-start | bytes 3538952 | tf_op jit(solution)/shard_map/ppermute | solution.py:15
  218.2 25.9 %collective-permute-start.44 = (bf16[576,1024]{1,0:T(8,128)(2,1)S(1)}, bf16[576,1024]{1,0:T(8,128)(2,1)S(1)}, u32[]{:S(2)}, u32[]{:S(2)}) collective-permute-start(bf16[576,1024]{1,0:T(8,128)(2,1)S(1)} %add_convert_fusion.3), channel_id=1, source_target_pairs={{8,16},{16,8},{9,17},{17,9},{10,18},{18,10},{11,19},{19,11},{12,20... | collective-permute-start | bytes 3538952 | tf_op jit(solution)/shard_map/ppermute | solution.py:15
  220.1 23.9 %collective-permute-start.45 = (bf16[128,2176]{1,0:T(8,128)(2,1)S(1)}, bf16[128,2176]{1,0:T(8,128)(2,1)S(1)}, u32[]{:S(2)}, u32[]{:S(2)}) collective-permute-start(bf16[128,2176]{1,0:T(8,128)(2,1)S(1)} %add_convert_fusion.9), channel_id=1, source_target_pairs={{0,2},{1,5},{2,0},{3,7},{4,6},{5,1},{6,4},{7,3},{8,10},{9,13},{10,... | collective-permute-start | bytes 1671176 | tf_op jit(solution)/shard_map/ppermute | solution.py:15
  222.9 21.1 %collective-permute-start.47 = (bf16[128,2048]{1,0:T(8,128)(2,1)S(1)}, bf16[128,2048]{1,0:T(8,128)(2,1)S(1)}, u32[]{:S(2)}, u32[]{:S(2)}) collective-permute-start(bf16[128,2048]{1,0:T(8,128)(2,1)S(1)} %get-tuple-element.301), channel_id=1, source_target_pairs={{0,4},{1,5},{2,6},{3,7},{4,0},{5,1},{6,2},{7,3},{8,12},{9,13},{10,... | collective-permute-start | bytes 1572872 | tf_op jit(solution)/shard_map/ppermute | solution.py:15
  224.4 19.6 %collective-permute-start.46 = (bf16[128,2048]{1,0:T(8,128)(2,1)S(1)}, bf16[128,2048]{1,0:T(8,128)(2,1)S(1)}, u32[]{:S(2)}, u32[]{:S(2)}) collective-permute-start(bf16[128,2048]{1,0:T(8,128)(2,1)S(1)} %get-tuple-element.302), channel_id=1, source_target_pairs={{0,2},{1,3},{2,0},{3,1},{4,6},{5,7},{6,4},{7,5},{8,10},{9,11},{10,... | collective-permute-start | bytes 1572872 | tf_op jit(solution)/shard_map/ppermute | solution.py:15
  245.0 31.7 %collective-permute-start.49 = (bf16[576,1024]{1,0:T(8,128)(2,1)S(1)}, bf16[576,1024]{1,0:T(8,128)(2,1)S(1)}, u32[]{:S(2)}, u32[]{:S(2)}) collective-permute-start(bf16[576,1024]{1,0:T(8,128)(2,1)S(1)} %add_convert_fusion.2), channel_id=1, source_target_pairs={{8,0},{16,24},{9,1},{17,25},{10,2},{18,26},{11,3},{19,27},{12,4},{... | collective-permute-start | bytes 3538952 | tf_op jit(solution)/shard_map/ppermute | solution.py:15
  246.3 30.4 %collective-permute-start.50 = (bf16[576,1024]{1,0:T(8,128)(2,1)S(1)}, bf16[576,1024]{1,0:T(8,128)(2,1)S(1)}, u32[]{:S(2)}, u32[]{:S(2)}) collective-permute-start(bf16[576,1024]{1,0:T(8,128)(2,1)S(1)} %add_convert_fusion.1), channel_id=1, source_target_pairs={{8,16},{16,8},{9,17},{17,9},{10,18},{18,10},{11,19},{19,11},{12,20... | collective-permute-start | bytes 3538952 | tf_op jit(solution)/shard_map/ppermute | solution.py:15
  249.0 21.4 %collective-permute-start.53 = (bf16[128,2176]{1,0:T(8,128)(2,1)S(1)}, bf16[128,2176]{1,0:T(8,128)(2,1)S(1)}, u32[]{:S(2)}, u32[]{:S(2)}) collective-permute-start(bf16[128,2176]{1,0:T(8,128)(2,1)S(1)} %get-tuple-element.297), channel_id=1, source_target_pairs={{0,4},{1,5},{2,6},{3,7},{4,0},{5,1},{6,2},{7,3},{8,12},{9,13},{10,... | collective-permute-start | bytes 1671176 | tf_op jit(solution)/shard_map/ppermute | solution.py:15
  250.4 19.9 %collective-permute-start.52 = (bf16[128,2176]{1,0:T(8,128)(2,1)S(1)}, bf16[128,2176]{1,0:T(8,128)(2,1)S(1)}, u32[]{:S(2)}, u32[]{:S(2)}) collective-permute-start(bf16[128,2176]{1,0:T(8,128)(2,1)S(1)} %get-tuple-element.298), channel_id=1, source_target_pairs={{0,2},{1,3},{2,0},{3,1},{4,6},{5,7},{6,4},{7,5},{8,10},{9,11},{10,... | collective-permute-start | bytes 1671176 | tf_op jit(solution)/shard_map/ppermute | solution.py:15
  251.9 18.4 %collective-permute-start.48 = (bf16[128,2048]{1,0:T(8,128)(2,1)S(1)}, bf16[128,2048]{1,0:T(8,128)(2,1)S(1)}, u32[]{:S(2)}, u32[]{:S(2)}) collective-permute-start(bf16[128,2048]{1,0:T(8,128)(2,1)S(1)} %add_convert_fusion.14), channel_id=1, source_target_pairs={{0,8},{24,16},{1,9},{25,17},{2,10},{26,18},{3,11},{27,19},{4,12},{... | collective-permute-start | bytes 1572872 | tf_op jit(solution)/shard_map/ppermute | solution.py:15
  278.3 31.3 %collective-permute-start.56 = (bf16[576,1024]{1,0:T(8,128)(2,1)S(1)}, bf16[576,1024]{1,0:T(8,128)(2,1)S(1)}, u32[]{:S(2)}, u32[]{:S(2)}) collective-permute-start(bf16[576,1024]{1,0:T(8,128)(2,1)S(1)} %add_convert_fusion), channel_id=1, source_target_pairs={{8,0},{16,24},{9,1},{17,25},{10,2},{18,26},{11,3},{19,27},{12,4},{... | collective-permute-start | bytes 3538952 | tf_op jit(solution)/shard_map/ppermute | solution.py:15
  280.0 27.8 %collective-permute-start.59 = (bf16[2,1152,128]{2,1,0:T(8,128)(2,1)S(1)}, bf16[2,1152,128]{2,1,0:T(8,128)(2,1)S(1)}, u32[]{:S(2)}, u32[]{:S(2)}) collective-permute-start(bf16[2,1152,128]{2,1,0:T(8,128)(2,1)S(1)} %get-tuple-element.311), channel_id=1, source_target_pairs={{0,6},{1,7},{2,4},{3,5},{4,2},{5,3},{6,0},{7,1},{8,14},{9,15},{10,... | collective-permute-start | bytes 1769480 | tf_op jit(solution)/shard_map/ppermute | solution.py:15
  282.1 25.9 %collective-permute-start.58 = (bf16[2,1152,128]{2,1,0:T(8,128)(2,1)S(1)}, bf16[2,1152,128]{2,1,0:T(8,128)(2,1)S(1)}, u32[]{:S(2)}, u32[]{:S(2)}) collective-permute-start(bf16[2,1152,128]{2,1,0:T(8,128)(2,1)S(1)} %get-tuple-element.312), channel_id=1, source_target_pairs={{0,4},{1,5},{2,6},{3,7},{4,0},{5,1},{6,2},{7,3},{8,12},{9,13},{10,... | collective-permute-start | bytes 1769480 | tf_op jit(solution)/shard_map/ppermute | solution.py:15
  282.7 25.3 %collective-permute-start.57 = (bf16[2,1152,128]{2,1,0:T(8,128)(2,1)S(1)}, bf16[2,1152,128]{2,1,0:T(8,128)(2,1)S(1)}, u32[]{:S(2)}, u32[]{:S(2)}) collective-permute-start(bf16[2,1152,128]{2,1,0:T(8,128)(2,1)S(1)} %get-tuple-element.313), channel_id=1, source_target_pairs={{0,2},{1,3},{2,0},{3,1},{4,6},{5,7},{6,4},{7,5},{8,10},{9,11},{10,... | collective-permute-start | bytes 1769480 | tf_op jit(solution)/shard_map/ppermute | solution.py:15
  284.8 22.9 %collective-permute-start.54 = (bf16[128,2176]{1,0:T(8,128)(2,1)S(1)}, bf16[128,2176]{1,0:T(8,128)(2,1)S(1)}, u32[]{:S(2)}, u32[]{:S(2)}) collective-permute-start(bf16[128,2176]{1,0:T(8,128)(2,1)S(1)} %add_convert_fusion.8), channel_id=1, source_target_pairs={{0,8},{24,16},{1,9},{25,17},{2,10},{26,18},{3,11},{27,19},{4,12},{... | collective-permute-start | bytes 1671176 | tf_op jit(solution)/shard_map/ppermute | solution.py:15
  310.6 18.7 %collective-permute-start.61 = (bf16[128,2048]{1,0:T(8,128)(2,1)}, bf16[128,2048]{1,0:T(8,128)(2,1)}, u32[]{:S(2)}, u32[]{:S(2)}) collective-permute-start(bf16[128,2048]{1,0:T(8,128)(2,1)} %add_convert_fusion.11), channel_id=1, source_target_pairs={{8,0},{16,24},{9,1},{17,25},{10,2},{18,26},{11,3},{19,27},{12,4},{... | collective-permute-start | bytes 1572872 | tf_op jit(solution)/shard_map/ppermute | solution.py:15
  313.3 19.7 %collective-permute-start.60 = (bf16[128,2176]{1,0:T(8,128)(2,1)}, bf16[128,2176]{1,0:T(8,128)(2,1)}, u32[]{:S(2)}, u32[]{:S(2)}) collective-permute-start(bf16[128,2176]{1,0:T(8,128)(2,1)} %add_convert_fusion.7), channel_id=1, source_target_pairs={{8,16},{16,8},{9,17},{17,9},{10,18},{18,10},{11,19},{19,11},{12,20... | collective-permute-start | bytes 1671176 | tf_op jit(solution)/shard_map/ppermute | solution.py:15
  317.5 14.6 %collective-permute-start.63 = (bf16[256,1024]{1,0:T(8,128)(2,1)}, bf16[256,1024]{1,0:T(8,128)(2,1)}, u32[]{:S(2)}, u32[]{:S(2)}) collective-permute-start(bf16[256,1024]{1,0:T(8,128)(2,1)} %get-tuple-element.299), channel_id=1, source_target_pairs={{0,4},{1,5},{2,6},{3,7},{4,0},{5,1},{6,2},{7,3},{8,12},{9,13},{10,... | collective-permute-start | bytes 1572872 | tf_op jit(solution)/shard_map/ppermute | solution.py:15
  318.7 14.4 %collective-permute-start.62 = (bf16[256,1024]{1,0:T(8,128)(2,1)}, bf16[256,1024]{1,0:T(8,128)(2,1)}, u32[]{:S(2)}, u32[]{:S(2)}) collective-permute-start(bf16[256,1024]{1,0:T(8,128)(2,1)} %get-tuple-element.300), channel_id=1, source_target_pairs={{0,2},{1,3},{2,0},{3,1},{4,6},{5,7},{6,4},{7,5},{8,10},{9,11},{10,... | collective-permute-start | bytes 1572872 | tf_op jit(solution)/shard_map/ppermute | solution.py:15
  335.5 18.8 %collective-permute-start.65 = (bf16[128,2176]{1,0:T(8,128)(2,1)S(1)}, bf16[128,2176]{1,0:T(8,128)(2,1)S(1)}, u32[]{:S(2)}, u32[]{:S(2)}) collective-permute-start(bf16[128,2176]{1,0:T(8,128)(2,1)S(1)} %add_convert_fusion.6), channel_id=1, source_target_pairs={{8,0},{16,24},{9,1},{17,25},{10,2},{18,26},{11,3},{19,27},{12,4},{... | collective-permute-start | bytes 1671176 | tf_op jit(solution)/shard_map/ppermute | solution.py:15
  (70 other events, 470.3 us)

commit v6 on v5

--- a/solution.py
+++ b/solution.py
@@ -299,7 +299,7 @@
         out_specs=[columns] * 3 + [first, second] * 2,
         out_shape=[jax.ShapeDtypeStruct((hidden, count), bf16)] * 3
         + [jax.ShapeDtypeStruct((half, width), bf16)] * 4,
-        compiler_params=pltpu.CompilerParams(vmem_limit_bytes=48 << 20),
+        compiler_params=pltpu.CompilerParams(vmem_limit_bytes=40 << 20),
         cost_estimate=pl.CostEstimate(
             flops=12 * count * width * hidden,
             bytes_accessed=2 * (4 * count * width + 3 * hidden * (width + count)),

time: 364 us -> 363 us (level)
  other arithmetic: 61 us -> 57.1 us
    unnamed x44, other arithmetic: 10.1 us -> 6.11 us
    unnamed x139 -> x127, local copies, waits for them, and re-layouts: 10.9 us -> 10.9 us
where the time goes in v6:
time: 363 us; the launch traced here: 356 us
  waiting for transfers between devices  144 us (40%)
  starting transfers between devices  84.5 us (23%)
  other arithmetic  57.1 us (16%)
  Pallas kernels  23.5 us (6%)
  matrix products  22.4 us (6%)
  local copies, waits for them, and re-layouts  21.9 us (6%)
    ppermute x64, waiting for transfers between devices, along(): return lax.ppermute(shard, axis, pairs)  143 us
    ppermute x64, starting transfers between devices, along(): return lax.ppermute(shard, axis, pairs)  81.3 us
    pallas_call x1, Pallas kernels, feed_forward(): pl.pallas_call(feed_forward_kernel, grid=(steps,), in_specs=[rows, rows,...  23.5 us
    dot_general x5, matrix products, times(): return jnp.dot(left, right, preferred_element_type=f32)  15.6 us
    unnamed x127, local copies, waits for them, and re-layouts  10.9 us
    convert_element_type x9, other arithmetic, add_pair(): (one.astype(f32) + other.astype(f32)).astype(bf16)  8.34 us
  transfers between devices with their start and end apart: 66, of which 29 were waited for; matrix products, arithmetic and copies ran while one was open for 25% of the time, Pallas kernels for 0%

profile of v6, /device:TPU:0, one launch (start us, length us, event | category | flops | bytes accessed | tf_op | source)
XLA Modules:
  0.0 356.3 jit_solution(11676384039696742354)
XLA Ops:
  1.5 3.0 collective-permute-start
  6.6 2.4 copy.72
  13.0 2.0 collective-permute-start.3
  15.2 9.7 %collective-permute-done.3 = bf16[8,128]{1,0:T(8,128)(2,1)S(1)} collective-permute-done((bf16[8,128]{1,0:T(8,128)(2,1)S(1)}, bf16[8,128]{1,0:T(8,128)(2,1)S(1)}, u32[]{:S(2)}, u32[]{:S(2)}) %collective-permute-start.3) | collective-permute-done | bytes 2080 | tf_op jit(solution)/shard_map/ppermute | solution.py:15
  35.1 13.3 %collective-permute-done.11 = bf16[128,1024]{1,0:T(8,128)(2,1)S(1)} collective-permute-done((bf16[128,1024]{1,0:T(8,128)(2,1)S(1)}, bf16[128,1024]{1,0:T(8,128)(2,1)S(1)}, u32[]{:S(2)}, u32[]{:S(2)}) %collective-permute-start.11) | collective-permute-done | bytes 262176 | tf_op jit(solution)/shard_map/ppermute | solution.py:15
  51.4 11.3 %collective-permute-done.15 = bf16[128,1024]{1,0:T(8,128)(2,1)S(1)} collective-permute-done((bf16[128,1024]{1,0:T(8,128)(2,1)S(1)}, bf16[128,1024]{1,0:T(8,128)(2,1)S(1)}, u32[]{:S(2)}, u32[]{:S(2)}) %collective-permute-start.15) | collective-permute-done | bytes 262176 | tf_op jit(solution)/shard_map/ppermute | solution.py:15
  64.7 2.9 collective-permute-done.18
  67.6 1.8 collective-permute-done.17
  70.9 1.8 fusion.70
  73.7 1.8 collective-permute-start.13
  78.1 3.9 %collective-permute-done.21 = bf16[256,1024]{1,0:T(8,128)(2,1)S(1)} collective-permute-done((bf16[256,1024]{1,0:T(8,128)(2,1)S(1)}, bf16[256,1024]{1,0:T(8,128)(2,1)S(1)}, u32[]{:S(2)}, u32[]{:S(2)}) %collective-permute-start.21) | collective-permute-done | bytes 524320 | tf_op jit(solution)/shard_map/ppermute | solution.py:15
  83.2 1.6 collective-permute-start.30
  87.8 11.1 %collective-permute-done.23 = bf16[256,1024]{1,0:T(8,128)(2,1)S(1)} collective-permute-done((bf16[256,1024]{1,0:T(8,128)(2,1)S(1)}, bf16[256,1024]{1,0:T(8,128)(2,1)S(1)}, u32[]{:S(2)}, u32[]{:S(2)}) %collective-permute-start.23) | collective-permute-done | bytes 524320 | tf_op jit(solution)/shard_map/ppermute | solution.py:15
  98.9 2.2 collective-permute-done.22
  101.8 2.7 collective-permute-done.28
  106.0 5.6 %collective-permute-done.30 = bf16[576,1024]{1,0:T(8,128)(2,1)S(1)} collective-permute-done((bf16[576,1024]{1,0:T(8,128)(2,1)S(1)}, bf16[576,1024]{1,0:T(8,128)(2,1)S(1)}, u32[]{:S(2)}, u32[]{:S(2)}) %collective-permute-start.30) | collective-permute-done | bytes 1179680 | tf_op jit(solution)/shard_map/ppermute | solution.py:15
  114.2 1.8 copy-done.26
  116.0 23.5 %shard_map.177 = (bf16[576,2048]{1,0:T(8,128)(2,1)S(1)}, bf16[576,2048]{1,0:T(8,128)(2,1)}, bf16[576,2048]{1,0:T(8,128)(2,1)}, bf16[1024,1024]{1,0:T(8,128)(2,1)...) custom-call(bf16[2048,1024]{1,0:T(8,128)(2,1)} %bitcast.278, ...), custom_call_target="tpu_custom_call" | custom-call | flops 14495514624 | bytes 27394048 | tf_op jit(solution)/shard_map/pallas_call | solution.py:295
  139.6 5.6 %convolution_convert_fusion.4 = bf16[576,1024]{1,0:T(8,128)(2,1)S(1)} fusion(bf16[576,2048]{1,0:T(8,128)(2,1)} %get-tuple-element.97, bf16[2048,1024]{1,0:T(8,128)(2,1)} %bitcast.279), kind=kOutput, calls=%fused_computation.32 | convolution fusion | flops 2416508928 | bytes 7733248 | tf_op jit(solution)/shard_map/dot_general | solution.py:229
  145.3 3.8 %collective-permute-start.38 = (bf16[576,1024]{1,0:T(8,128)(2,1)S(1)}, bf16[576,1024]{1,0:T(8,128)(2,1)S(1)}, u32[]{:S(2)}, u32[]{:S(2)}) collective-permute-start(bf16[576,1024]{1,0:T(8,128)(2,1)S(1)} %convolution_convert_fusion.4), channel_id=1, source_target_pairs={{0,8},{24,16},{1,9},{25,17},{2,10},{26,18},{3,11},{27,19},{4,12},{... | collective-permute-start | bytes 3538952 | tf_op jit(solution)/shard_map/ppermute | solution.py:15
  150.1 3.7 %convolution_convert_fusion.2 = bf16[576,1024]{1,0:T(8,128)(2,1)} fusion(bf16[576,2048]{1,0:T(8,128)(2,1)S(1)} %get-tuple-element.100, bf16[2048,1024]{1,0:T(8,128)(2,1)S(1)} %bitcast.277), kind=kOutput, calls=%fused_computation.30 | convolution fusion | flops 2416508928 | bytes 7733248 | tf_op jit(solution)/shard_map/dot_general | solution.py:229
  153.9 4.6 %collective-permute-done.32 = bf16[256,1024]{1,0:T(8,128)(2,1)S(1)} collective-permute-done((bf16[256,1024]{1,0:T(8,128)(2,1)S(1)}, bf16[256,1024]{1,0:T(8,128)(2,1)S(1)}, u32[]{:S(2)}, u32[]{:S(2)}) %collective-permute-start.32) | collective-permute-done | bytes 524320 | tf_op jit(solution)/shard_map/ppermute | solution.py:15
  161.2 3.7 %convolution_convert_fusion.3 = bf16[576,1024]{1,0:T(8,128)(2,1)} fusion(bf16[576,2048]{1,0:T(8,128)(2,1)S(1)} %copy-done.43, bf16[2048,1024]{1,0:T(8,128)(2,1)S(1)} %bitcast.280), kind=kOutput, calls=%fused_computation.31 | convolution fusion | flops 2416508928 | bytes 7733248 | tf_op jit(solution)/shard_map/dot_general | solution.py:229
  164.8 7.4 %collective-permute-done.33 = bf16[256,1024]{1,0:T(8,128)(2,1)S(1)} collective-permute-done((bf16[256,1024]{1,0:T(8,128)(2,1)S(1)}, bf16[256,1024]{1,0:T(8,128)(2,1)S(1)}, u32[]{:S(2)}, u32[]{:S(2)}) %collective-permute-start.33) | collective-permute-done | bytes 524320 | tf_op jit(solution)/shard_map/ppermute | solution.py:15
  179.1 1.7 collective-permute-start.39
  180.8 4.3 %collective-permute-start.40 = (bf16[576,1024]{1,0:T(8,128)(2,1)}, bf16[576,1024]{1,0:T(8,128)(2,1)}, u32[]{:S(2)}, u32[]{:S(2)}) collective-permute-start(bf16[576,1024]{1,0:T(8,128)(2,1)} %convolution_convert_fusion.3), channel_id=1, source_target_pairs={{0,8},{24,16},{1,9},{25,17},{2,10},{26,18},{3,11},{27,19},{4,12},{... | collective-permute-start | bytes 3538952 | tf_op jit(solution)/shard_map/ppermute | solution.py:15
  191.8 1.8 fusion
  198.5 1.7 convolution_convert_fusion
  201.1 2.5 pad_maximum_fusion.3
  203.6 5.9 %collective-permute-done.40 = bf16[576,1024]{1,0:T(8,128)(2,1)} collective-permute-done((bf16[576,1024]{1,0:T(8,128)(2,1)}, bf16[576,1024]{1,0:T(8,128)(2,1)}, u32[]{:S(2)}, u32[]{:S(2)}) %collective-permute-start.40) | collective-permute-done | bytes 1179680 | tf_op jit(solution)/shard_map/ppermute | solution.py:15
  209.5 2.9 broadcast_select_fusion.1
  212.4 2.2 collective-permute-start.43
  214.6 2.1 add_convert_fusion.3
  224.8 16.5 %collective-permute-done.43 = bf16[576,1024]{1,0:T(8,128)(2,1)S(1)} collective-permute-done((bf16[576,1024]{1,0:T(8,128)(2,1)S(1)}, bf16[576,1024]{1,0:T(8,128)(2,1)S(1)}, u32[]{:S(2)}, u32[]{:S(2)}) %collective-permute-start.43) | collective-permute-done | bytes 1179680 | tf_op jit(solution)/shard_map/ppermute | solution.py:15
  245.8 1.7 fusion.11
  250.5 8.3 %collective-permute-start.48 = (bf16[128,2048]{1,0:T(8,128)(2,1)S(1)}, bf16[128,2048]{1,0:T(8,128)(2,1)S(1)}, u32[]{:S(2)}, u32[]{:S(2)}) collective-permute-start(bf16[128,2048]{1,0:T(8,128)(2,1)S(1)} %add_convert_fusion.14), channel_id=1, source_target_pairs={{0,8},{24,16},{1,9},{25,17},{2,10},{26,18},{3,11},{27,19},{4,12},{... | collective-permute-start | bytes 1572872 | tf_op jit(solution)/shard_map/ppermute | solution.py:15
  258.7 2.1 bitcast_bitcast_fusion.1
  260.8 8.1 %collective-permute-done.48 = bf16[128,2048]{1,0:T(8,128)(2,1)S(1)} collective-permute-done((bf16[128,2048]{1,0:T(8,128)(2,1)S(1)}, bf16[128,2048]{1,0:T(8,128)(2,1)S(1)}, u32[]{:S(2)}, u32[]{:S(2)}) %collective-permute-start.48) | collective-permute-done | bytes 524320 | tf_op jit(solution)/shard_map/ppermute | solution.py:15
  268.9 6.3 %collective-permute-done.49 = bf16[576,1024]{1,0:T(8,128)(2,1)S(1)} collective-permute-done((bf16[576,1024]{1,0:T(8,128)(2,1)S(1)}, bf16[576,1024]{1,0:T(8,128)(2,1)S(1)}, u32[]{:S(2)}, u32[]{:S(2)}) %collective-permute-start.49) | collective-permute-done | bytes 1179680 | tf_op jit(solution)/shard_map/ppermute | solution.py:15
  278.5 2.1 collective-permute-start.59
  283.4 13.0 %collective-permute-start.54 = (bf16[128,2176]{1,0:T(8,128)(2,1)S(1)}, bf16[128,2176]{1,0:T(8,128)(2,1)S(1)}, u32[]{:S(2)}, u32[]{:S(2)}) collective-permute-start(bf16[128,2176]{1,0:T(8,128)(2,1)S(1)} %add_convert_fusion.8), channel_id=1, source_target_pairs={{0,8},{24,16},{1,9},{25,17},{2,10},{26,18},{3,11},{27,19},{4,12},{... | collective-permute-start | bytes 1671176 | tf_op jit(solution)/shard_map/ppermute | solution.py:15
  297.7 8.6 %collective-permute-done.54 = bf16[128,2176]{1,0:T(8,128)(2,1)S(1)} collective-permute-done((bf16[128,2176]{1,0:T(8,128)(2,1)S(1)}, bf16[128,2176]{1,0:T(8,128)(2,1)S(1)}, u32[]{:S(2)}, u32[]{:S(2)}) %collective-permute-start.54) | collective-permute-done | bytes 557088 | tf_op jit(solution)/shard_map/ppermute | solution.py:15
  306.5 1.7 collective-permute-done.56
  313.3 2.7 fusion.23
  324.2 3.0 copy.88
  327.3 3.0 copy.87
  336.5 2.6 add_convert_fusion.10
  339.1 13.9 %collective-permute-done.65 = bf16[128,2176]{1,0:T(8,128)(2,1)S(1)} collective-permute-done((bf16[128,2176]{1,0:T(8,128)(2,1)S(1)}, bf16[128,2176]{1,0:T(8,128)(2,1)S(1)}, u32[]{:S(2)}, u32[]{:S(2)}) %collective-permute-start.65) | collective-permute-done | bytes 557088 | tf_op jit(solution)/shard_map/ppermute | solution.py:15
  (381 shorter events, 103.7 us)
Async XLA Ops:
  1.5 11.5 %collective-permute-start = (bf16[8,128]{1,0:T(8,128)(2,1)S(1)}, bf16[8,128]{1,0:T(8,128)(2,1)S(1)}, u32[]{:S(2)}, u32[]{:S(2)}) collective-permute-start(bf16[8,128]{1,0:T(8,128)(2,1)S(1)} %fusion.53), channel_id=1, source_target_pairs={{0,2},{1,3},{2,0},{3,1},{4,6},{5,7},{6,4},{7,5},{8,10},{9,11},{10,... | collective-permute-start | bytes 6152 | tf_op jit(solution)/shard_map/ppermute | solution.py:15
  6.0 24.7 %collective-permute-start.6 = (bf16[128,3072]{1,0:T(8,128)(2,1)}, bf16[128,3072]{1,0:T(8,128)(2,1)S(1)}, u32[]{:S(2)}, u32[]{:S(2)}) collective-permute-start(bf16[128,3072]{1,0:T(8,128)(2,1)} %param.12), channel_id=1, source_target_pairs={{0,4},{1,5},{2,6},{3,7},{4,0},{5,1},{6,2},{7,3},{8,12},{9,13},{10,... | collective-permute-start | bytes 2359304 | tf_op jit(solution)/shard_map/ppermute | solution.py:15
  6.5 24.2 %collective-permute-start.5 = (bf16[128,3072]{1,0:T(8,128)(2,1)}, bf16[128,3072]{1,0:T(8,128)(2,1)S(1)}, u32[]{:S(2)}, u32[]{:S(2)}) collective-permute-start(bf16[128,3072]{1,0:T(8,128)(2,1)} %param.12), channel_id=1, source_target_pairs={{0,2},{1,3},{2,0},{3,1},{4,6},{5,7},{6,4},{7,5},{8,10},{9,11},{10,... | collective-permute-start | bytes 2359304 | tf_op jit(solution)/shard_map/ppermute | solution.py:15
  12.7 18.7 %collective-permute-start.12 = (bf16[4,576,128]{2,1,0:T(8,128)(2,1)}, bf16[4,576,128]{2,1,0:T(8,128)(2,1)}, u32[]{:S(2)}, u32[]{:S(2)}) collective-permute-start(bf16[4,576,128]{2,1,0:T(8,128)(2,1)} %select_bitcast_fusion.4), channel_id=1, source_target_pairs={{0,1},{1,0},{2,3},{3,2},{4,5},{5,4},{6,7},{7,6},{8,9},{9,8},{10,11... | collective-permute-start | bytes 1769480 | tf_op jit(solution)/shard_map/ppermute | solution.py:15
  13.0 12.0 %collective-permute-start.3 = (bf16[8,128]{1,0:T(8,128)(2,1)S(1)}, bf16[8,128]{1,0:T(8,128)(2,1)S(1)}, u32[]{:S(2)}, u32[]{:S(2)}) collective-permute-start(bf16[8,128]{1,0:T(8,128)(2,1)S(1)} %broadcast_select_fusion.82), channel_id=1, source_target_pairs={{0,4},{1,3},{2,6},{3,1},{4,0},{5,7},{6,2},{7,5},{8,12},{9,11},{10,... | collective-permute-start | bytes 6152 | tf_op jit(solution)/shard_map/ppermute | solution.py:15
  30.8 17.7 %collective-permute-start.8 = (bf16[128,3072]{1,0:T(8,128)(2,1)S(1)}, bf16[128,3072]{1,0:T(8,128)(2,1)S(1)}, u32[]{:S(2)}, u32[]{:S(2)}) collective-permute-start(bf16[128,3072]{1,0:T(8,128)(2,1)S(1)} %broadcast_select_fusion.5), channel_id=1, source_target_pairs={{0,4},{1,3},{2,6},{3,1},{4,0},{5,7},{6,2},{7,5},{8,12},{9,11},{10,... | collective-permute-start | bytes 2359304 | tf_op jit(solution)/shard_map/ppermute | solution.py:15
  32.7 15.8 %collective-permute-start.11 = (bf16[128,1024]{1,0:T(8,128)(2,1)S(1)}, bf16[128,1024]{1,0:T(8,128)(2,1)S(1)}, u32[]{:S(2)}, u32[]{:S(2)}) collective-permute-start(bf16[128,1024]{1,0:T(8,128)(2,1)S(1)} %copy-done.22), channel_id=1, source_target_pairs={{0,4},{1,5},{2,6},{3,7},{4,0},{5,1},{6,2},{7,3},{8,12},{9,13},{10,... | collective-permute-start | bytes 786440 | tf_op jit(solution)/shard_map/ppermute | solution.py:15
  34.2 14.2 %collective-permute-start.10 = (bf16[128,1024]{1,0:T(8,128)(2,1)S(1)}, bf16[128,1024]{1,0:T(8,128)(2,1)S(1)}, u32[]{:S(2)}, u32[]{:S(2)}) collective-permute-start(bf16[128,1024]{1,0:T(8,128)(2,1)S(1)} %copy-done.22), channel_id=1, source_target_pairs={{0,2},{1,3},{2,0},{3,1},{4,6},{5,7},{6,4},{7,5},{8,10},{9,11},{10,... | collective-permute-start | bytes 786440 | tf_op jit(solution)/shard_map/ppermute | solution.py:15
  35.0 35.4 %collective-permute-start.7 = (bf16[3,128,3072]{2,1,0:T(8,128)(2,1)S(1)}, bf16[3,128,3072]{2,1,0:T(8,128)(2,1)S(1)}, u32[]{:S(2)}, u32[]{:S(2)}) collective-permute-start(bf16[3,128,3072]{2,1,0:T(8,128)(2,1)S(1)} %pad_maximum_fusion), channel_id=1, source_target_pairs={{0,1},{1,0},{2,3},{3,2},{4,5},{5,4},{6,7},{7,6},{8,9},{9,8},{10,11... | collective-permute-start | bytes 7077896 | tf_op jit(solution)/shard_map/ppermute | solution.py:15
  48.5 14.1 %collective-permute-start.15 = (bf16[128,1024]{1,0:T(8,128)(2,1)S(1)}, bf16[128,1024]{1,0:T(8,128)(2,1)S(1)}, u32[]{:S(2)}, u32[]{:S(2)}) collective-permute-start(bf16[128,1024]{1,0:T(8,128)(2,1)S(1)} %broadcast_select_fusion.9), channel_id=1, source_target_pairs={{0,4},{1,3},{2,6},{3,1},{4,0},{5,7},{6,2},{7,5},{8,12},{9,11},{10,... | collective-permute-start | bytes 786440 | tf_op jit(solution)/shard_map/ppermute | solution.py:15
  49.2 20.8 %collective-permute-start.14 = (bf16[3,128,1024]{2,1,0:T(8,128)(2,1)S(1)}, bf16[3,128,1024]{2,1,0:T(8,128)(2,1)S(1)}, u32[]{:S(2)}, u32[]{:S(2)}) collective-permute-start(bf16[3,128,1024]{2,1,0:T(8,128)(2,1)S(1)} %pad_maximum_fusion.10), channel_id=1, source_target_pairs={{0,1},{1,0},{2,3},{3,2},{4,5},{5,4},{6,7},{7,6},{8,9},{9,8},{10,11... | collective-permute-start | bytes 2359304 | tf_op jit(solution)/shard_map/ppermute | solution.py:15
  49.4 15.4 %collective-permute-start.19 = (bf16[2,576,128]{2,1,0:T(8,128)(2,1)S(1)}, bf16[2,576,128]{2,1,0:T(8,128)(2,1)S(1)}, u32[]{:S(2)}, u32[]{:S(2)}) collective-permute-start(bf16[2,576,128]{2,1,0:T(8,128)(2,1)S(1)} %get-tuple-element.318), channel_id=1, source_target_pairs={{0,6},{1,7},{2,4},{3,5},{4,2},{5,3},{6,0},{7,1},{8,14},{9,15},{10,... | collective-permute-start | bytes 884744 | tf_op jit(solution)/shard_map/ppermute | solution.py:15
  50.9 16.7 %collective-permute-start.18 = (bf16[2,576,128]{2,1,0:T(8,128)(2,1)S(1)}, bf16[2,576,128]{2,1,0:T(8,128)(2,1)S(1)}, u32[]{:S(2)}, u32[]{:S(2)}) collective-permute-start(bf16[2,576,128]{2,1,0:T(8,128)(2,1)S(1)} %get-tuple-element.319), channel_id=1, source_target_pairs={{0,4},{1,5},{2,6},{3,7},{4,0},{5,1},{6,2},{7,3},{8,12},{9,13},{10,... | collective-permute-start | bytes 884744 | tf_op jit(solution)/shard_map/ppermute | solution.py:15
  69.4 12.6 %collective-permute-start.21 = (bf16[256,1024]{1,0:T(8,128)(2,1)S(1)}, bf16[256,1024]{1,0:T(8,128)(2,1)S(1)}, u32[]{:S(2)}, u32[]{:S(2)}) collective-permute-start(bf16[256,1024]{1,0:T(8,128)(2,1)S(1)} %bitcast.253), channel_id=1, source_target_pairs={{0,4},{1,5},{2,6},{3,7},{4,0},{5,1},{6,2},{7,3},{8,12},{9,13},{10,... | collective-permute-start | bytes 1572872 | tf_op jit(solution)/shard_map/ppermute | solution.py:15
  70.0 12.5 %collective-permute-start.20 = (bf16[256,1024]{1,0:T(8,128)(2,1)S(1)}, bf16[256,1024]{1,0:T(8,128)(2,1)S(1)}, u32[]{:S(2)}, u32[]{:S(2)}) collective-permute-start(bf16[256,1024]{1,0:T(8,128)(2,1)S(1)} %bitcast.254), channel_id=1, source_target_pairs={{0,2},{1,3},{2,0},{3,1},{4,6},{5,7},{6,4},{7,5},{8,10},{9,11},{10,... | collective-permute-start | bytes 1572872 | tf_op jit(solution)/shard_map/ppermute | solution.py:15
  82.6 29.3 %collective-permute-start.27 = (bf16[3,256,1024]{2,1,0:T(8,128)(2,1)S(1)}, bf16[3,256,1024]{2,1,0:T(8,128)(2,1)S(1)}, u32[]{:S(2)}, u32[]{:S(2)}) collective-permute-start(bf16[3,256,1024]{2,1,0:T(8,128)(2,1)S(1)} %pad_maximum_fusion.7), channel_id=1, source_target_pairs={{0,1},{1,0},{2,3},{3,2},{4,5},{5,4},{6,7},{7,6},{8,9},{9,8},{10,11... | collective-permute-start | bytes 4718600 | tf_op jit(solution)/shard_map/ppermute | solution.py:15
  83.2 28.4 %collective-permute-start.30 = (bf16[576,1024]{1,0:T(8,128)(2,1)S(1)}, bf16[576,1024]{1,0:T(8,128)(2,1)S(1)}, u32[]{:S(2)}, u32[]{:S(2)}) collective-permute-start(bf16[576,1024]{1,0:T(8,128)(2,1)S(1)} %bitcast.267), channel_id=1, source_target_pairs={{0,8},{8,0},{16,24},{24,16},{1,9},{9,1},{17,25},{25,17},{2,10},{10... | collective-permute-start | bytes 3538952 | tf_op jit(solution)/shard_map/ppermute | solution.py:15
  84.8 14.0 %collective-permute-start.23 = (bf16[256,1024]{1,0:T(8,128)(2,1)S(1)}, bf16[256,1024]{1,0:T(8,128)(2,1)S(1)}, u32[]{:S(2)}, u32[]{:S(2)}) collective-permute-start(bf16[256,1024]{1,0:T(8,128)(2,1)S(1)} %multiply_convert_fusion.1), channel_id=1, source_target_pairs={{0,4},{1,5},{2,6},{3,7},{4,0},{5,1},{6,2},{7,3},{8,12},{9,13},{10,... | collective-permute-start | bytes 1572872 | tf_op jit(solution)/shard_map/ppermute | solution.py:15
  86.2 14.8 %collective-permute-start.22 = (bf16[256,1024]{1,0:T(8,128)(2,1)S(1)}, bf16[256,1024]{1,0:T(8,128)(2,1)S(1)}, u32[]{:S(2)}, u32[]{:S(2)}) collective-permute-start(bf16[256,1024]{1,0:T(8,128)(2,1)S(1)} %multiply_convert_fusion.1), channel_id=1, source_target_pairs={{0,2},{1,3},{2,0},{3,1},{4,6},{5,7},{6,4},{7,5},{8,10},{9,11},{10,... | collective-permute-start | bytes 1572872 | tf_op jit(solution)/shard_map/ppermute | solution.py:15
  86.9 17.6 %collective-permute-start.28 = (bf16[256,1024]{1,0:T(8,128)(2,1)S(1)}, bf16[256,1024]{1,0:T(8,128)(2,1)S(1)}, u32[]{:S(2)}, u32[]{:S(2)}) collective-permute-start(bf16[256,1024]{1,0:T(8,128)(2,1)S(1)} %broadcast_select_fusion.7), channel_id=1, source_target_pairs={{0,4},{1,3},{2,6},{3,1},{4,0},{5,7},{6,2},{7,5},{8,12},{9,11},{10,... | collective-permute-start | bytes 1572872 | tf_op jit(solution)/shard_map/ppermute | solution.py:15
  145.3 32.3 %collective-permute-start.38 = (bf16[576,1024]{1,0:T(8,128)(2,1)S(1)}, bf16[576,1024]{1,0:T(8,128)(2,1)S(1)}, u32[]{:S(2)}, u32[]{:S(2)}) collective-permute-start(bf16[576,1024]{1,0:T(8,128)(2,1)S(1)} %convolution_convert_fusion.4), channel_id=1, source_target_pairs={{0,8},{24,16},{1,9},{25,17},{2,10},{26,18},{3,11},{27,19},{4,12},{... | collective-permute-start | bytes 3538952 | tf_op jit(solution)/shard_map/ppermute | solution.py:15
  159.1 13.1 %collective-permute-start.33 = (bf16[256,1024]{1,0:T(8,128)(2,1)S(1)}, bf16[256,1024]{1,0:T(8,128)(2,1)S(1)}, u32[]{:S(2)}, u32[]{:S(2)}) collective-permute-start(bf16[256,1024]{1,0:T(8,128)(2,1)S(1)} %get-tuple-element.303), channel_id=1, source_target_pairs={{0,2},{1,3},{2,0},{3,1},{4,6},{5,7},{6,4},{7,5},{8,10},{9,11},{10,... | collective-permute-start | bytes 1572872 | tf_op jit(solution)/shard_map/ppermute | solution.py:15
  159.9 12.8 %collective-permute-start.34 = (bf16[256,1024]{1,0:T(8,128)(2,1)S(1)}, bf16[256,1024]{1,0:T(8,128)(2,1)S(1)}, u32[]{:S(2)}, u32[]{:S(2)}) collective-permute-start(bf16[256,1024]{1,0:T(8,128)(2,1)S(1)} %get-tuple-element.304), channel_id=1, source_target_pairs={{0,4},{1,5},{2,6},{3,7},{4,0},{5,1},{6,2},{7,3},{8,12},{9,13},{10,... | collective-permute-start | bytes 1572872 | tf_op jit(solution)/shard_map/ppermute | solution.py:15
  176.9 12.4 %collective-permute-start.35 = (bf16[512,2048]{1,0:T(8,128)(2,1)S(1)}, bf16[512,2048]{1,0:T(8,128)(2,1)S(1)}, u32[]{:S(2)}, u32[]{:S(2)}) collective-permute-start(bf16[512,2048]{1,0:T(8,128)(2,1)S(1)} %pad_maximum_fusion.5), channel_id=1, source_target_pairs={{0,1},{1,0},{2,3},{3,2},{4,5},{5,4},{6,7},{7,6},{8,9},{9,8},{10,11... | collective-permute-start | bytes 6291464 | tf_op jit(solution)/shard_map/ppermute | solution.py:15
  177.1 26.5 %collective-permute-start.41 = (bf16[1024,1024]{1,0:T(8,128)(2,1)}, bf16[1024,1024]{1,0:T(8,128)(2,1)}, u32[]{:S(2)}, u32[]{:S(2)}) collective-permute-start(bf16[1024,1024]{1,0:T(8,128)(2,1)} %get-tuple-element.108), channel_id=1, source_target_pairs={{0,1},{1,0},{2,3},{3,2},{4,5},{5,4},{6,7},{7,6},{8,9},{9,8},{10,11... | collective-permute-start | bytes 6291464 | tf_op jit(solution)/shard_map/ppermute | solution.py:15
  179.1 24.5 %collective-permute-start.39 = (bf16[576,1024]{1,0:T(8,128)(2,1)}, bf16[576,1024]{1,0:T(8,128)(2,1)}, u32[]{:S(2)}, u32[]{:S(2)}) collective-permute-start(bf16[576,1024]{1,0:T(8,128)(2,1)} %add_convert_fusion.5), channel_id=1, source_target_pairs={{8,16},{16,8},{9,17},{17,9},{10,18},{18,10},{11,19},{19,11},{12,20... | collective-permute-start | bytes 3538952 | tf_op jit(solution)/shard_map/ppermute | solution.py:15
  180.8 28.7 %collective-permute-start.40 = (bf16[576,1024]{1,0:T(8,128)(2,1)}, bf16[576,1024]{1,0:T(8,128)(2,1)}, u32[]{:S(2)}, u32[]{:S(2)}) collective-permute-start(bf16[576,1024]{1,0:T(8,128)(2,1)} %convolution_convert_fusion.3), channel_id=1, source_target_pairs={{0,8},{24,16},{1,9},{25,17},{2,10},{26,18},{3,11},{27,19},{4,12},{... | collective-permute-start | bytes 3538952 | tf_op jit(solution)/shard_map/ppermute | solution.py:15
  190.3 19.2 %collective-permute-start.37 = (bf16[128,2048]{1,0:T(8,128)(2,1)}, bf16[128,2048]{1,0:T(8,128)(2,1)}, u32[]{:S(2)}, u32[]{:S(2)}) collective-permute-start(bf16[128,2048]{1,0:T(8,128)(2,1)} %add_convert_fusion.15), channel_id=1, source_target_pairs={{0,2},{1,5},{2,0},{3,7},{4,6},{5,1},{6,4},{7,3},{8,10},{9,13},{10,... | collective-permute-start | bytes 1572872 | tf_op jit(solution)/shard_map/ppermute | solution.py:15
  212.4 28.8 %collective-permute-start.43 = (bf16[576,1024]{1,0:T(8,128)(2,1)S(1)}, bf16[576,1024]{1,0:T(8,128)(2,1)S(1)}, u32[]{:S(2)}, u32[]{:S(2)}) collective-permute-start(bf16[576,1024]{1,0:T(8,128)(2,1)S(1)} %broadcast_select_fusion.1), channel_id=1, source_target_pairs={{0,8},{24,16},{8,0},{16,24},{1,9},{25,17},{9,1},{17,25},{2,10},{26... | collective-permute-start | bytes 3538952 | tf_op jit(solution)/shard_map/ppermute | solution.py:15
  216.7 25.9 %collective-permute-start.44 = (bf16[576,1024]{1,0:T(8,128)(2,1)S(1)}, bf16[576,1024]{1,0:T(8,128)(2,1)S(1)}, u32[]{:S(2)}, u32[]{:S(2)}) collective-permute-start(bf16[576,1024]{1,0:T(8,128)(2,1)S(1)} %add_convert_fusion.3), channel_id=1, source_target_pairs={{8,16},{16,8},{9,17},{17,9},{10,18},{18,10},{11,19},{19,11},{12,20... | collective-permute-start | bytes 3538952 | tf_op jit(solution)/shard_map/ppermute | solution.py:15
  218.7 23.9 %collective-permute-start.45 = (bf16[128,2176]{1,0:T(8,128)(2,1)S(1)}, bf16[128,2176]{1,0:T(8,128)(2,1)S(1)}, u32[]{:S(2)}, u32[]{:S(2)}) collective-permute-start(bf16[128,2176]{1,0:T(8,128)(2,1)S(1)} %add_convert_fusion.9), channel_id=1, source_target_pairs={{0,2},{1,5},{2,0},{3,7},{4,6},{5,1},{6,4},{7,3},{8,10},{9,13},{10,... | collective-permute-start | bytes 1671176 | tf_op jit(solution)/shard_map/ppermute | solution.py:15
  221.5 21.1 %collective-permute-start.47 = (bf16[128,2048]{1,0:T(8,128)(2,1)S(1)}, bf16[128,2048]{1,0:T(8,128)(2,1)S(1)}, u32[]{:S(2)}, u32[]{:S(2)}) collective-permute-start(bf16[128,2048]{1,0:T(8,128)(2,1)S(1)} %get-tuple-element.301), channel_id=1, source_target_pairs={{0,4},{1,5},{2,6},{3,7},{4,0},{5,1},{6,2},{7,3},{8,12},{9,13},{10,... | collective-permute-start | bytes 1572872 | tf_op jit(solution)/shard_map/ppermute | solution.py:15
  223.0 19.6 %collective-permute-start.46 = (bf16[128,2048]{1,0:T(8,128)(2,1)S(1)}, bf16[128,2048]{1,0:T(8,128)(2,1)S(1)}, u32[]{:S(2)}, u32[]{:S(2)}) collective-permute-start(bf16[128,2048]{1,0:T(8,128)(2,1)S(1)} %get-tuple-element.302), channel_id=1, source_target_pairs={{0,2},{1,3},{2,0},{3,1},{4,6},{5,7},{6,4},{7,5},{8,10},{9,11},{10,... | collective-permute-start | bytes 1572872 | tf_op jit(solution)/shard_map/ppermute | solution.py:15
  243.5 31.7 %collective-permute-start.49 = (bf16[576,1024]{1,0:T(8,128)(2,1)S(1)}, bf16[576,1024]{1,0:T(8,128)(2,1)S(1)}, u32[]{:S(2)}, u32[]{:S(2)}) collective-permute-start(bf16[576,1024]{1,0:T(8,128)(2,1)S(1)} %add_convert_fusion.2), channel_id=1, source_target_pairs={{8,0},{16,24},{9,1},{17,25},{10,2},{18,26},{11,3},{19,27},{12,4},{... | collective-permute-start | bytes 3538952 | tf_op jit(solution)/shard_map/ppermute | solution.py:15
  244.8 30.4 %collective-permute-start.50 = (bf16[576,1024]{1,0:T(8,128)(2,1)S(1)}, bf16[576,1024]{1,0:T(8,128)(2,1)S(1)}, u32[]{:S(2)}, u32[]{:S(2)}) collective-permute-start(bf16[576,1024]{1,0:T(8,128)(2,1)S(1)} %add_convert_fusion.1), channel_id=1, source_target_pairs={{8,16},{16,8},{9,17},{17,9},{10,18},{18,10},{11,19},{19,11},{12,20... | collective-permute-start | bytes 3538952 | tf_op jit(solution)/shard_map/ppermute | solution.py:15
  247.5 21.4 %collective-permute-start.53 = (bf16[128,2176]{1,0:T(8,128)(2,1)S(1)}, bf16[128,2176]{1,0:T(8,128)(2,1)S(1)}, u32[]{:S(2)}, u32[]{:S(2)}) collective-permute-start(bf16[128,2176]{1,0:T(8,128)(2,1)S(1)} %get-tuple-element.297), channel_id=1, source_target_pairs={{0,4},{1,5},{2,6},{3,7},{4,0},{5,1},{6,2},{7,3},{8,12},{9,13},{10,... | collective-permute-start | bytes 1671176 | tf_op jit(solution)/shard_map/ppermute | solution.py:15
  249.0 19.9 %collective-permute-start.52 = (bf16[128,2176]{1,0:T(8,128)(2,1)S(1)}, bf16[128,2176]{1,0:T(8,128)(2,1)S(1)}, u32[]{:S(2)}, u32[]{:S(2)}) collective-permute-start(bf16[128,2176]{1,0:T(8,128)(2,1)S(1)} %get-tuple-element.298), channel_id=1, source_target_pairs={{0,2},{1,3},{2,0},{3,1},{4,6},{5,7},{6,4},{7,5},{8,10},{9,11},{10,... | collective-permute-start | bytes 1671176 | tf_op jit(solution)/shard_map/ppermute | solution.py:15
  250.5 18.5 %collective-permute-start.48 = (bf16[128,2048]{1,0:T(8,128)(2,1)S(1)}, bf16[128,2048]{1,0:T(8,128)(2,1)S(1)}, u32[]{:S(2)}, u32[]{:S(2)}) collective-permute-start(bf16[128,2048]{1,0:T(8,128)(2,1)S(1)} %add_convert_fusion.14), channel_id=1, source_target_pairs={{0,8},{24,16},{1,9},{25,17},{2,10},{26,18},{3,11},{27,19},{4,12},{... | collective-permute-start | bytes 1572872 | tf_op jit(solution)/shard_map/ppermute | solution.py:15
  276.9 31.4 %collective-permute-start.56 = (bf16[576,1024]{1,0:T(8,128)(2,1)S(1)}, bf16[576,1024]{1,0:T(8,128)(2,1)S(1)}, u32[]{:S(2)}, u32[]{:S(2)}) collective-permute-start(bf16[576,1024]{1,0:T(8,128)(2,1)S(1)} %add_convert_fusion), channel_id=1, source_target_pairs={{8,0},{16,24},{9,1},{17,25},{10,2},{18,26},{11,3},{19,27},{12,4},{... | collective-permute-start | bytes 3538952 | tf_op jit(solution)/shard_map/ppermute | solution.py:15
  278.5 27.8 %collective-permute-start.59 = (bf16[2,1152,128]{2,1,0:T(8,128)(2,1)S(1)}, bf16[2,1152,128]{2,1,0:T(8,128)(2,1)S(1)}, u32[]{:S(2)}, u32[]{:S(2)}) collective-permute-start(bf16[2,1152,128]{2,1,0:T(8,128)(2,1)S(1)} %get-tuple-element.311), channel_id=1, source_target_pairs={{0,6},{1,7},{2,4},{3,5},{4,2},{5,3},{6,0},{7,1},{8,14},{9,15},{10,... | collective-permute-start | bytes 1769480 | tf_op jit(solution)/shard_map/ppermute | solution.py:15
  280.6 25.9 %collective-permute-start.58 = (bf16[2,1152,128]{2,1,0:T(8,128)(2,1)S(1)}, bf16[2,1152,128]{2,1,0:T(8,128)(2,1)S(1)}, u32[]{:S(2)}, u32[]{:S(2)}) collective-permute-start(bf16[2,1152,128]{2,1,0:T(8,128)(2,1)S(1)} %get-tuple-element.312), channel_id=1, source_target_pairs={{0,4},{1,5},{2,6},{3,7},{4,0},{5,1},{6,2},{7,3},{8,12},{9,13},{10,... | collective-permute-start | bytes 1769480 | tf_op jit(solution)/shard_map/ppermute | solution.py:15
  281.2 25.3 %collective-permute-start.57 = (bf16[2,1152,128]{2,1,0:T(8,128)(2,1)S(1)}, bf16[2,1152,128]{2,1,0:T(8,128)(2,1)S(1)}, u32[]{:S(2)}, u32[]{:S(2)}) collective-permute-start(bf16[2,1152,128]{2,1,0:T(8,128)(2,1)S(1)} %get-tuple-element.313), channel_id=1, source_target_pairs={{0,2},{1,3},{2,0},{3,1},{4,6},{5,7},{6,4},{7,5},{8,10},{9,11},{10,... | collective-permute-start | bytes 1769480 | tf_op jit(solution)/shard_map/ppermute | solution.py:15
  283.4 22.9 %collective-permute-start.54 = (bf16[128,2176]{1,0:T(8,128)(2,1)S(1)}, bf16[128,2176]{1,0:T(8,128)(2,1)S(1)}, u32[]{:S(2)}, u32[]{:S(2)}) collective-permute-start(bf16[128,2176]{1,0:T(8,128)(2,1)S(1)} %add_convert_fusion.8), channel_id=1, source_target_pairs={{0,8},{24,16},{1,9},{25,17},{2,10},{26,18},{3,11},{27,19},{4,12},{... | collective-permute-start | bytes 1671176 | tf_op jit(solution)/shard_map/ppermute | solution.py:15
  309.2 21.2 %collective-permute-start.61 = (bf16[128,2048]{1,0:T(8,128)(2,1)}, bf16[128,2048]{1,0:T(8,128)(2,1)}, u32[]{:S(2)}, u32[]{:S(2)}) collective-permute-start(bf16[128,2048]{1,0:T(8,128)(2,1)} %add_convert_fusion.11), channel_id=1, source_target_pairs={{8,0},{16,24},{9,1},{17,25},{10,2},{18,26},{11,3},{19,27},{12,4},{... | collective-permute-start | bytes 1572872 | tf_op jit(solution)/shard_map/ppermute | solution.py:15
  311.9 19.8 %collective-permute-start.60 = (bf16[128,2176]{1,0:T(8,128)(2,1)}, bf16[128,2176]{1,0:T(8,128)(2,1)}, u32[]{:S(2)}, u32[]{:S(2)}) collective-permute-start(bf16[128,2176]{1,0:T(8,128)(2,1)} %add_convert_fusion.7), channel_id=1, source_target_pairs={{8,16},{16,8},{9,17},{17,9},{10,18},{18,10},{11,19},{19,11},{12,20... | collective-permute-start | bytes 1671176 | tf_op jit(solution)/shard_map/ppermute | solution.py:15
  316.0 14.6 %collective-permute-start.63 = (bf16[256,1024]{1,0:T(8,128)(2,1)}, bf16[256,1024]{1,0:T(8,128)(2,1)}, u32[]{:S(2)}, u32[]{:S(2)}) collective-permute-start(bf16[256,1024]{1,0:T(8,128)(2,1)} %get-tuple-element.299), channel_id=1, source_target_pairs={{0,4},{1,5},{2,6},{3,7},{4,0},{5,1},{6,2},{7,3},{8,12},{9,13},{10,... | collective-permute-start | bytes 1572872 | tf_op jit(solution)/shard_map/ppermute | solution.py:15
  317.3 14.4 %collective-permute-start.62 = (bf16[256,1024]{1,0:T(8,128)(2,1)}, bf16[256,1024]{1,0:T(8,128)(2,1)}, u32[]{:S(2)}, u32[]{:S(2)}) collective-permute-start(bf16[256,1024]{1,0:T(8,128)(2,1)} %get-tuple-element.300), channel_id=1, source_target_pairs={{0,2},{1,3},{2,0},{3,1},{4,6},{5,7},{6,4},{7,5},{8,10},{9,11},{10,... | collective-permute-start | bytes 1572872 | tf_op jit(solution)/shard_map/ppermute | solution.py:15
  334.1 18.8 %collective-permute-start.65 = (bf16[128,2176]{1,0:T(8,128)(2,1)S(1)}, bf16[128,2176]{1,0:T(8,128)(2,1)S(1)}, u32[]{:S(2)}, u32[]{:S(2)}) collective-permute-start(bf16[128,2176]{1,0:T(8,128)(2,1)S(1)} %add_convert_fusion.6), channel_id=1, source_target_pairs={{8,0},{16,24},{9,1},{17,25},{10,2},{18,26},{11,3},{19,27},{12,4},{... | collective-permute-start | bytes 1671176 | tf_op jit(solution)/shard_map/ppermute | solution.py:15
  (64 other events, 419.9 us)
